TPU v7x, 32 devices: a whole 2x2x4 slice. The times are simulated.
32 devices in a mesh: groups: 2 (over y), slab: 4 (over z), sub: 2 (over x), comp: 2 (over core).
Axes of the slice: x: 2, y: 2, z: 4, core: 2. Of those that a mesh axis runs over, the one named last changes fastest.
Arguments:
- electric: float32 [3, 256, 64, 256], P(None, ('groups', 'slab'), 'sub', 'comp'), parts along dimension 1, may hold values from -6 to 6
- magnetic: float32 [3, 256, 64, 256], P(None, ('groups', 'slab'), 'sub', 'comp'), parts along dimension 1, may hold values from -6 to 6
- conduct: float32 [256, 64, 256], P(('groups', 'slab'), 'sub', 'comp'), parts along dimension 0, may hold values from 0.1 to 1
- temp_old: float32 [128, 32, 256], P(('groups', 'slab'), 'sub', 'comp'), parts along dimension 0, may hold values from 0.5 to 1.5
- capacity: float32 [128, 32, 256], P(('groups', 'slab'), 'sub', 'comp'), parts along dimension 0, may hold values from 1 to 4
- offsets: int32 [256, 64, 2], P(('groups', 'slab'), 'sub', 'comp'), parts along dimension 0, may hold values from -1 to 1, as said below
- targets: int32 [256, 64, 2], P(('groups', 'slab'), 'sub', 'comp'), parts along dimension 0, may hold values from 0 to 255
Outputs:
- electric_out: float32 [3, 256, 64, 256], P(None, ('groups', 'slab'), 'sub', 'comp'), parts along dimension 1
- magnetic_out: float32 [3, 256, 64, 256], P(None, ('groups', 'slab'), 'sub', 'comp'), parts along dimension 1
- temp_new: float32 [128, 32, 256], P(('groups', 'slab'), 'sub', 'comp'), parts along dimension 0
- conduct_new: float32 [256, 64, 256], P(('groups', 'slab'), 'sub', 'comp'), parts along dimension 0
There are 2 independent parts, one for each index of `groups`. A program takes and returns all parts, laid end to end along the dimension named above; each array names one. Nothing has to cross between parts.
Inputs may be any that keep to these rules, and one draw needn't show every extreme that they name: `offsets`: -1, 0 or 1; -1 never on the first slab and 1 never on the last; of the field blocks of one device at most 256 have -1 and at most 256 have 1, and each bound is reached by some device.
All inputs are finite; a program needn't handle non-finite values.
Results may differ from a plain program's by a relative error of at most 0.0001.
Values sent between devices are 32-bit elements; how exact they have to be, the bound alone decides.
No kernel may reach another device: no remote copies, remote signals or barrier semaphores. Data moves between devices by JAX's collectives and lax.ppermute only.
A program may use at most 64 MiB of HBM per device.

v0:
```python
import functools

import jax
import jax.numpy as jnp
from jax import lax
from jax.experimental import pallas as pl
from jax.experimental.pallas import tpu as pltpu
from jax.sharding import PartitionSpec as P

STEPS = 4
SWEEPS = 3
W = STEPS

time_step = 0.5
conduction = 2.0
heating = 0.25
softening = 0.25

F32 = jnp.float32
BF16 = jnp.bfloat16
VMEM_LIMIT = 56 * 1024 * 1024


def chebyshev_constants(sweep_count):
    lowest = 1.0
    highest = 4.0 + 12.0 * conduction
    center = 0.5 * (highest + lowest)
    spread = 0.5 * (highest - lowest)
    ratio = center / spread
    rhos = [1.0 / ratio]
    for sweep in range(sweep_count - 1):
        rhos.append(1.0 / (2.0 * ratio - rhos[-1]))
    return (center, spread, rhos)


def passed_along(array, axis, by):
    devices = lax.axis_size(axis)
    pairs = [(i, i + by) for i in range(devices) if 0 <= i + by < devices]
    return lax.ppermute(array, axis, pairs)


def swapped(array, axis):
    return lax.ppermute(array, axis, [(0, 1), (1, 0)])


def plane_list(s_dev):
    up, dn = [], []
    for f in range(7):
        up_rows = W if f in (0, 1, 2, 4, 5) else W - 1
        dn_rows = W if f in (1, 2) else W - 1
        for r in range(s_dev - up_rows, s_dev):
            up.append((f, r))
        for r in range(dn_rows):
            dn.append((f, r))
    return up, dn


def slab_messages(electric, magnetic, conduct, temp_old, capacity):
    s_dev = conduct.shape[0]

    def rows(f, a, b):
        if f < 3:
            return electric[f, a:b]
        if f < 6:
            return magnetic[f - 3, a:b]
        return conduct[a:b]

    def ends(i):
        return jnp.concatenate([temp_old[i], capacity[i]], 0)[None]

    up, dn = [], []
    for f in range(7):
        up_rows = W if f in (0, 1, 2, 4, 5) else W - 1
        dn_rows = W if f in (1, 2) else W - 1
        up.append(rows(f, s_dev - up_rows, s_dev))
        dn.append(rows(f, 0, dn_rows))
    up.append(ends(temp_old.shape[0] - 1))
    dn.append(ends(0))
    return jnp.concatenate(up, 0), jnp.concatenate(dn, 0)


def row_source(f, i, s_dev, own, lo, hi, up_index, dn_index):
    r = i - W
    if 0 <= r < s_dev:
        e_ref, h_ref, c_ref = own
        if f < 3:
            return e_ref, (f, r)
        if f < 6:
            return h_ref, (f - 3, r)
        return c_ref, (r,)
    if r < 0:
        key = (f, s_dev + r)
        return (lo, (up_index[key],)) if key in up_index else None
    key = (f, r - s_dev)
    return (hi, (dn_index[key],)) if key in dn_index else None


def indices_of(s_dev):
    up, dn = plane_list(s_dev)
    return (
        {key: n for n, key in enumerate(up)},
        {key: n for n, key in enumerate(dn)},
    )


def sub_pack_kernel(edges, e_ref, h_ref, c_ref, t_ref, cap_ref, lo_ref, hi_ref, *out_refs):
    s_dev, y_dev = c_ref.shape[0], c_ref.shape[1]
    ty = t_ref.shape[1]
    up_index, dn_index = indices_of(s_dev)
    own = (e_ref, h_ref, c_ref)
    for edge, out in zip(edges, out_refs):
        if edge == "high":
            y0, t0 = y_dev - W, ty - 1
        elif edge == "low":
            y0, t0 = 0, 0
        else:
            upper = lax.axis_index("sub") == 0
            y0 = jnp.where(upper, y_dev - W, 0)
            t0 = jnp.where(upper, ty - 1, 0)
        zero = jnp.zeros((W, 128), F32)
        for c in range(4):
            for i in range(s_dev + 2 * W):
                for half in range(2):
                    if c == 3 and half == 1:
                        continue
                    f = 6 if c == 3 else c + 3 * half
                    source = row_source(f, i, s_dev, own, lo_ref, hi_ref, up_index, dn_index)
                    if source is None:
                        value = zero
                    else:
                        ref, at = source
                        value = ref[at + (pl.ds(y0, W), slice(None))]
                    out[c, i, pl.ds(half * W, W), :] = value
        out[3, :, pl.ds(W, W), :] = jnp.zeros((s_dev + 2 * W, W, 128), F32)
        for i in range(t_ref.shape[0]):
            out[3, i, pl.ds(W, 1), :] = t_ref[i, pl.ds(t0, 1), :]
            out[3, i, pl.ds(W + 1, 1), :] = cap_ref[i, pl.ds(t0, 1), :]


def sub_exchange(electric, magnetic, conduct, temp_old, capacity, lo, hi):
    count = lax.axis_size("sub")
    edges = ("either",) if count == 2 else ("high", "low")
    s_ext = conduct.shape[0] + 2 * W
    shape = jax.ShapeDtypeStruct((4, s_ext, 2 * W, conduct.shape[2]), F32)
    messages = pl.pallas_call(
        functools.partial(sub_pack_kernel, edges),
        out_shape=[shape] * len(edges),
        compiler_params=pltpu.CompilerParams(vmem_limit_bytes=VMEM_LIMIT),
        name="sub_pack",
    )(electric, magnetic, conduct, temp_old, capacity, lo, hi)
    if count == 2:
        received = swapped(messages[0], "sub")
        return received, received
    return passed_along(messages[0], "sub", 1), passed_along(messages[1], "sub", -1)


def inside_flags(axis, count):
    index = lax.axis_index(axis)
    return (index > 0), (index < count - 1)


def comp_pack_kernel(
    n_sub, e_ref, h_ref, c_ref, t_ref, cap_ref, lo_ref, hi_ref, ml_ref, mh_ref, out_ref, a_ref, b_ref
):
    s_dev, y_dev, lanes = c_ref.shape
    y_ext = y_dev + 2 * W
    up_index, dn_index = indices_of(s_dev)
    own = (e_ref, h_ref, c_ref)
    has_lo, has_hi = inside_flags("sub", n_sub)
    first = jnp.where(lax.axis_index("comp") == 0, lanes - W, 0)
    lane = lax.broadcasted_iota(jnp.int32, (8, lanes), 1) // W
    a_ref[...] = jnp.zeros_like(a_ref)
    b_ref[...] = jnp.zeros_like(b_ref)
    blocks = (s_dev + 2 * W) // 8
    for b in range(blocks):
        acc_a = jnp.zeros((y_dev, lanes), F32)
        acc_b = jnp.zeros((y_dev, lanes), F32)
        acc_lo = jnp.zeros((8, lanes), F32)
        acc_hi = jnp.zeros((8, lanes), F32)
        for c in range(4):
            for j in range(8):
                i = b * 8 + j
                group = c * 8 + j
                shift = lax.rem(group * W - first + 2 * lanes, lanes)
                here = lane == group
                here_own = jnp.concatenate([here] * (y_dev // 8), 0)
                for which in range(2):
                    if c == 3 and which == 1:
                        continue
                    f = 6 if c == 3 else c + 3 * which
                    source = row_source(f, i, s_dev, own, lo_ref, hi_ref, up_index, dn_index)
                    if source is None:
                        continue
                    ref, at = source
                    moved = pltpu.roll(ref[at], shift, 1)
                    if which == 0:
                        acc_a = jnp.where(here_own, moved, acc_a)
                    else:
                        acc_b = jnp.where(here_own, moved, acc_b)
                acc_lo = jnp.where(here, pltpu.roll(ml_ref[c, i], shift, 1), acc_lo)
                acc_hi = jnp.where(here, pltpu.roll(mh_ref[c, i], shift, 1), acc_hi)
        acc_lo = jnp.where(has_lo, acc_lo, 0.0)
        acc_hi = jnp.where(has_hi, acc_hi, 0.0)
        a_ref[pl.ds(0, W), :] = acc_lo[:W]
        a_ref[pl.ds(W, y_dev), :] = acc_a
        a_ref[pl.ds(W + y_dev, W), :] = acc_hi[:W]
        b_ref[pl.ds(0, W), :] = acc_lo[W:]
        b_ref[pl.ds(W, y_dev), :] = acc_b
        b_ref[pl.ds(W + y_dev, W), :] = acc_hi[W:]
        out_ref[2 * b] = a_ref[...].T
        out_ref[2 * b + 1] = b_ref[...].T
    rows = t_ref.shape[0] * t_ref.shape[1] // lanes
    for n in range(rows):
        per = lanes // t_ref.shape[1]
        out_ref[2 * blocks + n] = t_ref[pl.ds(n * per, per)].reshape(lanes, lanes)
        out_ref[2 * blocks + rows + n] = cap_ref[pl.ds(n * per, per)].reshape(lanes, lanes)


def comp_pack(electric, magnetic, conduct, temp_old, capacity, lo, hi, m_lo, m_hi):
    s_dev, y_dev, lanes = conduct.shape
    count = 2 * ((s_dev + 2 * W) // 8) + 2 * (temp_old.shape[0] * temp_old.shape[1] // lanes)
    return pl.pallas_call(
        functools.partial(comp_pack_kernel, lax.axis_size("sub")),
        out_shape=jax.ShapeDtypeStruct((count, lanes, lanes), F32),
        scratch_shapes=[pltpu.VMEM((lanes, lanes), F32)] * 2,
        compiler_params=pltpu.CompilerParams(vmem_limit_bytes=VMEM_LIMIT),
        name="comp_pack",
    )(electric, magnetic, conduct, temp_old, capacity, lo, hi, m_lo, m_hi)


TOP = 8


def coefficients(conduct, inside):
    damping = 0.5 * time_step * conduct
    inverse = inside / (1.0 + damping)
    return (1.0 - damping) * inverse, time_step * inverse


def split_two(values):
    high = values.astype(BF16)
    low = (values - high.astype(F32)).astype(BF16)
    return jnp.concatenate([high, low], 1)


def main_kernel(
    n_slab, n_sub,
    e_ref, h_ref, c_ref, t_ref, ids_ref, lo_ref, hi_ref, ml_ref, mh_ref, own_ref, other_ref,
    e_out, h_out, d_out,
    es, hs, ce, ch, heat, sde, sdh, sce, sch, bt, bp,
):
    s_dev, y_dev, lanes = c_ref.shape
    s_ext, y_ext = s_dev + 2 * W, y_dev + 2 * W
    up_index, dn_index = indices_of(s_dev)
    own = (e_ref, h_ref, c_ref)
    slab_lo, slab_hi = inside_flags("slab", n_slab)
    sub_lo, sub_hi = inside_flags("sub", n_sub)
    comp = lax.axis_index("comp")

    def place(ref, at, f, i, half, c):
        source = row_source(f, i, s_dev, own, lo_ref, hi_ref, up_index, dn_index)
        if source is None:
            ref[at + (pl.ds(TOP + W, y_dev), slice(None))] = jnp.zeros((y_dev, lanes), F32)
        else:
            s, sat = source
            ref[at + (pl.ds(TOP + W, y_dev), slice(None))] = s[sat]
        low = ml_ref[c, i, pl.ds(half * W, W), :]
        high = mh_ref[c, i, pl.ds(half * W, W), :]
        ref[at + (pl.ds(TOP, W), slice(None))] = jnp.where(sub_lo, low, 0.0)
        ref[at + (pl.ds(TOP + W + y_dev, W), slice(None))] = jnp.where(sub_hi, high, 0.0)
        ref[at + (pl.ds(0, TOP), slice(None))] = jnp.zeros((TOP, lanes), F32)
        ref[at + (pl.ds(TOP + y_ext, 8), slice(None))] = jnp.zeros((8, lanes), F32)

    place_y = lax.broadcasted_iota(jnp.int32, (y_ext, lanes), 0)
    in_y = ((place_y >= W) | sub_lo) & ((place_y < W + y_dev) | sub_hi)
    in_y = jnp.where(in_y, 1.0, 0.0)
    lane = lax.broadcasted_iota(jnp.int32, (y_ext, lanes), 1)
    is_last = lane == lanes - 1
    is_first = lane == 0

    def slab_inside(i):
        good = ((i >= W) | slab_lo) & ((i < W + s_dev) | slab_hi)
        return jnp.where(good, 1.0, 0.0)

    for i in range(s_ext):
        for c in range(3):
            place(es, (c, i), c, i, 0, c)
            place(hs, (c, i), c + 3, i, 1, c)
        place(ce, (i,), 6, i, 0, 3)

    def coefs(i, carry):
        keep, gain = coefficients(ce[i, pl.ds(TOP, y_ext), :], in_y * slab_inside(i))
        ce[i, pl.ds(TOP, y_ext), :] = keep
        ch[i] = gain
        return carry

    lax.fori_loop(0, s_ext, coefs, 0)

    first = comp == 0
    blocks = s_ext // 8
    lane8 = lax.broadcasted_iota(jnp.int32, (8, lanes), 1)
    in_y8 = ((lane8 >= W) | sub_lo) & ((lane8 < W + y_dev) | sub_hi)
    in_y8 = jnp.where(in_y8, 1.0, 0.0)
    for b in range(blocks):
        for c in range(4):
            for j in range(8):
                i = b * 8 + j
                for which in range(2):
                    if c == 3 and which == 1:
                        continue
                    at = pl.ds((c * 8 + j) * W, W)
                    mine = own_ref[2 * b + which, at, :]
                    theirs = other_ref[2 * b + which, at, :]
                    target = (sdh if which else sde).at[c, i] if c < 3 else sce.at[i]
                    target[pl.ds(0, W), :] = jnp.where(first, mine, theirs)
                    target[pl.ds(W, W), :] = jnp.where(first, theirs, mine)

    def side_coefs(i, carry):
        sce[i], sch[i] = coefficients(sce[i], in_y8 * slab_inside(i))
        return carry

    lax.fori_loop(0, s_ext, side_coefs, 0)

    e_on = jnp.where(comp == 0, 1.0, 0.0)
    h_on = jnp.where(comp == 0, 0.0, 1.0)

    def up_y(v):
        return pltpu.roll(v, lanes - 1, 1)

    def down_y(v):
        return pltpu.roll(v, 1, 1)

    def up_x(v):
        return pltpu.roll(v, 7, 0)

    def down_x(v):
        return pltpu.roll(v, 1, 0)

    bt[...] = jnp.zeros_like(bt)

    def side_h(step, i):
        e0, e1, e2 = sde[0, i], sde[1, i], sde[2, i]
        bt[pl.ds(i * 16 + 2 * step, 1), :] = e0[W : W + 1] * e_on
        bt[pl.ds(i * 16 + 2 * step + 1, 1), :] = e1[W : W + 1] * e_on
        scale = (time_step * slab_inside(i)) * in_y8
        h0 = sdh[0, i] - scale * ((up_y(e2) - e2) - (up_x(e1) - e1))
        h1 = sdh[1, i] - scale * ((up_x(e0) - e0) - (sde[2, i + 1] - e2))
        h2 = sdh[2, i] - scale * ((sde[1, i + 1] - e1) - (up_y(e0) - e0))
        sdh[0, i], sdh[1, i], sdh[2, i] = h0, h1, h2
        bt[pl.ds(i * 16 + 8 + 2 * step, 1), :] = h0[W - 1 : W] * h_on
        bt[pl.ds(i * 16 + 8 + 2 * step + 1, 1), :] = h1[W - 1 : W] * h_on
        return h0, h1, h2

    def side_e(i, h0, h1, h2):
        keep, gain = sce[i], sch[i]
        sde[0, i] = keep * sde[0, i] + gain * ((h2 - down_y(h2)) - (h1 - down_x(h1)))
        sde[1, i] = keep * sde[1, i] + gain * ((h0 - down_x(h0)) - (h2 - sdh[2, i - 1]))
        sde[2, i] = keep * sde[2, i] + gain * ((h1 - sdh[1, i - 1]) - (h0 - down_y(h0)))

    for step in range(STEPS):
        side_h(step, step)

        def side_row(i, carry, step=step):
            side_e(i, *side_h(step, i))
            return carry

        lax.fori_loop(step + 1, s_ext - 1 - step, side_row, 0)

    for b in range(blocks):
        bp[b] = bt[pl.ds(b * lanes, lanes), :].T[:y_ext]

    centre = pl.ds(TOP, y_ext)
    above = pl.ds(TOP + 1, y_ext)
    below = pl.ds(TOP - 1, y_ext)

    def border(i, q, to):
        block, place = i // 8, i % 8
        return pltpu.roll(bp[block], lax.rem(2 * lanes + to - place * 16 - q, lanes), 1)

    def main_h(step, i):
        e0, e1, e2 = es[0, i, centre, :], es[1, i, centre, :], es[2, i, centre, :]
        e0x = jnp.where(is_last, border(i, 2 * step, lanes - 1), pltpu.roll(e0, lanes - 1, 1))
        e1x = jnp.where(is_last, border(i, 2 * step + 1, lanes - 1), pltpu.roll(e1, lanes - 1, 1))
        scale = (time_step * slab_inside(i)) * in_y
        h0 = hs[0, i, centre, :] - scale * ((es[2, i, above, :] - e2) - (e1x - e1))
        h1 = hs[1, i, centre, :] - scale * ((e0x - e0) - (es[2, i + 1, centre, :] - e2))
        h2 = hs[2, i, centre, :] - scale * ((es[1, i + 1, centre, :] - e1) - (es[0, i, above, :] - e0))
        hs[0, i, centre, :] = h0
        hs[1, i, centre, :] = h1
        hs[2, i, centre, :] = h2

    def main_e(step, i):
        h0, h1, h2 = hs[0, i, centre, :], hs[1, i, centre, :], hs[2, i, centre, :]
        h0x = jnp.where(is_first, border(i, 8 + 2 * step, 0), pltpu.roll(h0, 1, 1))
        h1x = jnp.where(is_first, border(i, 8 + 2 * step + 1, 0), pltpu.roll(h1, 1, 1))
        keep, gain = ce[i, centre, :], ch[i]
        e0, e1, e2 = es[0, i, centre, :], es[1, i, centre, :], es[2, i, centre, :]
        n0 = keep * e0 + gain * ((h2 - hs[2, i, below, :]) - (h1 - h1x))
        n1 = keep * e1 + gain * ((h0 - h0x) - (h2 - hs[2, i - 1, centre, :]))
        n2 = keep * e2 + gain * ((h1 - hs[1, i - 1, centre, :]) - (h0 - hs[0, i, below, :]))
        es[0, i, centre, :] = n0
        es[1, i, centre, :] = n1
        es[2, i, centre, :] = n2
        s0, s1, s2 = e0 + n0, e1 + n1, e2 + n2
        total = s0 * s0 + s1 * s1 + s2 * s2
        if step == 0:
            heat[i] = total
        else:
            heat[i] = heat[i] + total

    for step in range(STEPS):
        main_h(step, step)

        def main_row(i, carry, step=step):
            main_h(step, i)
            main_e(step, i)
            return carry

        lax.fori_loop(step + 1, s_ext - 1 - step, main_row, 0)

    ys = pl.ds(TOP + W, y_dev)
    for c in range(3):
        e_out[c] = es[c, pl.ds(W, s_dev), ys, :]
        h_out[c] = hs[c, pl.ds(W, s_dev), ys, :]

    loss = heat[pl.ds(W, s_dev), pl.ds(W, y_dev), :] * c_ref[...] * (0.25 * time_step * heating)
    parts = split_two(loss.reshape(s_dev * y_dev, lanes))
    thermal = t_ref.shape[0] * t_ref.shape[1]
    ids = ids_ref[...]
    for n in range(3):
        kinds = lax.broadcasted_iota(jnp.int32, (thermal, s_dev * y_dev), 0) + n * thermal
        chosen = jnp.where(kinds == ids, 1.0, 0.0).astype(BF16)
        sums = jnp.dot(chosen, parts, preferred_element_type=F32)
        d_out[n] = (sums[:, :lanes] + sums[:, lanes:]).reshape(t_ref.shape)

    ts, ty = t_ref.shape[0], t_ref.shape[1]
    per = lanes // ty
    row_t = lax.broadcasted_iota(jnp.int32, (ty, lanes), 0)
    lane_t = lax.broadcasted_iota(jnp.int32, (ty, lanes), 1)
    lo_plane, hi_plane = len(up_index), len(dn_index)
    for i in range(ts):
        x = t_ref[i]
        before = t_ref[i - 1] if i > 0 else lo_ref[lo_plane, pl.ds(0, ty), :]
        after = t_ref[i + 1] if i < ts - 1 else hi_ref[hi_plane, pl.ds(0, ty), :]
        edge_lo = jnp.where(sub_lo, ml_ref[3, i, pl.ds(W, 1), :], 0.0)
        edge_hi = jnp.where(sub_hi, mh_ref[3, i, pl.ds(W, 1), :], 0.0)
        left_y = jnp.where(row_t == 0, edge_lo, pltpu.roll(x, 1, 0))
        right_y = jnp.where(row_t == ty - 1, edge_hi, pltpu.roll(x, ty - 1, 0))
        beyond = other_ref[2 * blocks + i // per, pl.ds((i % per) * ty, ty), :]
        from_low = pltpu.roll(beyond, 1, 1) * h_on
        from_high = pltpu.roll(beyond, lanes - 1, 1) * e_on
        left_x = jnp.where(lane_t == 0, from_low, pltpu.roll(x, 1, 1))
        right_x = jnp.where(lane_t == lanes - 1, from_high, pltpu.roll(x, lanes - 1, 1))
        beside = before + after + left_y + right_y + left_x + right_x
        d_out[1, i] = d_out[1, i] - conduction * (6.0 * x - beside)


def main_call(electric, magnetic, conduct, temp_old, ids, lo, hi, m_lo, m_hi, own, other):
    s_dev, y_dev, lanes = conduct.shape
    s_ext, y_ext = s_dev + 2 * W, y_dev + 2 * W
    tall = TOP + y_ext + 8
    return pl.pallas_call(
        functools.partial(main_kernel, lax.axis_size("slab"), lax.axis_size("sub")),
        out_shape=[
            jax.ShapeDtypeStruct(electric.shape, F32),
            jax.ShapeDtypeStruct(magnetic.shape, F32),
            jax.ShapeDtypeStruct((3,) + temp_old.shape, F32),
        ],
        scratch_shapes=[
            pltpu.VMEM((3, s_ext, tall, lanes), F32),
            pltpu.VMEM((3, s_ext, tall, lanes), F32),
            pltpu.VMEM((s_ext, tall, lanes), F32),
            pltpu.VMEM((s_ext, y_ext, lanes), F32),
            pltpu.VMEM((s_ext, y_ext, lanes), F32),
            pltpu.VMEM((3, s_ext, 8, lanes), F32),
            pltpu.VMEM((3, s_ext, 8, lanes), F32),
            pltpu.VMEM((s_ext, 8, lanes), F32),
            pltpu.VMEM((s_ext, 8, lanes), F32),
            pltpu.VMEM((s_ext * 16, lanes), F32),
            pltpu.VMEM((s_ext // 8, y_ext, lanes), F32),
        ],
        compiler_params=pltpu.CompilerParams(vmem_limit_bytes=VMEM_LIMIT),
        name="leapfrog",
    )(electric, magnetic, conduct, temp_old, ids, lo, hi, m_lo, m_hi, own, other)


R = SWEEPS - 1
TTOP = 8


def thermal_kernel(
    n_slab, n_sub, z_ref, zo_ref, t_ref, cap_ref, lo_ref, hi_ref, ml_ref, mh_ref, other_ref,
    out_ref, d0, d1, r0, cs,
):
    ts, ty, lanes = t_ref.shape
    center, spread, rhos = chebyshev_constants(SWEEPS)
    slab_lo, slab_hi = inside_flags("slab", n_slab)
    sub_lo, sub_hi = inside_flags("sub", n_sub)
    comp = lax.axis_index("comp")
    y_ext = 24
    shift = 4
    chunk = pl.ds(TTOP, y_ext)
    above = pl.ds(TTOP + 1, y_ext)
    below = pl.ds(TTOP - 1, y_ext)
    for ref in (d0, d1, r0, cs):
        ref[...] = jnp.zeros_like(ref)
    per = lanes // ty
    caps = other_ref.shape[0] - ts // per
    for half, z in enumerate((z_ref, zo_ref)):
        r0[half, :, pl.ds(TTOP + shift - R, ty + 2 * R), :] = z[...]
    for i in range(ts):
        cs[0, i + 1, pl.ds(TTOP + shift, ty), :] = cap_ref[i]
        cs[0, i + 1, pl.ds(TTOP + shift - 1, 1), :] = ml_ref[3, i, pl.ds(W + 1, 1), :]
        cs[0, i + 1, pl.ds(TTOP + shift + ty, 1), :] = mh_ref[3, i, pl.ds(W + 1, 1), :]
        cs[1, i + 1, pl.ds(TTOP + shift, ty), :] = other_ref[caps + i // per, pl.ds((i % per) * ty, ty), :]
    cs[0, 0, pl.ds(TTOP + shift, ty), :] = lo_ref[lo_ref.shape[0] - 1, pl.ds(ty, ty), :]
    cs[0, ts + 1, pl.ds(TTOP + shift, ty), :] = hi_ref[hi_ref.shape[0] - 1, pl.ds(ty, ty), :]
    d0[...] = r0[...] * (1.0 / center)

    row = lax.broadcasted_iota(jnp.int32, (y_ext, lanes), 0)
    lane = lax.broadcasted_iota(jnp.int32, (y_ext, lanes), 1)
    in_y = ((row >= shift) | sub_lo) & ((row < shift + ty) | sub_hi)
    in_y = jnp.where(in_y, 1.0, 0.0)
    low_half = comp == 0

    def applied(ref, half, i, cap):
        v = ref[half, i, chunk, :]
        w = ref[1 - half, i, chunk, :]
        other_high = low_half if half == 0 else jnp.logical_not(low_half)
        from_low = jnp.where(other_high, 0.0, pltpu.roll(w, 1, 1))
        from_high = jnp.where(other_high, pltpu.roll(w, lanes - 1, 1), 0.0)
        left = jnp.where(lane == 0, from_low, pltpu.roll(v, 1, 1))
        right = jnp.where(lane == lanes - 1, from_high, pltpu.roll(v, lanes - 1, 1))
        beside = ref[half, i - 1, chunk, :] + ref[half, i + 1, chunk, :]
        beside = beside + ref[half, i, above, :] + ref[half, i, below, :] + left + right
        return v, cap * v + conduction * (6.0 * v - beside)

    for i in range(R - 1, ts + R + 1):
        inside = in_y
        if i < R:
            inside = inside * jnp.where(slab_lo, 1.0, 0.0)
        if i >= ts + R:
            inside = inside * jnp.where(slab_hi, 1.0, 0.0)
        for half in range(2):
            if half == 1 and not R <= i < ts + R:
                continue
            v, av = applied(d0, half, i, cs[half, i - 1, chunk, :])
            resid = (r0[half, i, chunk, :] - av) * inside
            r0[half, i, chunk, :] = resid
            d1[half, i, chunk, :] = (rhos[1] * rhos[0]) * v + (2.0 * rhos[1] / spread) * resid
    mine = pl.ds(TTOP + shift, ty)
    for i in range(R, ts + R):
        v, av = applied(d1, 0, i, cs[0, i - 1, chunk, :])
        resid = r0[0, i, chunk, :] - av
        last = (rhos[2] * rhos[1]) * v + (2.0 * rhos[2] / spread) * resid
        r0[0, i, chunk, :] = d0[0, i, chunk, :] + v + last
        out_ref[i - R] = t_ref[i - R] + r0[0, i, mine, :]


def thermal_call(z, z_other, temp_old, capacity, lo, hi, m_lo, m_hi, other):
    ts, ty, lanes = temp_old.shape
    wide = pltpu.VMEM((2, ts + 2 * R, TTOP + 24 + 8, lanes), F32)
    return pl.pallas_call(
        functools.partial(thermal_kernel, lax.axis_size("slab"), lax.axis_size("sub")),
        out_shape=jax.ShapeDtypeStruct(temp_old.shape, F32),
        scratch_shapes=[wide, wide, wide, pltpu.VMEM((2, ts + 2, TTOP + 24 + 8, lanes), F32)],
        compiler_params=pltpu.CompilerParams(vmem_limit_bytes=VMEM_LIMIT),
        name="conduction",
    )(z, z_other, temp_old, capacity, lo, hi, m_lo, m_hi, other)


def lookup_kernel(ids_ref, t_ref, lo_ref, hi_ref, c_ref, out_ref):
    ts, ty, lanes = t_ref.shape
    thermal = ts * ty
    s_dev, y_dev, _ = c_ref.shape
    rows = s_dev * y_dev // lanes
    columns = ids_ref[...].T
    tables = [split_two(r[...].reshape(thermal, lanes)) for r in (lo_ref, t_ref, hi_ref)]
    per = lanes // y_dev
    for a in range(rows):
        column = columns[:, a : a + 1]
        total = jnp.zeros((lanes, 2 * lanes), F32)
        for n in range(3):
            kinds = lax.broadcasted_iota(jnp.int32, (lanes, thermal), 1) + n * thermal
            chosen = jnp.where(kinds == column, 1.0, 0.0).astype(BF16)
            total = total + jnp.dot(chosen, tables[n], preferred_element_type=F32)
        looked = (total[:, :lanes] + total[:, lanes:]).reshape(per, y_dev, lanes)
        at = pl.ds(a * per, per)
        out_ref[at] = c_ref[at] / (1.0 + softening * looked * looked)


def lookup_call(ids, temp_new, lo, hi, conduct):
    return pl.pallas_call(
        lookup_kernel,
        out_shape=jax.ShapeDtypeStruct(conduct.shape, F32),
        compiler_params=pltpu.CompilerParams(vmem_limit_bytes=VMEM_LIMIT),
        name="lookup",
    )(ids, temp_new, lo, hi, conduct)


def sub_edges(values, depth):
    count = lax.axis_size("sub")
    index = lax.axis_index("sub")
    length = values.shape[1]
    if count == 2:
        start = jnp.where(index == 0, length - depth, 0)
        received = swapped(lax.dynamic_slice_in_dim(values, start, depth, axis=1), "sub")
        zero = jnp.zeros_like(received)
        return jnp.where(index == 0, zero, received), jnp.where(index == 0, received, zero)
    return (
        passed_along(values[:, length - depth :], "sub", 1),
        passed_along(values[:, :depth], "sub", -1),
    )


def on_device(electric, magnetic, conduct, temp_old, capacity, offsets, targets):
    lanes = conduct.shape[2]
    thermal = temp_old.shape[0] * temp_old.shape[1]
    ids = (offsets + 1) * thermal + targets
    ids_row = ids.reshape(1, -1)
    ids_square = ids.reshape(-1, lanes)

    up, dn = slab_messages(electric, magnetic, conduct, temp_old, capacity)
    lo, hi = passed_along(up, "slab", 1), passed_along(dn, "slab", -1)
    m_lo, m_hi = sub_exchange(electric, magnetic, conduct, temp_old, capacity, lo, hi)
    own = comp_pack(electric, magnetic, conduct, temp_old, capacity, lo, hi, m_lo, m_hi)
    other = swapped(own, "comp")
    electric, magnetic, sums = main_call(
        electric, magnetic, conduct, temp_old, ids_row, lo, hi, m_lo, m_hi, own, other
    )
    r0 = sums[1] + passed_along(sums[2], "slab", 1) + passed_along(sums[0], "slab", -1)
    y_lo, y_hi = sub_edges(r0, R)
    r_y = jnp.concatenate([y_lo, r0, y_hi], 1)
    s_lo = passed_along(r_y[-R:], "slab", 1)
    s_hi = passed_along(r_y[:R], "slab", -1)
    z = jnp.concatenate([s_lo, r_y, s_hi], 0)
    z_other = swapped(z, "comp")
    temp_new = thermal_call(z, z_other, temp_old, capacity, lo, hi, m_lo, m_hi, other)
    t_lo = passed_along(temp_new, "slab", 1)
    t_hi = passed_along(temp_new, "slab", -1)
    conduct_new = lookup_call(ids_square, temp_new, t_lo, t_hi, conduct)
    return (electric, magnetic, temp_new, conduct_new)


def solution(mesh):
    placed = (
        P(None, ("groups", "slab"), "sub", "comp"),
        P(None, ("groups", "slab"), "sub", "comp"),
        P(("groups", "slab"), "sub", "comp"),
        P(("groups", "slab"), "sub", "comp"),
        P(("groups", "slab"), "sub", "comp"),
        P(("groups", "slab"), "sub", "comp"),
        P(("groups", "slab"), "sub", "comp"),
    )
    return jax.shard_map(
        on_device,
        mesh=mesh,
        in_specs=placed,
        out_specs=(
            P(None, ("groups", "slab"), "sub", "comp"),
            P(None, ("groups", "slab"), "sub", "comp"),
            P(("groups", "slab"), "sub", "comp"),
            P(("groups", "slab"), "sub", "comp"),
        ),
        check_vma=False,
    )
```

profile of v0, /device:TPU:0, one launch (start us, length us, event | category | flops | bytes accessed | tf_op | source)
XLA Modules:
  0.0 155.9 jit_solution(4024675645902137163)
XLA Ops:
  0.6 0.8 bitcast_dynamic-update-slice_fusion.10
  1.4 0.8 bitcast_dynamic-update-slice_fusion.6
  2.3 0.9 bitcast_dynamic-update-slice_fusion.1
  3.2 0.9 bitcast_dynamic-update-slice_fusion
  4.1 0.8 bitcast_dynamic-update-slice_fusion.9
  4.9 0.8 bitcast_dynamic-update-slice_fusion.8
  5.7 0.8 bitcast_dynamic-update-slice_fusion.7
  6.5 0.8 bitcast_dynamic-update-slice_fusion.3
  7.3 0.8 bitcast_dynamic-update-slice_fusion.2
  8.2 0.7 slice_bitcast_fusion.2
  8.9 0.8 slice_dynamic-update-slice_fusion
  9.8 5.0 %collective-permute-start = (f32[27,32,128]{2,1,0:T(8,128)S(1)}, f32[27,32,128]{2,1,0:T(8,128)S(1)}, u32[]{:S(2)}, u32[]{:S(2)}) collective-permute-start(f32[27,32,128]{2,1,0:T(8,128)S(1)} %constant_dynamic-update-slice_fusion), channel_id=1, source_target_pairs={{0,4},{4,8},{8,12},{1,5},{5,9},{9,13},{2,6},{6,10},{10,14},{3,7},{... | collective-permute-start | bytes 1327112 | tf_op jit(solution)/shard_map/ppermute | solution.py:39
  14.7 1.3 collective-permute-start.1
  16.0 11.2 %collective-permute-done.1.hi_ref = f32[24,32,128]{2,1,0:T(8,128)S(1)} collective-permute-done((f32[24,32,128]{2,1,0:T(8,128)S(1)}, f32[24,32,128]{2,1,0:T(8,128)S(1)}, u32[]{:S(2)}, u32[]{:S(2)}) %collective-permute-start.1) | collective-permute-done | bytes 393248 | tf_op jit(solution)/shard_map/ppermute | solution.py:39
  27.2 0.8 copy-done.2
  28.0 0.8 copy-done.1
  28.7 3.4 %sub_pack.1 = f32[4,40,8,128]{3,2,1,0:T(8,128)} custom-call(f32[3,32,32,128]{3,2,1,0:T(8,128)} %e_ref.5, f32[3,32,32,128]{3,2,1,0:T(8,128)} %h_ref.5, f32[32,32,128]{2,1,0:T(8,128)} %c_ref.7, f32[16,16,128]{2,1,0:T(8,128)} %t_ref.7, f32[16,16,128]{2,1,0:T(8,128)} %cap_ref.5, f32[27,32,128]{2,1,0:T(8,128)} %copy-done.1, f32[24,32,128]{2,1,0:T(8,128)} %copy-done.2), custom_call_target="tpu_custom_call" | custom-call | tf_op jit(solution)/shard_map/sub_pack/pallas_call | solution.py:145
  32.1 1.5 collective-permute-start.2
  33.6 14.0 %collective-permute-done.2.ml_ref.mh_ref = f32[4,40,8,128]{3,2,1,0:T(8,128)S(1)} collective-permute-done((f32[4,40,8,128]{3,2,1,0:T(8,128)}, f32[4,40,8,128]{3,2,1,0:T(8,128)S(1)}, u32[]{:S(2)}, u32[]{:S(2)}) %collective-permute-start.2) | collective-permute-done | bytes 655392 | tf_op jit(solution)/shard_map/ppermute | solution.py:43
  47.6 0.8 copy-done
  48.4 5.6 %comp_pack.1.own_ref = f32[14,128,128]{2,1,0:T(8,128)} custom-call(f32[3,32,32,128]{3,2,1,0:T(8,128)} %e_ref.5, f32[3,32,32,128]{3,2,1,0:T(8,128)} %h_ref.5, f32[32,32,128]{2,1,0:T(8,128)} %c_ref.7, f32[16,16,128]{2,1,0:T(8,128)} %t_ref.7, f32[16,16,128]{2,1,0:T(8,128)} %cap_ref.5, f32[27,32,128]{2,1,0:T(8,128)} %copy-done.1, f32[24,32,128]{2,1,0:T(8,128)} %copy-done.2, ...), custom_call_target="tpu_custom_call" | custom-call | tf_op jit(solution)/shard_map/comp_pack/pallas_call | solution.py:222
  54.0 0.5 broadcast.5
  54.5 0.7 fusion.1
  55.2 0.7 reshape.14.ids_ref
  55.9 0.8 collective-permute-done.3.other_ref
  56.7 0.9 copy-done.3
  57.6 54.3 %leapfrog.1 = (f32[3,32,32,128]{3,2,1,0:T(8,128)}, f32[3,32,32,128]{3,2,1,0:T(8,128)}, f32[3,16,16,128]{3,2,1,0:T(8,128)}) custom-call(f32[3,32,32,128]{3,2,1,0:T(8,128)} %e_ref.5, f32[3,32,32,128]{3,2,1,0:T(8,128)} %h_ref.5, f32[32,32,128]{2,1,0:T(8,128)} %c_ref.7, f32[16,16,128]{2,1,0:T(8,128)} %t_ref.7, s32[1,1024]{1,0:T(1,128)} %reshape.14.ids_ref, ...), custom_call_target="tpu_custom_call" | custom-call | tf_op jit(solution)/shard_map/leapfrog/pallas_call | solution.py:462
  111.9 1.0 slice_bitcast_fusion.1
  112.9 3.5 %collective-permute-start.4 = (f32[16,16,128]{2,1,0:T(8,128)S(1)}, f32[16,16,128]{2,1,0:T(8,128)S(1)}, u32[]{:S(2)}, u32[]{:S(2)}) collective-permute-start(f32[16,16,128]{2,1,0:T(8,128)S(1)} %get-tuple-element.20), channel_id=1, source_target_pairs={{0,4},{4,8},{8,12},{1,5},{5,9},{9,13},{2,6},{6,10},{10,14},{3,7},{... | collective-permute-start | bytes 393224 | tf_op jit(solution)/shard_map/ppermute | solution.py:39
  116.4 1.3 collective-permute-start.5
  117.7 1.7 %collective-permute-done.4 = f32[16,16,128]{2,1,0:T(8,128)S(1)} collective-permute-done((f32[16,16,128]{2,1,0:T(8,128)S(1)}, f32[16,16,128]{2,1,0:T(8,128)S(1)}, u32[]{:S(2)}, u32[]{:S(2)}) %collective-permute-start.4) | collective-permute-done | bytes 131104 | tf_op jit(solution)/shard_map/ppermute | solution.py:39
  119.4 4.1 %collective-permute-done.5 = f32[16,16,128]{2,1,0:T(8,128)S(1)} collective-permute-done((f32[16,16,128]{2,1,0:T(8,128)S(1)}, f32[16,16,128]{2,1,0:T(8,128)S(1)}, u32[]{:S(2)}, u32[]{:S(2)}) %collective-permute-start.5) | collective-permute-done | bytes 131104 | tf_op jit(solution)/shard_map/ppermute | solution.py:39
  123.6 0.9 fusion
  124.5 1.5 collective-permute-start.6
  126.1 2.3 %collective-permute-done.6 = f32[16,2,128]{2,1,0:T(2,128)S(1)} collective-permute-done((f32[16,2,128]{2,1,0:T(2,128)S(1)}, f32[16,2,128]{2,1,0:T(2,128)S(1)}, u32[]{:S(2)}, u32[]{:S(2)}) %collective-permute-start.6) | collective-permute-done | bytes 16416 | tf_op jit(solution)/shard_map/ppermute | solution.py:43
  128.3 3.5 %collective-permute-start.7 = (f32[2,20,128]{2,1,0:T(8,128)S(1)}, f32[2,20,128]{2,1,0:T(8,128)S(1)}, u32[]{:S(2)}, u32[]{:S(2)}) collective-permute-start(f32[2,20,128]{2,1,0:T(8,128)S(1)} %get-tuple-element.22), channel_id=1, source_target_pairs={{0,4},{4,8},{8,12},{1,5},{5,9},{9,13},{2,6},{6,10},{10,14},{3,7},{... | collective-permute-start | bytes 61448 | tf_op jit(solution)/shard_map/ppermute | solution.py:39
  131.8 1.3 collective-permute-start.8
  133.3 4.2 %collective-permute-done.8 = f32[2,20,128]{2,1,0:T(8,128)S(1)} collective-permute-done((f32[2,20,128]{2,1,0:T(8,128)S(1)}, f32[2,20,128]{2,1,0:T(8,128)S(1)}, u32[]{:S(2)}, u32[]{:S(2)}) %collective-permute-start.8) | collective-permute-done | bytes 20512 | tf_op jit(solution)/shard_map/ppermute | solution.py:39
  137.7 1.5 collective-permute-done.9.zo_ref
  139.2 0.7 copy-done.5
  139.9 3.6 %conduction.1.t_ref = f32[16,16,128]{2,1,0:T(8,128)} custom-call(f32[20,20,128]{2,1,0:T(8,128)} %copy-done.4, f32[20,20,128]{2,1,0:T(8,128)} %copy-done.5, f32[16,16,128]{2,1,0:T(8,128)} %t_ref.7, f32[16,16,128]{2,1,0:T(8,128)} %cap_ref.5, f32[27,32,128]{2,1,0:T(8,128)} %copy-done.1, f32[24,32,128]{2,1,0:T(8,128)} %copy-done.2, f32[4,40,8,128]{3,2,1,0:T(8,128)} %copy-done, ...), custom_call_target="tpu_custom_call" | custom-call | tf_op jit(solution)/shard_map/conduction/pallas_call | solution.py:563
  143.5 1.3 collective-permute-start.11
  144.8 4.6 %collective-permute-start.10 = (f32[16,16,128]{2,1,0:T(8,128)}, f32[16,16,128]{2,1,0:T(8,128)S(1)}, u32[]{:S(2)}, u32[]{:S(2)}) collective-permute-start(f32[16,16,128]{2,1,0:T(8,128)} %conduction.1.t_ref), channel_id=1, source_target_pairs={{0,4},{4,8},{8,12},{1,5},{5,9},{9,13},{2,6},{6,10},{10,14},{3,7},{... | collective-permute-start | bytes 393224 | tf_op jit(solution)/shard_map/ppermute | solution.py:39
  149.4 0.6 reshape.15.ids_ref
  150.0 1.1 collective-permute-done.11.hi_ref
  151.2 1.3 collective-permute-done.10.lo_ref
  152.5 0.6 copy-done.7
  153.1 2.8 %lookup.1 = f32[32,32,128]{2,1,0:T(8,128)} custom-call(s32[8,128]{1,0:T(8,128)} %reshape.15.ids_ref, f32[16,16,128]{2,1,0:T(8,128)} %conduction.1.t_ref, f32[16,16,128]{2,1,0:T(8,128)} %copy-done.7, f32[16,16,128]{2,1,0:T(8,128)} %copy-done.6, f32[32,32,128]{2,1,0:T(8,128)} %c_ref.7), custom_call_target="tpu_custom_call" | custom-call | tf_op jit(solution)/shard_map/lookup/pallas_call | solution.py:593
  (24 shorter events, 0.4 us)
Async XLA Ops:
  9.8 17.4 %collective-permute-start = (f32[27,32,128]{2,1,0:T(8,128)S(1)}, f32[27,32,128]{2,1,0:T(8,128)S(1)}, u32[]{:S(2)}, u32[]{:S(2)}) collective-permute-start(f32[27,32,128]{2,1,0:T(8,128)S(1)} %constant_dynamic-update-slice_fusion), channel_id=1, source_target_pairs={{0,4},{4,8},{8,12},{1,5},{5,9},{9,13},{2,6},{6,10},{10,14},{3,7},{... | collective-permute-start | bytes 1327112 | tf_op jit(solution)/shard_map/ppermute | solution.py:39
  14.7 12.5 %collective-permute-start.1 = (f32[24,32,128]{2,1,0:T(8,128)S(1)}, f32[24,32,128]{2,1,0:T(8,128)S(1)}, u32[]{:S(2)}, u32[]{:S(2)}) collective-permute-start(f32[24,32,128]{2,1,0:T(8,128)S(1)} %constant_dynamic-update-slice_fusion.1), channel_id=1, source_target_pairs={{4,0},{8,4},{12,8},{5,1},{9,5},{13,9},{6,2},{10,6},{14,10},{7,3},{... | collective-permute-start | bytes 1179656 | tf_op jit(solution)/shard_map/ppermute | solution.py:39
  27.2 0.8 copy-start.2
  28.0 0.8 copy-start.1
  32.1 22.4 %copy-start.8 = (s32[32,32,1]{1,2,0:T(1,128)S(1)}, s32[32,32,1]{1,2,0:T(1,128)}, u32[]{:S(2)}) copy-start(s32[32,32,1]{1,2,0:T(1,128)} %param.13) | copy-start | bytes 12292
  32.1 22.4 %copy-start.9 = (s32[32,32,1]{1,2,0:T(1,128)S(1)}, s32[32,32,1]{1,2,0:T(1,128)}, u32[]{:S(2)}) copy-start(s32[32,32,1]{1,2,0:T(1,128)} %param.12) | copy-start | bytes 12292
  32.1 15.5 %collective-permute-start.2 = (f32[4,40,8,128]{3,2,1,0:T(8,128)}, f32[4,40,8,128]{3,2,1,0:T(8,128)S(1)}, u32[]{:S(2)}, u32[]{:S(2)}) collective-permute-start(f32[4,40,8,128]{3,2,1,0:T(8,128)} %sub_pack.1), channel_id=1, source_target_pairs={{0,2},{2,0},{1,3},{3,1},{4,6},{6,4},{5,7},{7,5},{8,10},{10,8},{9,1... | collective-permute-start | bytes 1966088 | tf_op jit(solution)/shard_map/ppermute | solution.py:43
  47.6 0.8 copy-start
  54.0 2.7 %collective-permute-start.3 = (f32[14,128,128]{2,1,0:T(8,128)}, f32[14,128,128]{2,1,0:T(8,128)S(1)}, u32[]{:S(2)}, u32[]{:S(2)}) collective-permute-start(f32[14,128,128]{2,1,0:T(8,128)} %comp_pack.1.own_ref), channel_id=1, source_target_pairs={{0,1},{1,0},{2,3},{3,2},{4,5},{5,4},{6,7},{7,6},{8,9},{9,8},{10,11... | collective-permute-start | bytes 2752520 | tf_op jit(solution)/shard_map/ppermute | solution.py:43
  56.7 0.9 copy-start.3
  112.9 6.5 %collective-permute-start.4 = (f32[16,16,128]{2,1,0:T(8,128)S(1)}, f32[16,16,128]{2,1,0:T(8,128)S(1)}, u32[]{:S(2)}, u32[]{:S(2)}) collective-permute-start(f32[16,16,128]{2,1,0:T(8,128)S(1)} %get-tuple-element.20), channel_id=1, source_target_pairs={{0,4},{4,8},{8,12},{1,5},{5,9},{9,13},{2,6},{6,10},{10,14},{3,7},{... | collective-permute-start | bytes 393224 | tf_op jit(solution)/shard_map/ppermute | solution.py:39
  116.4 7.2 %collective-permute-start.5 = (f32[16,16,128]{2,1,0:T(8,128)S(1)}, f32[16,16,128]{2,1,0:T(8,128)S(1)}, u32[]{:S(2)}, u32[]{:S(2)}) collective-permute-start(f32[16,16,128]{2,1,0:T(8,128)S(1)} %get-tuple-element.21), channel_id=1, source_target_pairs={{4,0},{8,4},{12,8},{5,1},{9,5},{13,9},{6,2},{10,6},{14,10},{7,3},{... | collective-permute-start | bytes 393224 | tf_op jit(solution)/shard_map/ppermute | solution.py:39
  124.5 3.8 %collective-permute-start.6 = (f32[16,2,128]{2,1,0:T(2,128)S(1)}, f32[16,2,128]{2,1,0:T(2,128)S(1)}, u32[]{:S(2)}, u32[]{:S(2)}) collective-permute-start(f32[16,2,128]{2,1,0:T(2,128)S(1)} %constant_dynamic-slice_fusion), channel_id=1, source_target_pairs={{0,2},{2,0},{1,3},{3,1},{4,6},{6,4},{5,7},{7,5},{8,10},{10,8},{9,1... | collective-permute-start | bytes 49160 | tf_op jit(solution)/shard_map/ppermute | solution.py:43
  128.3 5.0 %collective-permute-start.7 = (f32[2,20,128]{2,1,0:T(8,128)S(1)}, f32[2,20,128]{2,1,0:T(8,128)S(1)}, u32[]{:S(2)}, u32[]{:S(2)}) collective-permute-start(f32[2,20,128]{2,1,0:T(8,128)S(1)} %get-tuple-element.22), channel_id=1, source_target_pairs={{0,4},{4,8},{8,12},{1,5},{5,9},{9,13},{2,6},{6,10},{10,14},{3,7},{... | collective-permute-start | bytes 61448 | tf_op jit(solution)/shard_map/ppermute | solution.py:39
  131.8 5.7 %collective-permute-start.8 = (f32[2,20,128]{2,1,0:T(8,128)S(1)}, f32[2,20,128]{2,1,0:T(8,128)S(1)}, u32[]{:S(2)}, u32[]{:S(2)}) collective-permute-start(f32[2,20,128]{2,1,0:T(8,128)S(1)} %get-tuple-element.23), channel_id=1, source_target_pairs={{4,0},{8,4},{12,8},{5,1},{9,5},{13,9},{6,2},{10,6},{14,10},{7,3},{... | collective-permute-start | bytes 61448 | tf_op jit(solution)/shard_map/ppermute | solution.py:39
  137.6 1.6 %copy-start.4 = (f32[20,20,128]{2,1,0:T(8,128)}, f32[20,20,128]{2,1,0:T(8,128)S(1)}, u32[]{:S(2)}) copy-start(f32[20,20,128]{2,1,0:T(8,128)S(1)} %pad_maximum_fusion.z_ref) | copy-start | bytes 614404
  137.6 1.6 %collective-permute-start.9 = (f32[20,20,128]{2,1,0:T(8,128)S(1)}, f32[20,20,128]{2,1,0:T(8,128)S(1)}, u32[]{:S(2)}, u32[]{:S(2)}) collective-permute-start(f32[20,20,128]{2,1,0:T(8,128)S(1)} %pad_maximum_fusion.z_ref), channel_id=1, source_target_pairs={{0,1},{1,0},{2,3},{3,2},{4,5},{5,4},{6,7},{7,6},{8,9},{9,8},{10,11... | collective-permute-start | bytes 614408 | tf_op jit(solution)/shard_map/ppermute | solution.py:43
  139.2 0.7 copy-start.5
  143.5 7.6 %collective-permute-start.11 = (f32[16,16,128]{2,1,0:T(8,128)}, f32[16,16,128]{2,1,0:T(8,128)S(1)}, u32[]{:S(2)}, u32[]{:S(2)}) collective-permute-start(f32[16,16,128]{2,1,0:T(8,128)} %conduction.1.t_ref), channel_id=1, source_target_pairs={{4,0},{8,4},{12,8},{5,1},{9,5},{13,9},{6,2},{10,6},{14,10},{7,3},{... | collective-permute-start | bytes 393224 | tf_op jit(solution)/shard_map/ppermute | solution.py:39
  144.8 7.6 %collective-permute-start.10 = (f32[16,16,128]{2,1,0:T(8,128)}, f32[16,16,128]{2,1,0:T(8,128)S(1)}, u32[]{:S(2)}, u32[]{:S(2)}) collective-permute-start(f32[16,16,128]{2,1,0:T(8,128)} %conduction.1.t_ref), channel_id=1, source_target_pairs={{0,4},{4,8},{8,12},{1,5},{5,9},{9,13},{2,6},{6,10},{10,14},{3,7},{... | collective-permute-start | bytes 393224 | tf_op jit(solution)/shard_map/ppermute | solution.py:39
  151.2 1.3 copy-start.6
  152.5 0.7 copy-start.7
where the time goes:
time: 157 us; the launch traced here: 156 us
  Pallas kernels  69.7 us (44%)
  waiting for transfers between devices  42.4 us (27%)
  starting transfers between devices  24.7 us (16%)
  local copies, waits for them, and re-layouts  16.6 us (11%)
  other arithmetic  1.7 us (1%)
    pallas_call x1, Pallas kernels, main_call(): pl.pallas_call(functools.partial(main_kernel, lax.axis_size('slab'), lax....  54.3 us
    ppermute x8, waiting for transfers between devices, passed_along(): return lax.ppermute(array, axis, pairs)  23.9 us
    ppermute x8, starting transfers between devices, passed_along(): return lax.ppermute(array, axis, pairs)  21.6 us
    ppermute x4, waiting for transfers between devices, swapped(): return lax.ppermute(array, axis, [(0, 1), (1, 0)])  18.5 us
    unnamed x30, local copies, waits for them, and re-layouts  13 us
    pallas_call x1, Pallas kernels, comp_pack(): pl.pallas_call(functools.partial(comp_pack_kernel, lax.axis_size('sub')),...  5.55 us
    pallas_call x1, Pallas kernels, thermal_call(): pl.pallas_call(functools.partial(thermal_kernel, lax.axis_size('slab'), l...  3.65 us
    pallas_call x1, Pallas kernels, sub_exchange(): pl.pallas_call(functools.partial(sub_pack_kernel, edges), out_shape=[shap...  3.35 us
  transfers between devices with their start and end apart: 12, of which 11 were waited for; matrix products, arithmetic and copies ran while one was open for 2% of the time, Pallas kernels for 0%

commit v1 on v0

--- a/solution.py
+++ b/solution.py
@@ -18,7 +18,8 @@
 
 F32 = jnp.float32
 BF16 = jnp.bfloat16
-VMEM_LIMIT = 56 * 1024 * 1024
+VMEM_LIMIT = 26 * 1024 * 1024
+SMALL_LIMIT = 12 * 1024 * 1024
 
 
 def chebyshev_constants(sweep_count):
@@ -53,30 +54,6 @@
         for r in range(dn_rows):
             dn.append((f, r))
     return up, dn
-
-
-def slab_messages(electric, magnetic, conduct, temp_old, capacity):
-    s_dev = conduct.shape[0]
-
-    def rows(f, a, b):
-        if f < 3:
-            return electric[f, a:b]
-        if f < 6:
-            return magnetic[f - 3, a:b]
-        return conduct[a:b]
-
-    def ends(i):
-        return jnp.concatenate([temp_old[i], capacity[i]], 0)[None]
-
-    up, dn = [], []
-    for f in range(7):
-        up_rows = W if f in (0, 1, 2, 4, 5) else W - 1
-        dn_rows = W if f in (1, 2) else W - 1
-        up.append(rows(f, s_dev - up_rows, s_dev))
-        dn.append(rows(f, 0, dn_rows))
-    up.append(ends(temp_old.shape[0] - 1))
-    dn.append(ends(0))
-    return jnp.concatenate(up, 0), jnp.concatenate(dn, 0)
 
 
 def row_source(f, i, s_dev, own, lo, hi, up_index, dn_index):
@@ -103,64 +80,110 @@
     )
 
 
-def sub_pack_kernel(edges, e_ref, h_ref, c_ref, t_ref, cap_ref, lo_ref, hi_ref, *out_refs):
+def edge_rows(edge, y_dev, ty):
+    if edge == "high":
+        return y_dev - W, ty - 1
+    if edge == "low":
+        return 0, 0
+    upper = lax.axis_index("sub") == 0
+    return jnp.where(upper, y_dev - W, 0), jnp.where(upper, ty - 1, 0)
+
+
+def pack_kernel(edges, e_ref, h_ref, c_ref, t_ref, cap_ref, up_ref, dn_ref, *out_refs):
     s_dev, y_dev = c_ref.shape[0], c_ref.shape[1]
-    ty = t_ref.shape[1]
+    ts, ty = t_ref.shape[0], t_ref.shape[1]
+    for out, planes, i in zip((up_ref, dn_ref), plane_list(s_dev), (ts - 1, 0)):
+        for n, (f, r) in enumerate(planes):
+            if f < 3:
+                out[n] = e_ref[f, r]
+            elif f < 6:
+                out[n] = h_ref[f - 3, r]
+            else:
+                out[n] = c_ref[r]
+        out[len(planes), pl.ds(0, ty), :] = t_ref[i]
+        out[len(planes), pl.ds(ty, ty), :] = cap_ref[i]
+    for edge, out in zip(edges, out_refs):
+        y0, t0 = edge_rows(edge, y_dev, ty)
+        for c in range(3):
+            for r in range(s_dev):
+                out[c * s_dev + r, pl.ds(0, W), :] = e_ref[c, r, pl.ds(y0, W), :]
+                out[c * s_dev + r, pl.ds(W, W), :] = h_ref[c, r, pl.ds(y0, W), :]
+        for r in range(s_dev):
+            out[3 * s_dev + r // 2, pl.ds((r % 2) * W, W), :] = c_ref[r, pl.ds(y0, W), :]
+        base = 3 * s_dev + s_dev // 2
+        for i in range(ts):
+            out[base + i // 8, pl.ds(i % 8, 1), :] = t_ref[i, pl.ds(t0, 1), :]
+            out[base + (ts + i) // 8, pl.ds(i % 8, 1), :] = cap_ref[i, pl.ds(t0, 1), :]
+
+
+def corner_kernel(edges, s_dev, ty, lo_ref, hi_ref, *out_refs):
     up_index, dn_index = indices_of(s_dev)
-    own = (e_ref, h_ref, c_ref)
+    y_dev, lanes = lo_ref.shape[1], lo_ref.shape[2]
+    zero = jnp.zeros((W, lanes), F32)
     for edge, out in zip(edges, out_refs):
-        if edge == "high":
-            y0, t0 = y_dev - W, ty - 1
-        elif edge == "low":
-            y0, t0 = 0, 0
-        else:
-            upper = lax.axis_index("sub") == 0
-            y0 = jnp.where(upper, y_dev - W, 0)
-            t0 = jnp.where(upper, ty - 1, 0)
-        zero = jnp.zeros((W, 128), F32)
-        for c in range(4):
-            for i in range(s_dev + 2 * W):
-                for half in range(2):
-                    if c == 3 and half == 1:
-                        continue
-                    f = 6 if c == 3 else c + 3 * half
-                    source = row_source(f, i, s_dev, own, lo_ref, hi_ref, up_index, dn_index)
-                    if source is None:
-                        value = zero
-                    else:
-                        ref, at = source
-                        value = ref[at + (pl.ds(y0, W), slice(None))]
-                    out[c, i, pl.ds(half * W, W), :] = value
-        out[3, :, pl.ds(W, W), :] = jnp.zeros((s_dev + 2 * W, W, 128), F32)
-        for i in range(t_ref.shape[0]):
-            out[3, i, pl.ds(W, 1), :] = t_ref[i, pl.ds(t0, 1), :]
-            out[3, i, pl.ds(W + 1, 1), :] = cap_ref[i, pl.ds(t0, 1), :]
-
-
-def sub_exchange(electric, magnetic, conduct, temp_old, capacity, lo, hi):
-    count = lax.axis_size("sub")
-    edges = ("either",) if count == 2 else ("high", "low")
-    s_ext = conduct.shape[0] + 2 * W
-    shape = jax.ShapeDtypeStruct((4, s_ext, 2 * W, conduct.shape[2]), F32)
-    messages = pl.pallas_call(
-        functools.partial(sub_pack_kernel, edges),
-        out_shape=[shape] * len(edges),
-        compiler_params=pltpu.CompilerParams(vmem_limit_bytes=VMEM_LIMIT),
-        name="sub_pack",
-    )(electric, magnetic, conduct, temp_old, capacity, lo, hi)
-    if count == 2:
+        y0, _ = edge_rows(edge, y_dev, ty)
+        for f in range(7):
+            for k in range(2 * W):
+                i = k if k < W else s_dev + k
+                source = row_source(f, i, s_dev, None, lo_ref, hi_ref, up_index, dn_index)
+                value = zero if source is None else source[0][source[1] + (pl.ds(y0, W), slice(None))]
+                if f < 6:
+                    out[(f % 3) * 2 * W + k, pl.ds((f // 3) * W, W), :] = value
+                else:
+                    out[6 * W + k // 2, pl.ds((k % 2) * W, W), :] = value
+
+
+def y_tile(m_ref, k_ref, c, i, s_dev):
+    r = i - W
+    if 0 <= r < s_dev:
+        return m_ref, (c * s_dev + r if c < 3 else 3 * s_dev + r // 2)
+    k = i if r < 0 else i - s_dev
+    return k_ref, (c * 2 * W + k if c < 3 else 6 * W + k // 2)
+
+
+def sub_pass(messages):
+    if len(messages) == 1:
         received = swapped(messages[0], "sub")
         return received, received
     return passed_along(messages[0], "sub", 1), passed_along(messages[1], "sub", -1)
 
 
+def halo_exchange(electric, magnetic, conduct, temp_old, capacity):
+    s_dev, y_dev, lanes = conduct.shape
+    ts, ty, _ = temp_old.shape
+    edges = ("either",) if lax.axis_size("sub") == 2 else ("high", "low")
+    up, dn = plane_list(s_dev)
+    tiles = 3 * s_dev + s_dev // 2 + 2 * ts // 8
+    up, dn, *messages = pl.pallas_call(
+        functools.partial(pack_kernel, edges),
+        out_shape=[
+            jax.ShapeDtypeStruct((len(up) + 1, y_dev, lanes), F32),
+            jax.ShapeDtypeStruct((len(dn) + 1, y_dev, lanes), F32),
+        ]
+        + [jax.ShapeDtypeStruct((tiles, 8, lanes), F32)] * len(edges),
+        compiler_params=pltpu.CompilerParams(vmem_limit_bytes=SMALL_LIMIT),
+        name="pack",
+    )(electric, magnetic, conduct, temp_old, capacity)
+    m_lo, m_hi = sub_pass(messages)
+    lo, hi = passed_along(up, "slab", 1), passed_along(dn, "slab", -1)
+    corners = pl.pallas_call(
+        functools.partial(corner_kernel, edges, s_dev, ty),
+        out_shape=[jax.ShapeDtypeStruct((7 * W, 8, lanes), F32)] * len(edges),
+        compiler_params=pltpu.CompilerParams(vmem_limit_bytes=SMALL_LIMIT),
+        name="corners",
+    )(lo, hi)
+    k_lo, k_hi = sub_pass(corners)
+    return lo, hi, m_lo, m_hi, k_lo, k_hi
+
+
 def inside_flags(axis, count):
     index = lax.axis_index(axis)
     return (index > 0), (index < count - 1)
 
 
 def comp_pack_kernel(
-    n_sub, e_ref, h_ref, c_ref, t_ref, cap_ref, lo_ref, hi_ref, ml_ref, mh_ref, out_ref, a_ref, b_ref
+    n_sub, e_ref, h_ref, c_ref, t_ref, cap_ref, lo_ref, hi_ref, ml_ref, mh_ref, kl_ref, kh_ref,
+    out_ref, a_ref, b_ref,
 ):
     s_dev, y_dev, lanes = c_ref.shape
     y_ext = y_dev + 2 * W
@@ -185,7 +208,7 @@
                 here = lane == group
                 here_own = jnp.concatenate([here] * (y_dev // 8), 0)
                 for which in range(2):
-                    if c == 3 and which == 1:
+                    if c == 3 and which != i % 2:
                         continue
                     f = 6 if c == 3 else c + 3 * which
                     source = row_source(f, i, s_dev, own, lo_ref, hi_ref, up_index, dn_index)
@@ -197,8 +220,10 @@
                         acc_a = jnp.where(here_own, moved, acc_a)
                     else:
                         acc_b = jnp.where(here_own, moved, acc_b)
-                acc_lo = jnp.where(here, pltpu.roll(ml_ref[c, i], shift, 1), acc_lo)
-                acc_hi = jnp.where(here, pltpu.roll(mh_ref[c, i], shift, 1), acc_hi)
+                low, at = y_tile(ml_ref, kl_ref, c, i, s_dev)
+                high, _ = y_tile(mh_ref, kh_ref, c, i, s_dev)
+                acc_lo = jnp.where(here, pltpu.roll(low[at], shift, 1), acc_lo)
+                acc_hi = jnp.where(here, pltpu.roll(high[at], shift, 1), acc_hi)
         acc_lo = jnp.where(has_lo, acc_lo, 0.0)
         acc_hi = jnp.where(has_hi, acc_hi, 0.0)
         a_ref[pl.ds(0, W), :] = acc_lo[:W]
@@ -216,16 +241,16 @@
         out_ref[2 * blocks + rows + n] = cap_ref[pl.ds(n * per, per)].reshape(lanes, lanes)
 
 
-def comp_pack(electric, magnetic, conduct, temp_old, capacity, lo, hi, m_lo, m_hi):
+def comp_pack(electric, magnetic, conduct, temp_old, capacity, *halos):
     s_dev, y_dev, lanes = conduct.shape
     count = 2 * ((s_dev + 2 * W) // 8) + 2 * (temp_old.shape[0] * temp_old.shape[1] // lanes)
     return pl.pallas_call(
         functools.partial(comp_pack_kernel, lax.axis_size("sub")),
         out_shape=jax.ShapeDtypeStruct((count, lanes, lanes), F32),
         scratch_shapes=[pltpu.VMEM((lanes, lanes), F32)] * 2,
-        compiler_params=pltpu.CompilerParams(vmem_limit_bytes=VMEM_LIMIT),
+        compiler_params=pltpu.CompilerParams(vmem_limit_bytes=SMALL_LIMIT),
         name="comp_pack",
-    )(electric, magnetic, conduct, temp_old, capacity, lo, hi, m_lo, m_hi)
+    )(electric, magnetic, conduct, temp_old, capacity, *halos)
 
 
 TOP = 8
@@ -234,7 +259,11 @@
 def coefficients(conduct, inside):
     damping = 0.5 * time_step * conduct
     inverse = inside / (1.0 + damping)
-    return (1.0 - damping) * inverse, time_step * inverse
+    return (1.0 - damping) * inverse, (time_step * time_step) * inverse
+
+
+def scaled(values, scale):
+    return values if scale == 1.0 else values * scale
 
 
 def split_two(values):
@@ -245,7 +274,8 @@
 
 def main_kernel(
     n_slab, n_sub,
-    e_ref, h_ref, c_ref, t_ref, ids_ref, lo_ref, hi_ref, ml_ref, mh_ref, own_ref, other_ref,
+    e_ref, h_ref, c_ref, t_ref, ids_ref, lo_ref, hi_ref, ml_ref, mh_ref, kl_ref, kh_ref,
+    own_ref, other_ref,
     e_out, h_out, d_out,
     es, hs, ce, ch, heat, sde, sdh, sce, sch, bt, bp,
 ):
@@ -257,17 +287,19 @@
     sub_lo, sub_hi = inside_flags("sub", n_sub)
     comp = lax.axis_index("comp")
 
-    def place(ref, at, f, i, half, c):
+    def place(ref, at, f, i, half, c, scale=1.0):
         source = row_source(f, i, s_dev, own, lo_ref, hi_ref, up_index, dn_index)
         if source is None:
             ref[at + (pl.ds(TOP + W, y_dev), slice(None))] = jnp.zeros((y_dev, lanes), F32)
         else:
             s, sat = source
-            ref[at + (pl.ds(TOP + W, y_dev), slice(None))] = s[sat]
-        low = ml_ref[c, i, pl.ds(half * W, W), :]
-        high = mh_ref[c, i, pl.ds(half * W, W), :]
-        ref[at + (pl.ds(TOP, W), slice(None))] = jnp.where(sub_lo, low, 0.0)
-        ref[at + (pl.ds(TOP + W + y_dev, W), slice(None))] = jnp.where(sub_hi, high, 0.0)
+            ref[at + (pl.ds(TOP + W, y_dev), slice(None))] = scaled(s[sat], scale)
+        low, tile = y_tile(ml_ref, kl_ref, c, i, s_dev)
+        high, _ = y_tile(mh_ref, kh_ref, c, i, s_dev)
+        low = low[tile, pl.ds(half * W, W), :]
+        high = high[tile, pl.ds(half * W, W), :]
+        ref[at + (pl.ds(TOP, W), slice(None))] = scaled(jnp.where(sub_lo, low, 0.0), scale)
+        ref[at + (pl.ds(TOP + W + y_dev, W), slice(None))] = scaled(jnp.where(sub_hi, high, 0.0), scale)
         ref[at + (pl.ds(0, TOP), slice(None))] = jnp.zeros((TOP, lanes), F32)
         ref[at + (pl.ds(TOP + y_ext, 8), slice(None))] = jnp.zeros((8, lanes), F32)
 
@@ -285,8 +317,8 @@
     for i in range(s_ext):
         for c in range(3):
             place(es, (c, i), c, i, 0, c)
-            place(hs, (c, i), c + 3, i, 1, c)
-        place(ce, (i,), 6, i, 0, 3)
+            place(hs, (c, i), c + 3, i, 1, c, 1.0 / time_step)
+        place(ce, (i,), 6, i, i % 2, 3)
 
     def coefs(i, carry):
         keep, gain = coefficients(ce[i, pl.ds(TOP, y_ext), :], in_y * slab_inside(i))
@@ -306,11 +338,12 @@
             for j in range(8):
                 i = b * 8 + j
                 for which in range(2):
-                    if c == 3 and which == 1:
+                    if c == 3 and which != i % 2:
                         continue
                     at = pl.ds((c * 8 + j) * W, W)
-                    mine = own_ref[2 * b + which, at, :]
-                    theirs = other_ref[2 * b + which, at, :]
+                    scale = 1.0 / time_step if which and c < 3 else 1.0
+                    mine = scaled(own_ref[2 * b + which, at, :], scale)
+                    theirs = scaled(other_ref[2 * b + which, at, :], scale)
                     target = (sdh if which else sde).at[c, i] if c < 3 else sce.at[i]
                     target[pl.ds(0, W), :] = jnp.where(first, mine, theirs)
                     target[pl.ds(W, W), :] = jnp.where(first, theirs, mine)
@@ -340,31 +373,32 @@
 
     def side_h(step, i):
         e0, e1, e2 = sde[0, i], sde[1, i], sde[2, i]
-        bt[pl.ds(i * 16 + 2 * step, 1), :] = e0[W : W + 1] * e_on
-        bt[pl.ds(i * 16 + 2 * step + 1, 1), :] = e1[W : W + 1] * e_on
-        scale = (time_step * slab_inside(i)) * in_y8
-        h0 = sdh[0, i] - scale * ((up_y(e2) - e2) - (up_x(e1) - e1))
-        h1 = sdh[1, i] - scale * ((up_x(e0) - e0) - (sde[2, i + 1] - e2))
-        h2 = sdh[2, i] - scale * ((sde[1, i + 1] - e1) - (up_y(e0) - e0))
+        at = i * 16 + 2 * step
+        bt[pl.ds(at, 1), :] = e0[W : W + 1] * e_on
+        bt[pl.ds(at + 1, 1), :] = e1[W : W + 1] * e_on
+        inside = in_y8 if i >= W else in_y8 * slab_inside(i)
+        h0 = (sdh[0, i] - ((up_y(e2) - e2) - (up_x(e1) - e1))) * inside
+        h1 = (sdh[1, i] - ((up_x(e0) - e0) - (sde[2, i + 1] - e2))) * inside
+        h2 = (sdh[2, i] - ((sde[1, i + 1] - e1) - (up_y(e0) - e0))) * inside
         sdh[0, i], sdh[1, i], sdh[2, i] = h0, h1, h2
-        bt[pl.ds(i * 16 + 8 + 2 * step, 1), :] = h0[W - 1 : W] * h_on
-        bt[pl.ds(i * 16 + 8 + 2 * step + 1, 1), :] = h1[W - 1 : W] * h_on
-        return h0, h1, h2
-
-    def side_e(i, h0, h1, h2):
+        bt[pl.ds(at + 8, 1), :] = h0[W - 1 : W] * h_on
+        bt[pl.ds(at + 9, 1), :] = h1[W - 1 : W] * h_on
+
+    def side_e(i):
+        h0, h1, h2 = sdh[0, i], sdh[1, i], sdh[2, i]
         keep, gain = sce[i], sch[i]
         sde[0, i] = keep * sde[0, i] + gain * ((h2 - down_y(h2)) - (h1 - down_x(h1)))
         sde[1, i] = keep * sde[1, i] + gain * ((h0 - down_x(h0)) - (h2 - sdh[2, i - 1]))
         sde[2, i] = keep * sde[2, i] + gain * ((h1 - sdh[1, i - 1]) - (h0 - down_y(h0)))
 
-    for step in range(STEPS):
-        side_h(step, step)
-
-        def side_row(i, carry, step=step):
-            side_e(i, *side_h(step, i))
-            return carry
-
-        lax.fori_loop(step + 1, s_ext - 1 - step, side_row, 0)
+    def side_step(step, carry):
+        for i in range(s_ext - 1):
+            side_h(step, i)
+        for i in range(1, s_ext - 1):
+            side_e(i)
+        return carry
+
+    lax.fori_loop(0, STEPS, side_step, 0)
 
     for b in range(blocks):
         bp[b] = bt[pl.ds(b * lanes, lanes), :].T[:y_ext]
@@ -374,20 +408,23 @@
     below = pl.ds(TOP - 1, y_ext)
 
     def border(i, q, to):
-        block, place = i // 8, i % 8
-        return pltpu.roll(bp[block], lax.rem(2 * lanes + to - place * 16 - q, lanes), 1)
+        shift = lax.rem(2 * lanes + to - (i % 8) * 16 - q, lanes)
+        return pltpu.roll(bp[i // 8], shift, 1)
+
+    def put_h(c, i, curl):
+        value = hs[c, i, centre, :] - curl
+        if i < W:
+            value = value * slab_inside(i)
+        hs[c, i, pl.ds(TOP, 8), :] = value[:8] * in_y[:8]
+        hs[c, i, pl.ds(TOP + 8, y_ext - 8), :] = value[8:]
 
     def main_h(step, i):
         e0, e1, e2 = es[0, i, centre, :], es[1, i, centre, :], es[2, i, centre, :]
         e0x = jnp.where(is_last, border(i, 2 * step, lanes - 1), pltpu.roll(e0, lanes - 1, 1))
         e1x = jnp.where(is_last, border(i, 2 * step + 1, lanes - 1), pltpu.roll(e1, lanes - 1, 1))
-        scale = (time_step * slab_inside(i)) * in_y
-        h0 = hs[0, i, centre, :] - scale * ((es[2, i, above, :] - e2) - (e1x - e1))
-        h1 = hs[1, i, centre, :] - scale * ((e0x - e0) - (es[2, i + 1, centre, :] - e2))
-        h2 = hs[2, i, centre, :] - scale * ((es[1, i + 1, centre, :] - e1) - (es[0, i, above, :] - e0))
-        hs[0, i, centre, :] = h0
-        hs[1, i, centre, :] = h1
-        hs[2, i, centre, :] = h2
+        put_h(0, i, (es[2, i, above, :] - e2) - (e1x - e1))
+        put_h(1, i, (e0x - e0) - (es[2, i + 1, centre, :] - e2))
+        put_h(2, i, (es[1, i + 1, centre, :] - e1) - (es[0, i, above, :] - e0))
 
     def main_e(step, i):
         h0, h1, h2 = hs[0, i, centre, :], hs[1, i, centre, :], hs[2, i, centre, :]
@@ -401,29 +438,27 @@
         es[0, i, centre, :] = n0
         es[1, i, centre, :] = n1
         es[2, i, centre, :] = n2
-        s0, s1, s2 = e0 + n0, e1 + n1, e2 + n2
-        total = s0 * s0 + s1 * s1 + s2 * s2
-        if step == 0:
-            heat[i] = total
-        else:
-            heat[i] = heat[i] + total
-
-    for step in range(STEPS):
-        main_h(step, step)
-
-        def main_row(i, carry, step=step):
+        if W <= i < W + s_dev:
+            s0, s1, s2 = e0 + n0, e1 + n1, e2 + n2
+            heat[i - W] = heat[i - W] + (s0 * s0 + s1 * s1 + s2 * s2)
+
+    heat[...] = jnp.zeros_like(heat)
+
+    def main_step(step, carry):
+        for i in range(s_ext - 1):
             main_h(step, i)
+        for i in range(1, s_ext - 1):
             main_e(step, i)
-            return carry
-
-        lax.fori_loop(step + 1, s_ext - 1 - step, main_row, 0)
+        return carry
+
+    lax.fori_loop(0, STEPS, main_step, 0)
 
     ys = pl.ds(TOP + W, y_dev)
     for c in range(3):
         e_out[c] = es[c, pl.ds(W, s_dev), ys, :]
-        h_out[c] = hs[c, pl.ds(W, s_dev), ys, :]
-
-    loss = heat[pl.ds(W, s_dev), pl.ds(W, y_dev), :] * c_ref[...] * (0.25 * time_step * heating)
+        h_out[c] = hs[c, pl.ds(W, s_dev), ys, :] * time_step
+
+    loss = heat[:, pl.ds(W, y_dev), :] * c_ref[...] * (0.25 * time_step * heating)
     parts = split_two(loss.reshape(s_dev * y_dev, lanes))
     thermal = t_ref.shape[0] * t_ref.shape[1]
     ids = ids_ref[...]
@@ -442,8 +477,9 @@
         x = t_ref[i]
         before = t_ref[i - 1] if i > 0 else lo_ref[lo_plane, pl.ds(0, ty), :]
         after = t_ref[i + 1] if i < ts - 1 else hi_ref[hi_plane, pl.ds(0, ty), :]
-        edge_lo = jnp.where(sub_lo, ml_ref[3, i, pl.ds(W, 1), :], 0.0)
-        edge_hi = jnp.where(sub_hi, mh_ref[3, i, pl.ds(W, 1), :], 0.0)
+        tile = 3 * s_dev + s_dev // 2 + i // 8
+        edge_lo = jnp.where(sub_lo, ml_ref[tile, pl.ds(i % 8, 1), :], 0.0)
+        edge_hi = jnp.where(sub_hi, mh_ref[tile, pl.ds(i % 8, 1), :], 0.0)
         left_y = jnp.where(row_t == 0, edge_lo, pltpu.roll(x, 1, 0))
         right_y = jnp.where(row_t == ty - 1, edge_hi, pltpu.roll(x, ty - 1, 0))
         beyond = other_ref[2 * blocks + i // per, pl.ds((i % per) * ty, ty), :]
@@ -455,7 +491,7 @@
         d_out[1, i] = d_out[1, i] - conduction * (6.0 * x - beside)
 
 
-def main_call(electric, magnetic, conduct, temp_old, ids, lo, hi, m_lo, m_hi, own, other):
+def main_call(electric, magnetic, conduct, temp_old, ids, *halos):
     s_dev, y_dev, lanes = conduct.shape
     s_ext, y_ext = s_dev + 2 * W, y_dev + 2 * W
     tall = TOP + y_ext + 8
@@ -471,7 +507,7 @@
             pltpu.VMEM((3, s_ext, tall, lanes), F32),
             pltpu.VMEM((s_ext, tall, lanes), F32),
             pltpu.VMEM((s_ext, y_ext, lanes), F32),
-            pltpu.VMEM((s_ext, y_ext, lanes), F32),
+            pltpu.VMEM((s_dev, y_ext, lanes), F32),
             pltpu.VMEM((3, s_ext, 8, lanes), F32),
             pltpu.VMEM((3, s_ext, 8, lanes), F32),
             pltpu.VMEM((s_ext, 8, lanes), F32),
@@ -481,7 +517,7 @@
         ],
         compiler_params=pltpu.CompilerParams(vmem_limit_bytes=VMEM_LIMIT),
         name="leapfrog",
-    )(electric, magnetic, conduct, temp_old, ids, lo, hi, m_lo, m_hi, own, other)
+    )(electric, magnetic, conduct, temp_old, ids, *halos)
 
 
 R = SWEEPS - 1
@@ -510,8 +546,9 @@
         r0[half, :, pl.ds(TTOP + shift - R, ty + 2 * R), :] = z[...]
     for i in range(ts):
         cs[0, i + 1, pl.ds(TTOP + shift, ty), :] = cap_ref[i]
-        cs[0, i + 1, pl.ds(TTOP + shift - 1, 1), :] = ml_ref[3, i, pl.ds(W + 1, 1), :]
-        cs[0, i + 1, pl.ds(TTOP + shift + ty, 1), :] = mh_ref[3, i, pl.ds(W + 1, 1), :]
+        tile = ml_ref.shape[0] - ts // 8 + i // 8
+        cs[0, i + 1, pl.ds(TTOP + shift - 1, 1), :] = ml_ref[tile, pl.ds(i % 8, 1), :]
+        cs[0, i + 1, pl.ds(TTOP + shift + ty, 1), :] = mh_ref[tile, pl.ds(i % 8, 1), :]
         cs[1, i + 1, pl.ds(TTOP + shift, ty), :] = other_ref[caps + i // per, pl.ds((i % per) * ty, ty), :]
     cs[0, 0, pl.ds(TTOP + shift, ty), :] = lo_ref[lo_ref.shape[0] - 1, pl.ds(ty, ty), :]
     cs[0, ts + 1, pl.ds(TTOP + shift, ty), :] = hi_ref[hi_ref.shape[0] - 1, pl.ds(ty, ty), :]
@@ -564,7 +601,7 @@
         functools.partial(thermal_kernel, lax.axis_size("slab"), lax.axis_size("sub")),
         out_shape=jax.ShapeDtypeStruct(temp_old.shape, F32),
         scratch_shapes=[wide, wide, wide, pltpu.VMEM((2, ts + 2, TTOP + 24 + 8, lanes), F32)],
-        compiler_params=pltpu.CompilerParams(vmem_limit_bytes=VMEM_LIMIT),
+        compiler_params=pltpu.CompilerParams(vmem_limit_bytes=SMALL_LIMIT),
         name="conduction",
     )(z, z_other, temp_old, capacity, lo, hi, m_lo, m_hi, other)
 
@@ -593,7 +630,7 @@
     return pl.pallas_call(
         lookup_kernel,
         out_shape=jax.ShapeDtypeStruct(conduct.shape, F32),
-        compiler_params=pltpu.CompilerParams(vmem_limit_bytes=VMEM_LIMIT),
+        compiler_params=pltpu.CompilerParams(vmem_limit_bytes=SMALL_LIMIT),
         name="lookup",
     )(ids, temp_new, lo, hi, conduct)
 
@@ -620,13 +657,12 @@
     ids_row = ids.reshape(1, -1)
     ids_square = ids.reshape(-1, lanes)
 
-    up, dn = slab_messages(electric, magnetic, conduct, temp_old, capacity)
-    lo, hi = passed_along(up, "slab", 1), passed_along(dn, "slab", -1)
-    m_lo, m_hi = sub_exchange(electric, magnetic, conduct, temp_old, capacity, lo, hi)
-    own = comp_pack(electric, magnetic, conduct, temp_old, capacity, lo, hi, m_lo, m_hi)
+    halos = halo_exchange(electric, magnetic, conduct, temp_old, capacity)
+    lo, hi, m_lo, m_hi = halos[:4]
+    own = comp_pack(electric, magnetic, conduct, temp_old, capacity, *halos)
     other = swapped(own, "comp")
     electric, magnetic, sums = main_call(
-        electric, magnetic, conduct, temp_old, ids_row, lo, hi, m_lo, m_hi, own, other
+        electric, magnetic, conduct, temp_old, ids_row, *halos, own, other
     )
     r0 = sums[1] + passed_along(sums[2], "slab", 1) + passed_along(sums[0], "slab", -1)
     y_lo, y_hi = sub_edges(r0, R)

time: 157 us -> 94.5 us (0.60)
  Pallas kernels: 69.7 us -> 21.6 us
  waiting for transfers between devices: 42.4 us -> 30.3 us
  local copies, waits for them, and re-layouts: 16.6 us -> 11.1 us
  other arithmetic: 1.7 us -> 3.58 us
  starting transfers between devices: 24.7 us -> 26.5 us
    pallas_call x1, Pallas kernels: 54.3 us -> 14.3 us  [main_call(): pl.pallas_call(functools.partial(main_kernel, lax.axis_size('slab'), lax....]
    ppermute x4 -> x5, waiting for transfers between devices: 18.5 us -> 7.06 us  [swapped(): return lax.ppermute(array, axis, [(0, 1), (1, 0)])]
    unnamed x30 -> x32, local copies, waits for them, and re-layouts: 13 us -> 9.64 us
    pallas_call x1 -> x2, Pallas kernels: 3.35 us -> 0.22 us  [the longest x1 0.19 us: halo_exchange(): pl.pallas_call(functools.partial(pack_kernel, edges), out_shape=[jax.Shap...]
    pallas_call x1, Pallas kernels: 5.55 us -> 2.87 us  [comp_pack(): pl.pallas_call(functools.partial(comp_pack_kernel, lax.axis_size('sub')),...]
    add x1, other arithmetic: 0.7 us -> 2.59 us  [on_device(): ids = (offsets + 1) * thermal + targets]
    ppermute x4 -> x5, starting transfers between devices: 3.1 us -> 4.72 us  [swapped(): return lax.ppermute(array, axis, [(0, 1), (1, 0)])]
  transfers between devices with their start and end apart: 12 -> 13, of which waited for: 11 -> 10; matrix products, arithmetic and copies ran while one was open for 2% -> 4% of each run, Pallas kernels for 0% -> 0%
where the time goes in v1:
time: 94.5 us; the launch traced here: 93.8 us
  waiting for transfers between devices  30.3 us (32%)
  starting transfers between devices  26.5 us (28%)
  Pallas kernels  21.6 us (23%)
  local copies, waits for them, and re-layouts  11.1 us (12%)
  other arithmetic  3.58 us (4%)
    ppermute x8, waiting for transfers between devices, passed_along(): return lax.ppermute(array, axis, pairs)  23.2 us
    ppermute x8, starting transfers between devices, passed_along(): return lax.ppermute(array, axis, pairs)  21.7 us
    pallas_call x1, Pallas kernels, main_call(): pl.pallas_call(functools.partial(main_kernel, lax.axis_size('slab'), lax....  14.3 us
    unnamed x32, local copies, waits for them, and re-layouts  9.64 us
    ppermute x5, waiting for transfers between devices, swapped(): return lax.ppermute(array, axis, [(0, 1), (1, 0)])  7.06 us
    ppermute x5, starting transfers between devices, swapped(): return lax.ppermute(array, axis, [(0, 1), (1, 0)])  4.72 us
    pallas_call x1, Pallas kernels, comp_pack(): pl.pallas_call(functools.partial(comp_pack_kernel, lax.axis_size('sub')),...  2.87 us
    pallas_call x1, Pallas kernels, thermal_call(): pl.pallas_call(functools.partial(thermal_kernel, lax.axis_size('slab'), l...  2.69 us
  transfers between devices with their start and end apart: 13, of which 10 were waited for; matrix products, arithmetic and copies ran while one was open for 4% of the time, Pallas kernels for 0%

profile of v1, /device:TPU:0, one launch (start us, length us, event | category | flops | bytes accessed | tf_op | source)
XLA Modules:
  0.0 93.8 jit_solution(2912234719208114997)
XLA Ops:
  0.6 1.4 %copy-done = f32[3,32,32,128]{3,2,1,0:T(8,128)S(1)} copy-done((f32[3,32,32,128]{3,2,1,0:T(8,128)S(1)}, f32[3,32,32,128]{3,2,1,0:T(8,128)}, u32[]{:S(2)}) %copy-start) | copy-done | bytes 1572888
  2.0 1.4 %copy-done.2 = f32[3,32,32,128]{3,2,1,0:T(8,128)S(1)} copy-done((f32[3,32,32,128]{3,2,1,0:T(8,128)S(1)}, f32[3,32,32,128]{3,2,1,0:T(8,128)}, u32[]{:S(2)}) %copy-start.2) | copy-done | bytes 1572888
  3.4 1.0 %copy-done.4 = f32[32,32,128]{2,1,0:T(8,128)S(1)} copy-done((f32[32,32,128]{2,1,0:T(8,128)S(1)}, f32[32,32,128]{2,1,0:T(8,128)}, u32[]{:S(2)}) %copy-start.4) | copy-done | bytes 524312
  4.5 0.9 copy-done.6
  5.4 0.9 copy-done.10
  6.3 0.2 pack.1
  6.5 5.1 %collective-permute-start = (f32[27,32,128]{2,1,0:T(8,128)S(1)}, f32[27,32,128]{2,1,0:T(8,128)S(1)}, u32[]{:S(2)}, u32[]{:S(2)}) collective-permute-start(f32[27,32,128]{2,1,0:T(8,128)S(1)} %get-tuple-element.10), channel_id=1, source_target_pairs={{0,4},{4,8},{8,12},{1,5},{5,9},{9,13},{2,6},{6,10},{10,14},{3,7},{... | collective-permute-start | bytes 1327112 | tf_op jit(solution)/shard_map/ppermute | solution.py:40
  11.6 1.3 %collective-permute-start.1 = (f32[24,32,128]{2,1,0:T(8,128)S(1)}, f32[24,32,128]{2,1,0:T(8,128)S(1)}, u32[]{:S(2)}, u32[]{:S(2)}) collective-permute-start(f32[24,32,128]{2,1,0:T(8,128)S(1)} %get-tuple-element.11), channel_id=1, source_target_pairs={{4,0},{8,4},{12,8},{5,1},{9,5},{13,9},{6,2},{10,6},{14,10},{7,3},{... | collective-permute-start | bytes 1179656 | tf_op jit(solution)/shard_map/ppermute | solution.py:40
  12.9 1.5 %collective-permute-start.2 = (f32[116,8,128]{2,1,0:T(8,128)S(1)}, f32[116,8,128]{2,1,0:T(8,128)S(1)}, u32[]{:S(2)}, u32[]{:S(2)}) collective-permute-start(f32[116,8,128]{2,1,0:T(8,128)S(1)} %get-tuple-element.12), channel_id=1, source_target_pairs={{0,2},{2,0},{1,3},{3,1},{4,6},{6,4},{5,7},{7,5},{8,10},{10,8},{9,1... | collective-permute-start | bytes 1425416 | tf_op jit(solution)/shard_map/ppermute | solution.py:44
  14.4 9.6 %collective-permute-done.1.hi_ref = f32[24,32,128]{2,1,0:T(8,128)S(1)} collective-permute-done((f32[24,32,128]{2,1,0:T(8,128)S(1)}, f32[24,32,128]{2,1,0:T(8,128)S(1)}, u32[]{:S(2)}, u32[]{:S(2)}) %collective-permute-start.1) | collective-permute-done | bytes 393248 | tf_op jit(solution)/shard_map/ppermute | solution.py:40
  24.1 0.0 collective-permute-done.lo_ref
  24.1 0.0 copy-start.15
  24.1 0.0 copy-start.5
  24.1 0.0 copy-start.7
  24.1 1.5 %collective-permute-start.3 = (f32[28,8,128]{2,1,0:T(8,128)S(1)}, f32[28,8,128]{2,1,0:T(8,128)S(1)}, u32[]{:S(2)}, u32[]{:S(2)}) collective-permute-start(f32[28,8,128]{2,1,0:T(8,128)S(1)} %corners.1), channel_id=1, source_target_pairs={{0,2},{2,0},{1,3},{3,1},{4,6},{6,4},{5,7},{7,5},{8,10},{10,8},{9,1... | collective-permute-start | bytes 344072 | tf_op jit(solution)/shard_map/ppermute | solution.py:44
  25.7 0.0 collective-permute-done.2.ml_ref.mh_ref
  25.7 3.3 %collective-permute-done.3.kl_ref.kh_ref = f32[28,8,128]{2,1,0:T(8,128)S(1)} collective-permute-done((f32[28,8,128]{2,1,0:T(8,128)S(1)}, f32[28,8,128]{2,1,0:T(8,128)S(1)}, u32[]{:S(2)}, u32[]{:S(2)}) %collective-permute-start.3) | collective-permute-done | bytes 114720 | tf_op jit(solution)/shard_map/ppermute | solution.py:44
  29.0 2.9 %comp_pack.1.own_ref = f32[14,128,128]{2,1,0:T(8,128)} custom-call(f32[3,32,32,128]{3,2,1,0:T(8,128)S(1)} %copy-done.1, f32[3,32,32,128]{3,2,1,0:T(8,128)S(1)} %copy-done.2, f32[32,32,128]{2,1,0:T(8,128)S(1)} %copy-done.4, f32[16,16,128]{2,1,0:T(8,128)S(1)} %copy-done.6, f32[16,16,128]{2,1,0:T(8,128)S(1)} %copy-done.10, ...), custom_call_target="tpu_custom_call" | custom-call | tf_op jit(solution)/shard_map/comp_pack/pallas_call | solution.py:247
  31.9 0.5 broadcast.5
  32.4 2.6 %fusion.1 = (s32[32,32]{1,0:T(8,128)}, s32[32,32,1]{1,2,0:T(1,128)}) fusion(s32[]{:T(128)} %broadcast.5, s32[32,32,1]{1,2,0:T(1,128)S(1)} %copy-done.15, s32[32,32,1]{1,2,0:T(1,128)} %param.12), kind=kLoop, calls=%fused_computation.12 | loop fusion | flops 3072 | bytes 16388 | tf_op jit(solution)/shard_map/add | solution.py:656
  35.0 0.8 reshape.14.ids_ref
  35.8 0.0 collective-permute-done.4.other_ref
  35.8 0.0 copy-start.3
  35.8 1.4 %copy-done.3 = f32[3,32,32,128]{3,2,1,0:T(8,128)S(1)} copy-done((f32[3,32,32,128]{3,2,1,0:T(8,128)S(1)}, f32[3,32,32,128]{3,2,1,0:T(8,128)}, u32[]{:S(2)}) %copy-start.3) | copy-done | bytes 1572888
  37.2 0.9 copy-done.9
  38.1 14.3 %leapfrog.1 = (f32[3,32,32,128]{3,2,1,0:T(8,128)}, f32[3,32,32,128]{3,2,1,0:T(8,128)}, f32[3,16,16,128]{3,2,1,0:T(8,128)S(1)}) custom-call(f32[3,32,32,128]{3,2,1,0:T(8,128)S(1)} %copy-done.1, f32[3,32,32,128]{3,2,1,0:T(8,128)S(1)} %copy-done.3, f32[32,32,128]{2,1,0:T(8,128)S(1)} %copy-done.5, f32[16,16,128]{2,1,0:T(8,128)S(1)} %copy-done.7, ...), custom_call_target="tpu_custom_call" | custom-call | tf_op jit(solution)/shard_map/leapfrog/pallas_call | solution.py:498
  52.4 0.7 copy-done.13
  53.1 3.5 %collective-permute-start.5 = (f32[16,16,128]{2,1,0:T(8,128)S(1)}, f32[16,16,128]{2,1,0:T(8,128)S(1)}, u32[]{:S(2)}, u32[]{:S(2)}) collective-permute-start(f32[16,16,128]{2,1,0:T(8,128)S(1)} %get-tuple-element.18), channel_id=1, source_target_pairs={{0,4},{4,8},{8,12},{1,5},{5,9},{9,13},{2,6},{6,10},{10,14},{3,7},{... | collective-permute-start | bytes 393224 | tf_op jit(solution)/shard_map/ppermute | solution.py:40
  56.6 1.3 %collective-permute-start.6 = (f32[16,16,128]{2,1,0:T(8,128)S(1)}, f32[16,16,128]{2,1,0:T(8,128)S(1)}, u32[]{:S(2)}, u32[]{:S(2)}) collective-permute-start(f32[16,16,128]{2,1,0:T(8,128)S(1)} %get-tuple-element.19), channel_id=1, source_target_pairs={{4,0},{8,4},{12,8},{5,1},{9,5},{13,9},{6,2},{10,6},{14,10},{7,3},{... | collective-permute-start | bytes 393224 | tf_op jit(solution)/shard_map/ppermute | solution.py:40
  57.9 2.1 %collective-permute-done.5 = f32[16,16,128]{2,1,0:T(8,128)S(1)} collective-permute-done((f32[16,16,128]{2,1,0:T(8,128)S(1)}, f32[16,16,128]{2,1,0:T(8,128)S(1)}, u32[]{:S(2)}, u32[]{:S(2)}) %collective-permute-start.5) | collective-permute-done | bytes 131104 | tf_op jit(solution)/shard_map/ppermute | solution.py:40
  60.0 4.1 %collective-permute-done.6 = f32[16,16,128]{2,1,0:T(8,128)S(1)} collective-permute-done((f32[16,16,128]{2,1,0:T(8,128)S(1)}, f32[16,16,128]{2,1,0:T(8,128)S(1)}, u32[]{:S(2)}, u32[]{:S(2)}) %collective-permute-start.6) | collective-permute-done | bytes 131104 | tf_op jit(solution)/shard_map/ppermute | solution.py:40
  64.1 0.9 fusion
  65.1 1.6 %collective-permute-start.7 = (f32[16,2,128]{2,1,0:T(2,128)S(1)}, f32[16,2,128]{2,1,0:T(2,128)S(1)}, u32[]{:S(2)}, u32[]{:S(2)}) collective-permute-start(f32[16,2,128]{2,1,0:T(2,128)S(1)} %constant_dynamic-slice_fusion), channel_id=1, source_target_pairs={{0,2},{2,0},{1,3},{3,1},{4,6},{6,4},{5,7},{7,5},{8,10},{10,8},{9,1... | collective-permute-start | bytes 49160 | tf_op jit(solution)/shard_map/ppermute | solution.py:44
  66.6 2.3 %collective-permute-done.7 = f32[16,2,128]{2,1,0:T(2,128)S(1)} collective-permute-done((f32[16,2,128]{2,1,0:T(2,128)S(1)}, f32[16,2,128]{2,1,0:T(2,128)S(1)}, u32[]{:S(2)}, u32[]{:S(2)}) %collective-permute-start.7) | collective-permute-done | bytes 16416 | tf_op jit(solution)/shard_map/ppermute | solution.py:44
  68.9 3.5 %collective-permute-start.8 = (f32[2,20,128]{2,1,0:T(8,128)S(1)}, f32[2,20,128]{2,1,0:T(8,128)S(1)}, u32[]{:S(2)}, u32[]{:S(2)}) collective-permute-start(f32[2,20,128]{2,1,0:T(8,128)S(1)} %get-tuple-element.20), channel_id=1, source_target_pairs={{0,4},{4,8},{8,12},{1,5},{5,9},{9,13},{2,6},{6,10},{10,14},{3,7},{... | collective-permute-start | bytes 61448 | tf_op jit(solution)/shard_map/ppermute | solution.py:40
  72.4 1.3 %collective-permute-start.9 = (f32[2,20,128]{2,1,0:T(8,128)S(1)}, f32[2,20,128]{2,1,0:T(8,128)S(1)}, u32[]{:S(2)}, u32[]{:S(2)}) collective-permute-start(f32[2,20,128]{2,1,0:T(8,128)S(1)} %get-tuple-element.21), channel_id=1, source_target_pairs={{4,0},{8,4},{12,8},{5,1},{9,5},{13,9},{6,2},{10,6},{14,10},{7,3},{... | collective-permute-start | bytes 61448 | tf_op jit(solution)/shard_map/ppermute | solution.py:40
  73.7 0.2 collective-permute-done.8
  73.9 4.2 %collective-permute-done.9 = f32[2,20,128]{2,1,0:T(8,128)S(1)} collective-permute-done((f32[2,20,128]{2,1,0:T(8,128)S(1)}, f32[2,20,128]{2,1,0:T(8,128)S(1)}, u32[]{:S(2)}, u32[]{:S(2)}) %collective-permute-start.9) | collective-permute-done | bytes 20512 | tf_op jit(solution)/shard_map/ppermute | solution.py:40
  78.2 0.1 collective-permute-start.10
  78.3 1.5 %collective-permute-done.10.zo_ref = f32[20,20,128]{2,1,0:T(8,128)S(1)} collective-permute-done((f32[20,20,128]{2,1,0:T(8,128)S(1)}, f32[20,20,128]{2,1,0:T(8,128)S(1)}, u32[]{:S(2)}, u32[]{:S(2)}) %collective-permute-start.10) | collective-permute-done | bytes 204832 | tf_op jit(solution)/shard_map/ppermute | solution.py:44
  79.8 2.7 %conduction.1.t_ref = f32[16,16,128]{2,1,0:T(8,128)} custom-call(f32[20,20,128]{2,1,0:T(8,128)S(1)} %pad_maximum_fusion.z_ref, f32[20,20,128]{2,1,0:T(8,128)S(1)} %collective-permute-done.10.zo_ref, f32[16,16,128]{2,1,0:T(8,128)S(1)} %copy-done.7, f32[16,16,128]{2,1,0:T(8,128)S(1)} %copy-done.11, f32[27,32,128]{2,1,0:T(8,128)S(1)} %collective-permute-done.lo_ref, ...), custom_call_target="tpu_custom_call" | custom-call | tf_op jit(solution)/shard_map/conduction/pallas_call | solution.py:600
  82.4 1.3 %collective-permute-start.12 = (f32[16,16,128]{2,1,0:T(8,128)}, f32[16,16,128]{2,1,0:T(8,128)S(1)}, u32[]{:S(2)}, u32[]{:S(2)}) collective-permute-start(f32[16,16,128]{2,1,0:T(8,128)} %conduction.1.t_ref), channel_id=1, source_target_pairs={{4,0},{8,4},{12,8},{5,1},{9,5},{13,9},{6,2},{10,6},{14,10},{7,3},{... | collective-permute-start | bytes 393224 | tf_op jit(solution)/shard_map/ppermute | solution.py:40
  83.7 4.6 %collective-permute-start.11 = (f32[16,16,128]{2,1,0:T(8,128)}, f32[16,16,128]{2,1,0:T(8,128)S(1)}, u32[]{:S(2)}, u32[]{:S(2)}) collective-permute-start(f32[16,16,128]{2,1,0:T(8,128)} %conduction.1.t_ref), channel_id=1, source_target_pairs={{0,4},{4,8},{8,12},{1,5},{5,9},{9,13},{2,6},{6,10},{10,14},{3,7},{... | collective-permute-start | bytes 393224 | tf_op jit(solution)/shard_map/ppermute | solution.py:40
  88.3 0.1 reshape.15.ids_ref
  88.4 1.7 %collective-permute-done.12.hi_ref = f32[16,16,128]{2,1,0:T(8,128)S(1)} collective-permute-done((f32[16,16,128]{2,1,0:T(8,128)}, f32[16,16,128]{2,1,0:T(8,128)S(1)}, u32[]{:S(2)}, u32[]{:S(2)}) %collective-permute-start.12) | collective-permute-done | bytes 131104 | tf_op jit(solution)/shard_map/ppermute | solution.py:40
  90.1 1.3 %collective-permute-done.11.lo_ref = f32[16,16,128]{2,1,0:T(8,128)S(1)} collective-permute-done((f32[16,16,128]{2,1,0:T(8,128)}, f32[16,16,128]{2,1,0:T(8,128)S(1)}, u32[]{:S(2)}, u32[]{:S(2)}) %collective-permute-start.11) | collective-permute-done | bytes 131104 | tf_op jit(solution)/shard_map/ppermute | solution.py:40
  91.4 0.9 copy-done.12
  92.3 1.6 %lookup.1 = f32[32,32,128]{2,1,0:T(8,128)} custom-call(s32[8,128]{1,0:T(8,128)S(1)} %reshape.15.ids_ref, f32[16,16,128]{2,1,0:T(8,128)S(1)} %copy-done.12, f32[16,16,128]{2,1,0:T(8,128)S(1)} %collective-permute-done.11.lo_ref, f32[16,16,128]{2,1,0:T(8,128)S(1)} %collective-permute-done.12.hi_ref, f32[32,32,128]{2,1,0:T(8,128)S(1)} %copy-done.5), custom_call_target="tpu_custom_call" | custom-call | tf_op jit(solution)/shard_map/lookup/pallas_call | solution.py:630
  (26 shorter events, 0.2 us)
Async XLA Ops:
  0.6 1.4 %copy-start = (f32[3,32,32,128]{3,2,1,0:T(8,128)S(1)}, f32[3,32,32,128]{3,2,1,0:T(8,128)}, u32[]{:S(2)}) copy-start(f32[3,32,32,128]{3,2,1,0:T(8,128)} %e_ref.5) | copy-start | bytes 4718596
  2.0 1.4 %copy-start.2 = (f32[3,32,32,128]{3,2,1,0:T(8,128)S(1)}, f32[3,32,32,128]{3,2,1,0:T(8,128)}, u32[]{:S(2)}) copy-start(f32[3,32,32,128]{3,2,1,0:T(8,128)} %h_ref.5) | copy-start | bytes 4718596
  3.4 1.0 %copy-start.4 = (f32[32,32,128]{2,1,0:T(8,128)S(1)}, f32[32,32,128]{2,1,0:T(8,128)}, u32[]{:S(2)}) copy-start(f32[32,32,128]{2,1,0:T(8,128)} %c_ref.7) | copy-start | bytes 1572868
  4.5 0.9 copy-start.6
  5.4 0.9 copy-start.10
  6.3 22.7 %copy-start.1 = (f32[3,32,32,128]{3,2,1,0:T(8,128)S(1)}, f32[3,32,32,128]{3,2,1,0:T(8,128)}, u32[]{:S(2)}) copy-start(f32[3,32,32,128]{3,2,1,0:T(8,128)} %e_ref.5) | copy-start | bytes 4718596
  6.5 17.6 %collective-permute-start = (f32[27,32,128]{2,1,0:T(8,128)S(1)}, f32[27,32,128]{2,1,0:T(8,128)S(1)}, u32[]{:S(2)}, u32[]{:S(2)}) collective-permute-start(f32[27,32,128]{2,1,0:T(8,128)S(1)} %get-tuple-element.10), channel_id=1, source_target_pairs={{0,4},{4,8},{8,12},{1,5},{5,9},{9,13},{2,6},{6,10},{10,14},{3,7},{... | collective-permute-start | bytes 1327112 | tf_op jit(solution)/shard_map/ppermute | solution.py:40
  11.6 12.5 %collective-permute-start.1 = (f32[24,32,128]{2,1,0:T(8,128)S(1)}, f32[24,32,128]{2,1,0:T(8,128)S(1)}, u32[]{:S(2)}, u32[]{:S(2)}) collective-permute-start(f32[24,32,128]{2,1,0:T(8,128)S(1)} %get-tuple-element.11), channel_id=1, source_target_pairs={{4,0},{8,4},{12,8},{5,1},{9,5},{13,9},{6,2},{10,6},{14,10},{7,3},{... | collective-permute-start | bytes 1179656 | tf_op jit(solution)/shard_map/ppermute | solution.py:40
  12.9 12.8 %collective-permute-start.2 = (f32[116,8,128]{2,1,0:T(8,128)S(1)}, f32[116,8,128]{2,1,0:T(8,128)S(1)}, u32[]{:S(2)}, u32[]{:S(2)}) collective-permute-start(f32[116,8,128]{2,1,0:T(8,128)S(1)} %get-tuple-element.12), channel_id=1, source_target_pairs={{0,2},{2,0},{1,3},{3,1},{4,6},{6,4},{5,7},{7,5},{8,10},{10,8},{9,1... | collective-permute-start | bytes 1425416 | tf_op jit(solution)/shard_map/ppermute | solution.py:44
  24.1 8.3 %copy-start.15 = (s32[32,32,1]{1,2,0:T(1,128)S(1)}, s32[32,32,1]{1,2,0:T(1,128)}, u32[]{:S(2)}) copy-start(s32[32,32,1]{1,2,0:T(1,128)} %param.13) | copy-start | bytes 12292
  24.1 11.7 %copy-start.5 = (f32[32,32,128]{2,1,0:T(8,128)S(1)}, f32[32,32,128]{2,1,0:T(8,128)}, u32[]{:S(2)}) copy-start(f32[32,32,128]{2,1,0:T(8,128)} %c_ref.7) | copy-start | bytes 1572868
  24.1 11.7 %copy-start.7 = (f32[16,16,128]{2,1,0:T(8,128)S(1)}, f32[16,16,128]{2,1,0:T(8,128)}, u32[]{:S(2)}) copy-start(f32[16,16,128]{2,1,0:T(8,128)} %t_ref.7) | copy-start | bytes 393220
  24.1 4.9 %collective-permute-start.3 = (f32[28,8,128]{2,1,0:T(8,128)S(1)}, f32[28,8,128]{2,1,0:T(8,128)S(1)}, u32[]{:S(2)}, u32[]{:S(2)}) collective-permute-start(f32[28,8,128]{2,1,0:T(8,128)S(1)} %corners.1), channel_id=1, source_target_pairs={{0,2},{2,0},{1,3},{3,1},{4,6},{6,4},{5,7},{7,5},{8,10},{10,8},{9,1... | collective-permute-start | bytes 344072 | tf_op jit(solution)/shard_map/ppermute | solution.py:44
  29.0 2.9 %copy-start.8 = (f32[28,8,128]{2,1,0:T(8,128)}, f32[28,8,128]{2,1,0:T(8,128)S(1)}, u32[]{:S(2)}) copy-start(f32[28,8,128]{2,1,0:T(8,128)S(1)} %collective-permute-done.3.kl_ref.kh_ref) | copy-start | bytes 344068
  31.9 3.9 %collective-permute-start.4 = (f32[14,128,128]{2,1,0:T(8,128)}, f32[14,128,128]{2,1,0:T(8,128)}, u32[]{:S(2)}, u32[]{:S(2)}) collective-permute-start(f32[14,128,128]{2,1,0:T(8,128)} %comp_pack.1.own_ref), channel_id=1, source_target_pairs={{0,1},{1,0},{2,3},{3,2},{4,5},{5,4},{6,7},{7,6},{8,9},{9,8},{10,11... | collective-permute-start | bytes 2752520 | tf_op jit(solution)/shard_map/ppermute | solution.py:44
  35.8 1.4 %copy-start.3 = (f32[3,32,32,128]{3,2,1,0:T(8,128)S(1)}, f32[3,32,32,128]{3,2,1,0:T(8,128)}, u32[]{:S(2)}) copy-start(f32[3,32,32,128]{3,2,1,0:T(8,128)} %h_ref.5) | copy-start | bytes 4718596
  37.2 0.9 copy-start.9
  52.4 0.7 copy-start.13
  52.4 27.4 %copy-start.11 = (f32[16,16,128]{2,1,0:T(8,128)S(1)}, f32[16,16,128]{2,1,0:T(8,128)}, u32[]{:S(2)}) copy-start(f32[16,16,128]{2,1,0:T(8,128)} %cap_ref.5) | copy-start | bytes 393220
  53.1 6.9 %collective-permute-start.5 = (f32[16,16,128]{2,1,0:T(8,128)S(1)}, f32[16,16,128]{2,1,0:T(8,128)S(1)}, u32[]{:S(2)}, u32[]{:S(2)}) collective-permute-start(f32[16,16,128]{2,1,0:T(8,128)S(1)} %get-tuple-element.18), channel_id=1, source_target_pairs={{0,4},{4,8},{8,12},{1,5},{5,9},{9,13},{2,6},{6,10},{10,14},{3,7},{... | collective-permute-start | bytes 393224 | tf_op jit(solution)/shard_map/ppermute | solution.py:40
  56.6 7.5 %collective-permute-start.6 = (f32[16,16,128]{2,1,0:T(8,128)S(1)}, f32[16,16,128]{2,1,0:T(8,128)S(1)}, u32[]{:S(2)}, u32[]{:S(2)}) collective-permute-start(f32[16,16,128]{2,1,0:T(8,128)S(1)} %get-tuple-element.19), channel_id=1, source_target_pairs={{4,0},{8,4},{12,8},{5,1},{9,5},{13,9},{6,2},{10,6},{14,10},{7,3},{... | collective-permute-start | bytes 393224 | tf_op jit(solution)/shard_map/ppermute | solution.py:40
  65.1 3.8 %collective-permute-start.7 = (f32[16,2,128]{2,1,0:T(2,128)S(1)}, f32[16,2,128]{2,1,0:T(2,128)S(1)}, u32[]{:S(2)}, u32[]{:S(2)}) collective-permute-start(f32[16,2,128]{2,1,0:T(2,128)S(1)} %constant_dynamic-slice_fusion), channel_id=1, source_target_pairs={{0,2},{2,0},{1,3},{3,1},{4,6},{6,4},{5,7},{7,5},{8,10},{10,8},{9,1... | collective-permute-start | bytes 49160 | tf_op jit(solution)/shard_map/ppermute | solution.py:44
  68.9 5.0 %collective-permute-start.8 = (f32[2,20,128]{2,1,0:T(8,128)S(1)}, f32[2,20,128]{2,1,0:T(8,128)S(1)}, u32[]{:S(2)}, u32[]{:S(2)}) collective-permute-start(f32[2,20,128]{2,1,0:T(8,128)S(1)} %get-tuple-element.20), channel_id=1, source_target_pairs={{0,4},{4,8},{8,12},{1,5},{5,9},{9,13},{2,6},{6,10},{10,14},{3,7},{... | collective-permute-start | bytes 61448 | tf_op jit(solution)/shard_map/ppermute | solution.py:40
  72.4 5.7 %collective-permute-start.9 = (f32[2,20,128]{2,1,0:T(8,128)S(1)}, f32[2,20,128]{2,1,0:T(8,128)S(1)}, u32[]{:S(2)}, u32[]{:S(2)}) collective-permute-start(f32[2,20,128]{2,1,0:T(8,128)S(1)} %get-tuple-element.21), channel_id=1, source_target_pairs={{4,0},{8,4},{12,8},{5,1},{9,5},{13,9},{6,2},{10,6},{14,10},{7,3},{... | collective-permute-start | bytes 61448 | tf_op jit(solution)/shard_map/ppermute | solution.py:40
  78.2 10.1 %copy-start.14 = (s32[32,32,1]{1,2,0:T(1,128)S(1)}, s32[32,32,1]{1,2,0:T(1,128)}, u32[]{:S(2)}) copy-start(s32[32,32,1]{1,2,0:T(1,128)} %get-tuple-element.17) | copy-start | bytes 12292
  78.2 1.6 %collective-permute-start.10 = (f32[20,20,128]{2,1,0:T(8,128)S(1)}, f32[20,20,128]{2,1,0:T(8,128)S(1)}, u32[]{:S(2)}, u32[]{:S(2)}) collective-permute-start(f32[20,20,128]{2,1,0:T(8,128)S(1)} %pad_maximum_fusion.z_ref), channel_id=1, source_target_pairs={{0,1},{1,0},{2,3},{3,2},{4,5},{5,4},{6,7},{7,6},{8,9},{9,8},{10,11... | collective-permute-start | bytes 614408 | tf_op jit(solution)/shard_map/ppermute | solution.py:44
  82.4 7.6 %collective-permute-start.12 = (f32[16,16,128]{2,1,0:T(8,128)}, f32[16,16,128]{2,1,0:T(8,128)S(1)}, u32[]{:S(2)}, u32[]{:S(2)}) collective-permute-start(f32[16,16,128]{2,1,0:T(8,128)} %conduction.1.t_ref), channel_id=1, source_target_pairs={{4,0},{8,4},{12,8},{5,1},{9,5},{13,9},{6,2},{10,6},{14,10},{7,3},{... | collective-permute-start | bytes 393224 | tf_op jit(solution)/shard_map/ppermute | solution.py:40
  83.7 7.6 %collective-permute-start.11 = (f32[16,16,128]{2,1,0:T(8,128)}, f32[16,16,128]{2,1,0:T(8,128)S(1)}, u32[]{:S(2)}, u32[]{:S(2)}) collective-permute-start(f32[16,16,128]{2,1,0:T(8,128)} %conduction.1.t_ref), channel_id=1, source_target_pairs={{0,4},{4,8},{8,12},{1,5},{5,9},{9,13},{2,6},{6,10},{10,14},{3,7},{... | collective-permute-start | bytes 393224 | tf_op jit(solution)/shard_map/ppermute | solution.py:40
  91.4 0.9 copy-start.12

commit v2 on v1

--- a/solution.py
+++ b/solution.py
@@ -18,8 +18,9 @@
 
 F32 = jnp.float32
 BF16 = jnp.bfloat16
-VMEM_LIMIT = 26 * 1024 * 1024
+VMEM_LIMIT = 20 * 1024 * 1024
 SMALL_LIMIT = 12 * 1024 * 1024
+PACK_LIMIT = 62 * 1024 * 1024
 
 
 def chebyshev_constants(sweep_count):
@@ -80,100 +81,144 @@
     )
 
 
-def edge_rows(edge, y_dev, ty):
-    if edge == "high":
-        return y_dev - W, ty - 1
-    if edge == "low":
-        return 0, 0
-    upper = lax.axis_index("sub") == 0
-    return jnp.where(upper, y_dev - W, 0), jnp.where(upper, ty - 1, 0)
-
-
-def pack_kernel(edges, e_ref, h_ref, c_ref, t_ref, cap_ref, up_ref, dn_ref, *out_refs):
+def pack_kernel(
+    edges, e_ref, h_ref, c_ref, t_ref, cap_ref, off_ref, tgt_ref, ids_ref, up_ref, dn_ref, *refs
+):
+    count = len(edges)
+    sides, ups, downs = refs[:count], refs[count : 2 * count], refs[2 * count : 3 * count]
+    es, hs, cs, ts_, caps, sems = refs[3 * count :]
     s_dev, y_dev = c_ref.shape[0], c_ref.shape[1]
     ts, ty = t_ref.shape[0], t_ref.shape[1]
+    copies = []
+
+    def copy(src, dst):
+        copies.append(pltpu.make_async_copy(src, dst, sems.at[len(copies)]))
+        copies[-1].start()
+
+    starts = []
+    for n, edge in enumerate(edges):
+        if edge == "high":
+            y8, t8, y0, t0 = y_dev - 8, ty - 8, 8 - W, 7
+        elif edge == "low":
+            y8, t8, y0, t0 = 0, 0, 0, 0
+        else:
+            upper = lax.axis_index("sub") == 0
+            y8 = pl.multiple_of(jnp.where(upper, y_dev - 8, 0), 8)
+            t8 = pl.multiple_of(jnp.where(upper, ty - 8, 0), 8)
+            y0, t0 = jnp.where(upper, 8 - W, 0), jnp.where(upper, 7, 0)
+        starts.append((y0, t0))
+        copy(e_ref.at[:, :, pl.ds(y8, 8), :], es.at[n])
+        copy(h_ref.at[:, :, pl.ds(y8, 8), :], hs.at[n])
+        copy(c_ref.at[:, pl.ds(y8, 8), :], cs.at[n])
+        copy(t_ref.at[:, pl.ds(t8, 8), :], ts_.at[n])
+        copy(cap_ref.at[:, pl.ds(t8, 8), :], caps.at[n])
+    edge_copies = len(copies)
     for out, planes, i in zip((up_ref, dn_ref), plane_list(s_dev), (ts - 1, 0)):
-        for n, (f, r) in enumerate(planes):
-            if f < 3:
-                out[n] = e_ref[f, r]
-            elif f < 6:
-                out[n] = h_ref[f - 3, r]
-            else:
-                out[n] = c_ref[r]
-        out[len(planes), pl.ds(0, ty), :] = t_ref[i]
-        out[len(planes), pl.ds(ty, ty), :] = cap_ref[i]
-    for edge, out in zip(edges, out_refs):
-        y0, t0 = edge_rows(edge, y_dev, ty)
+        at = 0
+        for f in range(7):
+            rows = [r for g, r in planes if g == f]
+            span = pl.ds(rows[0], len(rows))
+            src = e_ref.at[f, span] if f < 3 else h_ref.at[f - 3, span] if f < 6 else c_ref.at[span]
+            copy(src, out.at[pl.ds(at, len(rows))])
+            at += len(rows)
+        copy(t_ref.at[i], out.at[at, pl.ds(0, ty), :])
+        copy(cap_ref.at[i], out.at[at, pl.ds(ty, ty), :])
+    lanes = ids_ref.shape[1]
+    part = lax.broadcasted_iota(jnp.int32, (1, lanes), 1) // y_dev
+    for a in range(ids_ref.shape[0]):
+        row = jnp.zeros((1, lanes), jnp.int32)
+        for k in range(lanes // y_dev):
+            s = a * (lanes // y_dev) + k
+            kind = (off_ref[s] + 1) * (ts * ty) + tgt_ref[s]
+            kind = jnp.concatenate([kind] * (lanes // y_dev), 1)
+            row = jnp.where(part == k, kind, row)
+        ids_ref[pl.ds(a, 1), :] = row
+    for c in copies[:edge_copies]:
+        c.wait()
+    for n in range(count):
+        out = sides[n]
+        y0, t0 = starts[n]
         for c in range(3):
             for r in range(s_dev):
-                out[c * s_dev + r, pl.ds(0, W), :] = e_ref[c, r, pl.ds(y0, W), :]
-                out[c * s_dev + r, pl.ds(W, W), :] = h_ref[c, r, pl.ds(y0, W), :]
+                out[c * s_dev + r, pl.ds(0, W), :] = es[n, c, r, pl.ds(y0, W), :]
+                out[c * s_dev + r, pl.ds(W, W), :] = hs[n, c, r, pl.ds(y0, W), :]
         for r in range(s_dev):
-            out[3 * s_dev + r // 2, pl.ds((r % 2) * W, W), :] = c_ref[r, pl.ds(y0, W), :]
+            out[3 * s_dev + r // 2, pl.ds((r % 2) * W, W), :] = cs[n, r, pl.ds(y0, W), :]
         base = 3 * s_dev + s_dev // 2
         for i in range(ts):
-            out[base + i // 8, pl.ds(i % 8, 1), :] = t_ref[i, pl.ds(t0, 1), :]
-            out[base + (ts + i) // 8, pl.ds(i % 8, 1), :] = cap_ref[i, pl.ds(t0, 1), :]
-
-
-def corner_kernel(edges, s_dev, ty, lo_ref, hi_ref, *out_refs):
-    up_index, dn_index = indices_of(s_dev)
-    y_dev, lanes = lo_ref.shape[1], lo_ref.shape[2]
-    zero = jnp.zeros((W, lanes), F32)
-    for edge, out in zip(edges, out_refs):
-        y0, _ = edge_rows(edge, y_dev, ty)
-        for f in range(7):
-            for k in range(2 * W):
-                i = k if k < W else s_dev + k
-                source = row_source(f, i, s_dev, None, lo_ref, hi_ref, up_index, dn_index)
-                value = zero if source is None else source[0][source[1] + (pl.ds(y0, W), slice(None))]
-                if f < 6:
-                    out[(f % 3) * 2 * W + k, pl.ds((f // 3) * W, W), :] = value
-                else:
-                    out[6 * W + k // 2, pl.ds((k % 2) * W, W), :] = value
-
-
-def y_tile(m_ref, k_ref, c, i, s_dev):
+            out[base + i // 8, pl.ds(i % 8, 1), :] = ts_[n, i, pl.ds(t0, 1), :]
+            out[base + (ts + i) // 8, pl.ds(i % 8, 1), :] = caps[n, i, pl.ds(t0, 1), :]
+        for corner, r0 in ((ups[n], s_dev - W), (downs[n], 0)):
+            for c in range(3):
+                corner[pl.ds(c * W, W)] = out[pl.ds(c * s_dev + r0, W)]
+            corner[pl.ds(3 * W, W // 2)] = out[pl.ds(3 * s_dev + r0 // 2, W // 2)]
+    for c in copies[edge_copies:]:
+        c.wait()
+
+
+def y_tile(m_ref, k_refs, c, i, s_dev):
     r = i - W
     if 0 <= r < s_dev:
         return m_ref, (c * s_dev + r if c < 3 else 3 * s_dev + r // 2)
-    k = i if r < 0 else i - s_dev
-    return k_ref, (c * 2 * W + k if c < 3 else 6 * W + k // 2)
-
-
-def sub_pass(messages):
-    if len(messages) == 1:
-        received = swapped(messages[0], "sub")
-        return received, received
-    return passed_along(messages[0], "sub", 1), passed_along(messages[1], "sub", -1)
-
-
-def halo_exchange(electric, magnetic, conduct, temp_old, capacity):
+    k = i if r < 0 else r - s_dev
+    return k_refs[0 if r < 0 else 1], (c * W + k if c < 3 else 3 * W + k // 2)
+
+
+def along_both(array, by_slab, by_sub):
+    slabs, subs = lax.axis_size("slab"), lax.axis_size("sub")
+    pairs = []
+    for k in range(slabs):
+        for u in range(subs):
+            to_k, to_u = k + by_slab, (1 - u if by_sub is None else u + by_sub)
+            if 0 <= to_k < slabs and 0 <= to_u < subs:
+                pairs.append((k * subs + u, to_k * subs + to_u))
+    return lax.ppermute(array, ("slab", "sub"), pairs)
+
+
+def halo_exchange(electric, magnetic, conduct, temp_old, capacity, offsets, targets):
     s_dev, y_dev, lanes = conduct.shape
     ts, ty, _ = temp_old.shape
-    edges = ("either",) if lax.axis_size("sub") == 2 else ("high", "low")
+    two = lax.axis_size("sub") == 2
+    edges = ("either",) if two else ("high", "low")
+    count = len(edges)
     up, dn = plane_list(s_dev)
     tiles = 3 * s_dev + s_dev // 2 + 2 * ts // 8
-    up, dn, *messages = pl.pallas_call(
+    corner = jax.ShapeDtypeStruct((3 * W + W // 2, 8, lanes), F32)
+    ids, up, dn, *messages = pl.pallas_call(
         functools.partial(pack_kernel, edges),
+        in_specs=[pl.BlockSpec(memory_space=pltpu.HBM)] * 5
+        + [pl.BlockSpec(memory_space=pltpu.VMEM)] * 2,
         out_shape=[
+            jax.ShapeDtypeStruct((s_dev * y_dev // lanes, lanes), jnp.int32),
             jax.ShapeDtypeStruct((len(up) + 1, y_dev, lanes), F32),
             jax.ShapeDtypeStruct((len(dn) + 1, y_dev, lanes), F32),
         ]
-        + [jax.ShapeDtypeStruct((tiles, 8, lanes), F32)] * len(edges),
-        compiler_params=pltpu.CompilerParams(vmem_limit_bytes=SMALL_LIMIT),
+        + [jax.ShapeDtypeStruct((tiles, 8, lanes), F32)] * count
+        + [corner] * (2 * count),
+        scratch_shapes=[
+            pltpu.VMEM((count, 3, s_dev, 8, lanes), F32),
+            pltpu.VMEM((count, 3, s_dev, 8, lanes), F32),
+            pltpu.VMEM((count, s_dev, 8, lanes), F32),
+            pltpu.VMEM((count, ts, 8, lanes), F32),
+            pltpu.VMEM((count, ts, 8, lanes), F32),
+            pltpu.SemaphoreType.DMA((5 * count + 18,)),
+        ],
+        compiler_params=pltpu.CompilerParams(vmem_limit_bytes=PACK_LIMIT),
         name="pack",
-    )(electric, magnetic, conduct, temp_old, capacity)
-    m_lo, m_hi = sub_pass(messages)
+    )(
+        electric, magnetic, conduct, temp_old, capacity,
+        offsets.reshape(s_dev, 1, y_dev), targets.reshape(s_dev, 1, y_dev),
+    )
+    sides, ups, downs = messages[:count], messages[count : 2 * count], messages[2 * count :]
     lo, hi = passed_along(up, "slab", 1), passed_along(dn, "slab", -1)
-    corners = pl.pallas_call(
-        functools.partial(corner_kernel, edges, s_dev, ty),
-        out_shape=[jax.ShapeDtypeStruct((7 * W, 8, lanes), F32)] * len(edges),
-        compiler_params=pltpu.CompilerParams(vmem_limit_bytes=SMALL_LIMIT),
-        name="corners",
-    )(lo, hi)
-    k_lo, k_hi = sub_pass(corners)
-    return lo, hi, m_lo, m_hi, k_lo, k_hi
+    if two:
+        m = swapped(sides[0], "sub")
+        k = (along_both(ups[0], 1, None), along_both(downs[0], -1, None))
+        return ids, (lo, hi, m, m) + k + k
+    m_lo, m_hi = passed_along(sides[0], "sub", 1), passed_along(sides[1], "sub", -1)
+    k_lo = (along_both(ups[0], 1, 1), along_both(downs[0], -1, 1))
+    k_hi = (along_both(ups[1], 1, -1), along_both(downs[1], -1, -1))
+    return ids, (lo, hi, m_lo, m_hi) + k_lo + k_hi
 
 
 def inside_flags(axis, count):
@@ -181,76 +226,116 @@
     return (index > 0), (index < count - 1)
 
 
-def comp_pack_kernel(
-    n_sub, e_ref, h_ref, c_ref, t_ref, cap_ref, lo_ref, hi_ref, ml_ref, mh_ref, kl_ref, kh_ref,
-    out_ref, a_ref, b_ref,
+def column_shift(group, lanes):
+    first = jnp.where(lax.axis_index("comp") == 0, lanes - W, 0)
+    return lax.rem(group * W - first + 2 * lanes, lanes)
+
+
+def gather_columns(sources, which_rows, height, lanes, lane):
+    accs = [jnp.zeros((height, lanes), F32), jnp.zeros((height, lanes), F32)]
+    for c in range(4):
+        for j in range(8):
+            group = c * 8 + j
+            shift = column_shift(group, lanes)
+            here = jnp.concatenate([lane == group] * (height // 8), 0)
+            for which in range(2):
+                if c == 3 and which != which_rows(j) % 2:
+                    continue
+                value = sources(6 if c == 3 else c + 3 * which, j)
+                if value is not None:
+                    accs[which] = jnp.where(here, pltpu.roll(value, shift, 1), accs[which])
+    return accs
+
+
+def columns_kernel(e_ref, h_ref, c_ref, t_ref, cap_ref, out_ref, turn):
+    s_dev, y_dev, lanes = c_ref.shape
+    lane = lax.broadcasted_iota(jnp.int32, (8, lanes), 1) // W
+    turn[...] = jnp.zeros_like(turn)
+    for b in range(s_dev // 8):
+
+        def source(f, j, b=b):
+            r = b * 8 + j
+            return e_ref[f, r] if f < 3 else h_ref[f - 3, r] if f < 6 else c_ref[r]
+
+        accs = gather_columns(source, lambda j: j, y_dev, lanes, lane)
+        for which in range(2):
+            turn[pl.ds(W, y_dev), :] = accs[which]
+            out_ref[2 * b + which] = turn[...].T
+    base = s_dev // 4
+    rows = t_ref.shape[0] * t_ref.shape[1] // lanes
+    per = lanes // t_ref.shape[1]
+    for n in range(rows):
+        out_ref[base + n] = t_ref[pl.ds(n * per, per)].reshape(lanes, lanes)
+        out_ref[base + rows + n] = cap_ref[pl.ds(n * per, per)].reshape(lanes, lanes)
+
+
+def rims_kernel(
+    n_sub, s_dev, lo_ref, hi_ref, ml_ref, mh_ref, kl0_ref, kl1_ref, kh0_ref, kh1_ref, out_ref, turn
 ):
-    s_dev, y_dev, lanes = c_ref.shape
+    y_dev, lanes = lo_ref.shape[1], lo_ref.shape[2]
     y_ext = y_dev + 2 * W
     up_index, dn_index = indices_of(s_dev)
-    own = (e_ref, h_ref, c_ref)
     has_lo, has_hi = inside_flags("sub", n_sub)
-    first = jnp.where(lax.axis_index("comp") == 0, lanes - W, 0)
     lane = lax.broadcasted_iota(jnp.int32, (8, lanes), 1) // W
-    a_ref[...] = jnp.zeros_like(a_ref)
-    b_ref[...] = jnp.zeros_like(b_ref)
-    blocks = (s_dev + 2 * W) // 8
-    for b in range(blocks):
-        acc_a = jnp.zeros((y_dev, lanes), F32)
-        acc_b = jnp.zeros((y_dev, lanes), F32)
-        acc_lo = jnp.zeros((8, lanes), F32)
-        acc_hi = jnp.zeros((8, lanes), F32)
+
+    def beside(rows):
+        low = jnp.zeros((8, lanes), F32)
+        high = jnp.zeros((8, lanes), F32)
         for c in range(4):
             for j in range(8):
-                i = b * 8 + j
                 group = c * 8 + j
-                shift = lax.rem(group * W - first + 2 * lanes, lanes)
-                here = lane == group
-                here_own = jnp.concatenate([here] * (y_dev // 8), 0)
-                for which in range(2):
-                    if c == 3 and which != i % 2:
-                        continue
-                    f = 6 if c == 3 else c + 3 * which
-                    source = row_source(f, i, s_dev, own, lo_ref, hi_ref, up_index, dn_index)
-                    if source is None:
-                        continue
-                    ref, at = source
-                    moved = pltpu.roll(ref[at], shift, 1)
-                    if which == 0:
-                        acc_a = jnp.where(here_own, moved, acc_a)
-                    else:
-                        acc_b = jnp.where(here_own, moved, acc_b)
-                low, at = y_tile(ml_ref, kl_ref, c, i, s_dev)
-                high, _ = y_tile(mh_ref, kh_ref, c, i, s_dev)
-                acc_lo = jnp.where(here, pltpu.roll(low[at], shift, 1), acc_lo)
-                acc_hi = jnp.where(here, pltpu.roll(high[at], shift, 1), acc_hi)
-        acc_lo = jnp.where(has_lo, acc_lo, 0.0)
-        acc_hi = jnp.where(has_hi, acc_hi, 0.0)
-        a_ref[pl.ds(0, W), :] = acc_lo[:W]
-        a_ref[pl.ds(W, y_dev), :] = acc_a
-        a_ref[pl.ds(W + y_dev, W), :] = acc_hi[:W]
-        b_ref[pl.ds(0, W), :] = acc_lo[W:]
-        b_ref[pl.ds(W, y_dev), :] = acc_b
-        b_ref[pl.ds(W + y_dev, W), :] = acc_hi[W:]
-        out_ref[2 * b] = a_ref[...].T
-        out_ref[2 * b + 1] = b_ref[...].T
-    rows = t_ref.shape[0] * t_ref.shape[1] // lanes
-    for n in range(rows):
-        per = lanes // t_ref.shape[1]
-        out_ref[2 * blocks + n] = t_ref[pl.ds(n * per, per)].reshape(lanes, lanes)
-        out_ref[2 * blocks + rows + n] = cap_ref[pl.ds(n * per, per)].reshape(lanes, lanes)
-
-
-def comp_pack(electric, magnetic, conduct, temp_old, capacity, *halos):
-    s_dev, y_dev, lanes = conduct.shape
-    count = 2 * ((s_dev + 2 * W) // 8) + 2 * (temp_old.shape[0] * temp_old.shape[1] // lanes)
+                shift = column_shift(group, lanes)
+                a, tile = y_tile(ml_ref, (kl0_ref, kl1_ref), c, rows[j], s_dev)
+                b, _ = y_tile(mh_ref, (kh0_ref, kh1_ref), c, rows[j], s_dev)
+                low = jnp.where(lane == group, pltpu.roll(a[tile], shift, 1), low)
+                high = jnp.where(lane == group, pltpu.roll(b[tile], shift, 1), high)
+        return jnp.where(has_lo, low, 0.0), jnp.where(has_hi, high, 0.0)
+
+    turn[...] = jnp.zeros_like(turn)
+    for b in range(s_dev // 8):
+        low, high = beside([W + b * 8 + j for j in range(8)])
+        turn[pl.ds(16 * b, 8), :] = low
+        turn[pl.ds(16 * b + 8, 8), :] = high
+    out_ref[0] = turn[...].T
+
+    rows = [k if k < W else s_dev + k for k in range(2 * W)]
+
+    def source(f, j):
+        found = row_source(f, rows[j], s_dev, None, lo_ref, hi_ref, up_index, dn_index)
+        return None if found is None else found[0][found[1]]
+
+    accs = gather_columns(source, lambda j: j, y_dev, lanes, lane)
+    low, high = beside(rows)
+    turn[...] = jnp.zeros_like(turn)
+    for which in range(2):
+        turn[pl.ds(which * y_ext, W), :] = low[which * W : which * W + W]
+        turn[pl.ds(which * y_ext + W, y_dev), :] = accs[which]
+        turn[pl.ds(which * y_ext + W + y_dev, W), :] = high[which * W : which * W + W]
+    out_ref[1] = turn[...].T
+
+
+def own_columns(electric, magnetic, conduct, temp_old, capacity):
+    s_dev, _, lanes = conduct.shape
+    count = s_dev // 4 + 2 * (temp_old.shape[0] * temp_old.shape[1] // lanes)
     return pl.pallas_call(
-        functools.partial(comp_pack_kernel, lax.axis_size("sub")),
+        columns_kernel,
         out_shape=jax.ShapeDtypeStruct((count, lanes, lanes), F32),
-        scratch_shapes=[pltpu.VMEM((lanes, lanes), F32)] * 2,
+        scratch_shapes=[pltpu.VMEM((lanes, lanes), F32)],
         compiler_params=pltpu.CompilerParams(vmem_limit_bytes=SMALL_LIMIT),
-        name="comp_pack",
-    )(electric, magnetic, conduct, temp_old, capacity, *halos)
+        cost_estimate=pl.CostEstimate(flops=10**7, bytes_accessed=8 * 10**6, transcendentals=0),
+        name="columns",
+    )(electric, magnetic, conduct, temp_old, capacity)
+
+
+def rim_columns(s_dev, *halos):
+    lanes = halos[0].shape[2]
+    return pl.pallas_call(
+        functools.partial(rims_kernel, lax.axis_size("sub"), s_dev),
+        out_shape=jax.ShapeDtypeStruct((2, lanes, lanes), F32),
+        scratch_shapes=[pltpu.VMEM((lanes, lanes), F32)],
+        compiler_params=pltpu.CompilerParams(vmem_limit_bytes=SMALL_LIMIT),
+        name="rims",
+    )(*halos)
 
 
 TOP = 8
@@ -274,10 +359,10 @@
 
 def main_kernel(
     n_slab, n_sub,
-    e_ref, h_ref, c_ref, t_ref, ids_ref, lo_ref, hi_ref, ml_ref, mh_ref, kl_ref, kh_ref,
-    own_ref, other_ref,
+    e_ref, h_ref, c_ref, t_ref, ids_ref, lo_ref, hi_ref, ml_ref, mh_ref,
+    kl0_ref, kl1_ref, kh0_ref, kh1_ref, own_ref, other_ref, own_rim, other_rim,
     e_out, h_out, d_out,
-    es, hs, ce, ch, heat, sde, sdh, sce, sch, bt, bp,
+    e_done, h_done, out_sem, es, hs, ce, ch, heat, sde, sdh, sce, sch, bt, bp,
 ):
     s_dev, y_dev, lanes = c_ref.shape
     s_ext, y_ext = s_dev + 2 * W, y_dev + 2 * W
@@ -294,8 +379,8 @@
         else:
             s, sat = source
             ref[at + (pl.ds(TOP + W, y_dev), slice(None))] = scaled(s[sat], scale)
-        low, tile = y_tile(ml_ref, kl_ref, c, i, s_dev)
-        high, _ = y_tile(mh_ref, kh_ref, c, i, s_dev)
+        low, tile = y_tile(ml_ref, (kl0_ref, kl1_ref), c, i, s_dev)
+        high, _ = y_tile(mh_ref, (kh0_ref, kh1_ref), c, i, s_dev)
         low = low[tile, pl.ds(half * W, W), :]
         high = high[tile, pl.ds(half * W, W), :]
         ref[at + (pl.ds(TOP, W), slice(None))] = scaled(jnp.where(sub_lo, low, 0.0), scale)
@@ -333,20 +418,34 @@
     lane8 = lax.broadcasted_iota(jnp.int32, (8, lanes), 1)
     in_y8 = ((lane8 >= W) | sub_lo) & ((lane8 < W + y_dev) | sub_hi)
     in_y8 = jnp.where(in_y8, 1.0, 0.0)
-    for b in range(blocks):
-        for c in range(4):
-            for j in range(8):
-                i = b * 8 + j
-                for which in range(2):
-                    if c == 3 and which != i % 2:
+    lane_turn = lax.broadcasted_iota(jnp.int32, (lanes, lanes), 1)
+    for b in range(s_dev // 8 + 1):
+        for which in range(2):
+            halves = []
+            for cols, rim in ((own_ref, own_rim), (other_ref, other_rim)):
+                if b < s_dev // 8:
+                    at = 16 * b + W * which
+                    low = pltpu.roll(rim[0], (lanes - at) % lanes, 1)
+                    high = pltpu.roll(rim[0], (W + y_dev - at - 8) % lanes, 1)
+                    value = jnp.where(lane_turn < W, low, cols[2 * b + which])
+                    value = jnp.where(lane_turn >= W + y_dev, high, value)
+                else:
+                    value = pltpu.roll(rim[1], (lanes - which * y_ext) % lanes, 1)
+                halves.append(value)
+            low = jnp.where(first, halves[0], halves[1])
+            high = jnp.where(first, halves[1], halves[0])
+            for c in range(4):
+                for j in range(8):
+                    if c == 3 and which != j % 2:
                         continue
-                    at = pl.ds((c * 8 + j) * W, W)
+                    i = W + 8 * b + j
+                    if b == s_dev // 8:
+                        i = j if j < W else s_dev + j
+                    at = (c * 8 + j) * W
                     scale = 1.0 / time_step if which and c < 3 else 1.0
-                    mine = scaled(own_ref[2 * b + which, at, :], scale)
-                    theirs = scaled(other_ref[2 * b + which, at, :], scale)
                     target = (sdh if which else sde).at[c, i] if c < 3 else sce.at[i]
-                    target[pl.ds(0, W), :] = jnp.where(first, mine, theirs)
-                    target[pl.ds(W, W), :] = jnp.where(first, theirs, mine)
+                    target[pl.ds(0, W), :] = scaled(low[at : at + W], scale)
+                    target[pl.ds(W, W), :] = scaled(high[at : at + W], scale)
 
     def side_coefs(i, carry):
         sce[i], sch[i] = coefficients(sce[i], in_y8 * slab_inside(i))
@@ -454,17 +553,23 @@
     lax.fori_loop(0, STEPS, main_step, 0)
 
     ys = pl.ds(TOP + W, y_dev)
+    copies = []
     for c in range(3):
-        e_out[c] = es[c, pl.ds(W, s_dev), ys, :]
-        h_out[c] = hs[c, pl.ds(W, s_dev), ys, :] * time_step
+        e_done[c] = es[c, pl.ds(W, s_dev), ys, :]
+        copies.append(pltpu.make_async_copy(e_done.at[c], e_out.at[c], out_sem.at[2 * c]))
+        copies[-1].start()
+        h_done[c] = hs[c, pl.ds(W, s_dev), ys, :] * time_step
+        copies.append(pltpu.make_async_copy(h_done.at[c], h_out.at[c], out_sem.at[2 * c + 1]))
+        copies[-1].start()
 
     loss = heat[:, pl.ds(W, y_dev), :] * c_ref[...] * (0.25 * time_step * heating)
     parts = split_two(loss.reshape(s_dev * y_dev, lanes))
     thermal = t_ref.shape[0] * t_ref.shape[1]
     ids = ids_ref[...]
     for n in range(3):
-        kinds = lax.broadcasted_iota(jnp.int32, (thermal, s_dev * y_dev), 0) + n * thermal
-        chosen = jnp.where(kinds == ids, 1.0, 0.0).astype(BF16)
+        kinds = lax.broadcasted_iota(jnp.int32, (thermal, lanes), 0) + n * thermal
+        chosen = [jnp.where(kinds == ids[a : a + 1], 1.0, 0.0).astype(BF16) for a in range(ids.shape[0])]
+        chosen = jnp.concatenate(chosen, 1)
         sums = jnp.dot(chosen, parts, preferred_element_type=F32)
         d_out[n] = (sums[:, :lanes] + sums[:, lanes:]).reshape(t_ref.shape)
 
@@ -482,13 +587,15 @@
         edge_hi = jnp.where(sub_hi, mh_ref[tile, pl.ds(i % 8, 1), :], 0.0)
         left_y = jnp.where(row_t == 0, edge_lo, pltpu.roll(x, 1, 0))
         right_y = jnp.where(row_t == ty - 1, edge_hi, pltpu.roll(x, ty - 1, 0))
-        beyond = other_ref[2 * blocks + i // per, pl.ds((i % per) * ty, ty), :]
+        beyond = other_ref[s_dev // 4 + i // per, pl.ds((i % per) * ty, ty), :]
         from_low = pltpu.roll(beyond, 1, 1) * h_on
         from_high = pltpu.roll(beyond, lanes - 1, 1) * e_on
         left_x = jnp.where(lane_t == 0, from_low, pltpu.roll(x, 1, 1))
         right_x = jnp.where(lane_t == lanes - 1, from_high, pltpu.roll(x, lanes - 1, 1))
         beside = before + after + left_y + right_y + left_x + right_x
         d_out[1, i] = d_out[1, i] - conduction * (6.0 * x - beside)
+    for copy in copies:
+        copy.wait()
 
 
 def main_call(electric, magnetic, conduct, temp_old, ids, *halos):
@@ -502,7 +609,15 @@
             jax.ShapeDtypeStruct(magnetic.shape, F32),
             jax.ShapeDtypeStruct((3,) + temp_old.shape, F32),
         ],
+        out_specs=[
+            pl.BlockSpec(memory_space=pl.ANY),
+            pl.BlockSpec(memory_space=pl.ANY),
+            pl.BlockSpec(memory_space=pltpu.VMEM),
+        ],
         scratch_shapes=[
+            pltpu.VMEM(electric.shape, F32),
+            pltpu.VMEM(magnetic.shape, F32),
+            pltpu.SemaphoreType.DMA((6,)),
             pltpu.VMEM((3, s_ext, tall, lanes), F32),
             pltpu.VMEM((3, s_ext, tall, lanes), F32),
             pltpu.VMEM((s_ext, tall, lanes), F32),
@@ -651,30 +766,37 @@
 
 
 def on_device(electric, magnetic, conduct, temp_old, capacity, offsets, targets):
-    lanes = conduct.shape[2]
-    thermal = temp_old.shape[0] * temp_old.shape[1]
-    ids = (offsets + 1) * thermal + targets
-    ids_row = ids.reshape(1, -1)
-    ids_square = ids.reshape(-1, lanes)
-
-    halos = halo_exchange(electric, magnetic, conduct, temp_old, capacity)
+    ids, halos = halo_exchange(
+        electric, magnetic, conduct, temp_old, capacity, offsets, targets
+    )
     lo, hi, m_lo, m_hi = halos[:4]
-    own = comp_pack(electric, magnetic, conduct, temp_old, capacity, *halos)
+    fields = (electric, magnetic, conduct, temp_old, capacity)
+    *fields, ids = lax.optimization_barrier(fields + (ids,))
+    own = own_columns(*fields)
+    own, *halos = lax.optimization_barrier((own,) + halos)
     other = swapped(own, "comp")
+    own_rim = rim_columns(conduct.shape[0], *halos)
+    other_rim = swapped(own_rim, "comp")
     electric, magnetic, sums = main_call(
-        electric, magnetic, conduct, temp_old, ids_row, *halos, own, other
+        electric, magnetic, conduct, temp_old, ids, *halos, own, other, own_rim, other_rim
     )
-    r0 = sums[1] + passed_along(sums[2], "slab", 1) + passed_along(sums[0], "slab", -1)
+    below, here, above = sums[0], sums[1], sums[2]
+    from_low = passed_along(jnp.concatenate([here[-R:], above], 0), "slab", 1)
+    from_high = passed_along(jnp.concatenate([below, here[:R]], 0), "slab", -1)
+    far_low = passed_along(above[-R:], "slab", 2)
+    far_high = passed_along(below[:R], "slab", -2)
+    index = lax.axis_index("slab")
+    low_rows = jnp.where(index > 0, below[-R:] + from_low[:R] + far_low, 0.0)
+    high_rows = above[:R] + from_high[-R:] + far_high
+    high_rows = jnp.where(index < lax.axis_size("slab") - 1, high_rows, 0.0)
+    r0 = jnp.concatenate([low_rows, here + from_low[R:] + from_high[:-R], high_rows], 0)
     y_lo, y_hi = sub_edges(r0, R)
-    r_y = jnp.concatenate([y_lo, r0, y_hi], 1)
-    s_lo = passed_along(r_y[-R:], "slab", 1)
-    s_hi = passed_along(r_y[:R], "slab", -1)
-    z = jnp.concatenate([s_lo, r_y, s_hi], 0)
+    z = jnp.concatenate([y_lo, r0, y_hi], 1)
     z_other = swapped(z, "comp")
     temp_new = thermal_call(z, z_other, temp_old, capacity, lo, hi, m_lo, m_hi, other)
     t_lo = passed_along(temp_new, "slab", 1)
     t_hi = passed_along(temp_new, "slab", -1)
-    conduct_new = lookup_call(ids_square, temp_new, t_lo, t_hi, conduct)
+    conduct_new = lookup_call(ids, temp_new, t_lo, t_hi, conduct)
     return (electric, magnetic, temp_new, conduct_new)
 
 

time: 94.5 us -> 78.6 us (0.83)
  waiting for transfers between devices: 30.3 us -> 13.2 us
  starting transfers between devices: 26.5 us -> 34.1 us
  local copies, waits for them, and re-layouts: 11.1 us -> 5.9 us
  other arithmetic: 3.58 us -> 1.86 us
    ppermute x8, waiting for transfers between devices: 23.2 us -> 6.47 us  [passed_along(): return lax.ppermute(array, axis, pairs)]
    ppermute x0 -> x2, starting transfers between devices: none -> 5.81 us  [along_both(): return lax.ppermute(array, ('slab', 'sub'), pairs)]
    unnamed x32 -> x28, local copies, waits for them, and re-layouts: 9.64 us -> 5.88 us
    pallas_call x3, Pallas kernels: 3.09 us -> 5.63 us  [the longest x1 3.6 us: halo_exchange(): pl.pallas_call(functools.partial(pack_kernel, edges), in_specs=[pl.BlockS...]
    add x2 -> x1, other arithmetic: 3.52 us -> 0.99 us  [on_device(): here + from_low[R:] + from_high[:-R]]
    ppermute x8, starting transfers between devices: 21.7 us -> 23.9 us  [passed_along(): return lax.ppermute(array, axis, pairs)]
    pallas_call x1, Pallas kernels: 2.69 us -> 1.51 us  [thermal_call(): pl.pallas_call(functools.partial(thermal_kernel, lax.axis_size('slab'), l...]
    ppermute x5, waiting for transfers between devices: 7.06 us -> 5.89 us  [swapped(): return lax.ppermute(array, axis, [(0, 1), (1, 0)])]
  transfers between devices with their start and end apart: 13 -> 15, of which waited for: 10 -> 7; matrix products, arithmetic and copies ran while one was open for 4% -> 1% of each run, Pallas kernels for 0% -> 3%
where the time goes in v2:
time: 78.6 us; the launch traced here: 77.9 us
  starting transfers between devices  34.1 us (43%)
  Pallas kernels  21.9 us (28%)
  waiting for transfers between devices  13.2 us (17%)
  local copies, waits for them, and re-layouts  5.9 us (8%)
  other arithmetic  1.86 us (2%)
  between operations  0.95 us (1%)
    ppermute x8, starting transfers between devices, passed_along(): return lax.ppermute(array, axis, pairs)  23.9 us
    pallas_call x1, Pallas kernels, main_call(): pl.pallas_call(functools.partial(main_kernel, lax.axis_size('slab'), lax....  13.2 us
    ppermute x8, waiting for transfers between devices, passed_along(): return lax.ppermute(array, axis, pairs)  6.47 us
    ppermute x5, waiting for transfers between devices, swapped(): return lax.ppermute(array, axis, [(0, 1), (1, 0)])  5.89 us
    unnamed x28, local copies, waits for them, and re-layouts  5.88 us
    ppermute x2, starting transfers between devices, along_both(): return lax.ppermute(array, ('slab', 'sub'), pairs)  5.81 us
    ppermute x5, starting transfers between devices, swapped(): return lax.ppermute(array, axis, [(0, 1), (1, 0)])  4.3 us
    pallas_call x1, Pallas kernels, halo_exchange(): pl.pallas_call(functools.partial(pack_kernel, edges), in_specs=[pl.BlockS...  3.6 us
  transfers between devices with their start and end apart: 15, of which 7 were waited for; matrix products, arithmetic and copies ran while one was open for 1% of the time, Pallas kernels for 3%

profile of v2, /device:TPU:0, one launch (start us, length us, event | category | flops | bytes accessed | tf_op | source)
XLA Modules:
  0.0 77.9 jit_solution(1254496159799722853)
XLA Ops:
  0.6 3.6 %pack.1 = (s32[8,128]{1,0:T(8,128)}, f32[27,32,128]{2,1,0:T(8,128)}, f32[24,32,128]{2,1,0:T(8,128)}, f32[116,8,128]{2,1,0:T(8,128)}, f32[14,8,128]{2,1,0:T(8,128)}, /*index=5*/f32[14,8,128]{2,1,0:T(8,128)}) custom-call(f32[3,32,32,128]{3,2,1,0:T(8,128)} %e_ref.4, f32[3,32,32,128]{3,2,1,0:T(8,128)} %h_ref.4, f32[32,32,128]{2,1,0:T(8,128)} %c_ref.6, ...), custom_call_target="tpu_custom_call" | custom-call | tf_op jit(solution)/shard_map/pack/pallas_call | solution.py:187
  4.2 3.0 %collective-permute-start.2 = (f32[116,8,128]{2,1,0:T(8,128)}, f32[116,8,128]{2,1,0:T(8,128)S(1)}, u32[]{:S(2)}, u32[]{:S(2)}) collective-permute-start(f32[116,8,128]{2,1,0:T(8,128)} %get-tuple-element.37), channel_id=1, source_target_pairs={{0,2},{2,0},{1,3},{3,1},{4,6},{6,4},{5,7},{7,5},{8,10},{10,8},{9,1... | collective-permute-start | bytes 1425416 | tf_op jit(solution)/shard_map/ppermute | solution.py:45
  7.2 3.5 %collective-permute-start = (f32[27,32,128]{2,1,0:T(8,128)}, f32[27,32,128]{2,1,0:T(8,128)S(1)}, u32[]{:S(2)}, u32[]{:S(2)}) collective-permute-start(f32[27,32,128]{2,1,0:T(8,128)} %get-tuple-element.35), channel_id=1, source_target_pairs={{0,4},{4,8},{8,12},{1,5},{5,9},{9,13},{2,6},{6,10},{10,14},{3,7},{... | collective-permute-start | bytes 1327112 | tf_op jit(solution)/shard_map/ppermute | solution.py:41
  10.8 1.3 %collective-permute-start.1 = (f32[24,32,128]{2,1,0:T(8,128)}, f32[24,32,128]{2,1,0:T(8,128)S(1)}, u32[]{:S(2)}, u32[]{:S(2)}) collective-permute-start(f32[24,32,128]{2,1,0:T(8,128)} %get-tuple-element.36), channel_id=1, source_target_pairs={{4,0},{8,4},{12,8},{5,1},{9,5},{13,9},{6,2},{10,6},{14,10},{7,3},{... | collective-permute-start | bytes 1179656 | tf_op jit(solution)/shard_map/ppermute | solution.py:41
  12.1 4.5 %collective-permute-start.3 = (f32[14,8,128]{2,1,0:T(8,128)}, f32[14,8,128]{2,1,0:T(8,128)S(1)}, u32[]{:S(2)}, u32[]{:S(2)}) collective-permute-start(f32[14,8,128]{2,1,0:T(8,128)} %get-tuple-element.38), channel_id=1, source_target_pairs={{0,6},{2,4},{4,10},{6,8},{8,14},{10,12},{1,7},{3,5},{5,11},{7,9},{... | collective-permute-start | bytes 172040 | tf_op jit(solution)/shard_map/ppermute | solution.py:175
  16.6 1.3 %collective-permute-start.4 = (f32[14,8,128]{2,1,0:T(8,128)}, f32[14,8,128]{2,1,0:T(8,128)S(1)}, u32[]{:S(2)}, u32[]{:S(2)}) collective-permute-start(f32[14,8,128]{2,1,0:T(8,128)} %get-tuple-element.39), channel_id=1, source_target_pairs={{4,2},{6,0},{8,6},{10,4},{12,10},{14,8},{5,3},{7,1},{9,7},{11,5},{... | collective-permute-start | bytes 172040 | tf_op jit(solution)/shard_map/ppermute | solution.py:175
  17.9 0.0 copy-start.1
  17.9 1.4 %copy-done.1 = f32[3,32,32,128]{3,2,1,0:T(8,128)S(1)} copy-done((f32[3,32,32,128]{3,2,1,0:T(8,128)S(1)}, f32[3,32,32,128]{3,2,1,0:T(8,128)}, u32[]{:S(2)}) %copy-start.1) | copy-done | bytes 1572888
  19.3 1.0 %copy-done.3 = f32[32,32,128]{2,1,0:T(8,128)S(1)} copy-done((f32[32,32,128]{2,1,0:T(8,128)S(1)}, f32[32,32,128]{2,1,0:T(8,128)}, u32[]{:S(2)}) %copy-start.3) | copy-done | bytes 524312
  20.3 0.9 %copy-done.6 = f32[16,16,128]{2,1,0:T(8,128)S(1)} copy-done((f32[16,16,128]{2,1,0:T(8,128)S(1)}, f32[16,16,128]{2,1,0:T(8,128)}, u32[]{:S(2)}) %copy-start.6) | copy-done | bytes 131096
  21.3 0.9 %copy-done.9 = f32[16,16,128]{2,1,0:T(8,128)S(1)} copy-done((f32[16,16,128]{2,1,0:T(8,128)S(1)}, f32[16,16,128]{2,1,0:T(8,128)}, u32[]{:S(2)}) %copy-start.9) | copy-done | bytes 131096
  22.2 1.3 %columns.1.own_ref = f32[12,128,128]{2,1,0:T(8,128)S(1)} custom-call(f32[3,32,32,128]{3,2,1,0:T(8,128)S(1)} %copy-done, f32[3,32,32,128]{3,2,1,0:T(8,128)S(1)} %copy-done.1, f32[32,32,128]{2,1,0:T(8,128)S(1)} %copy-done.3, f32[16,16,128]{2,1,0:T(8,128)S(1)} %copy-done.6, f32[16,16,128]{2,1,0:T(8,128)S(1)} %copy-done.9), custom_call_target="tpu_custom_call" | custom-call | flops 10000000 | bytes 8000000 | tf_op jit(solution)/shard_map/columns/pallas_call | solution.py:320
  23.4 0.0 copy-start.2
  23.4 0.0 copy-start.7
  23.5 0.0 collective-permute-done.3.kl0_ref.kh0_ref
  23.5 0.9 %collective-permute-done.4.kl1_ref.kh1_ref = f32[14,8,128]{2,1,0:T(8,128)S(1)} collective-permute-done((f32[14,8,128]{2,1,0:T(8,128)}, f32[14,8,128]{2,1,0:T(8,128)S(1)}, u32[]{:S(2)}, u32[]{:S(2)}) %collective-permute-start.4) | collective-permute-done | bytes 57376 | tf_op jit(solution)/shard_map/ppermute | solution.py:175
  24.4 0.0 collective-permute-done.1.hi_ref
  24.4 0.0 collective-permute-done.lo_ref
  24.4 0.0 collective-permute-done.2.ml_ref.mh_ref
  24.4 0.1 collective-permute-start.5
  24.4 0.8 rims.1.own_rim
  25.2 0.6 collective-permute-start.6
  25.8 1.1 %collective-permute-done.6.other_rim = f32[2,128,128]{2,1,0:T(8,128)S(1)} collective-permute-done((f32[2,128,128]{2,1,0:T(8,128)S(1)}, f32[2,128,128]{2,1,0:T(8,128)S(1)}, u32[]{:S(2)}, u32[]{:S(2)}) %collective-permute-start.6) | collective-permute-done | bytes 131104 | tf_op jit(solution)/shard_map/ppermute | solution.py:45
  26.9 0.0 collective-permute-done.5.other_ref
  26.9 13.2 %leapfrog.1 = (f32[3,32,32,128]{3,2,1,0:T(8,128)}, f32[3,32,32,128]{3,2,1,0:T(8,128)}, f32[3,16,16,128]{3,2,1,0:T(8,128)S(1)}) custom-call(f32[3,32,32,128]{3,2,1,0:T(8,128)S(1)} %copy-done, f32[3,32,32,128]{3,2,1,0:T(8,128)S(1)} %copy-done.2, f32[32,32,128]{2,1,0:T(8,128)S(1)} %copy-done.3, f32[16,16,128]{2,1,0:T(8,128)S(1)} %copy-done.7, ...), custom_call_target="tpu_custom_call" | custom-call | tf_op jit(solution)/shard_map/leapfrog/pallas_call | solution.py:605
  40.2 0.0 copy-start.11
  40.2 0.0 copy-start.8
  40.2 0.0 copy-start.10
  40.3 0.7 copy-done.11
  41.0 5.3 %collective-permute-start.7 = (f32[18,16,128]{2,1,0:T(8,128)S(1)}, f32[18,16,128]{2,1,0:T(8,128)}, u32[]{:S(2)}, u32[]{:S(2)}) collective-permute-start(f32[18,16,128]{2,1,0:T(8,128)S(1)} %pad_maximum_fusion.1), channel_id=1, source_target_pairs={{0,4},{4,8},{8,12},{1,5},{5,9},{9,13},{2,6},{6,10},{10,14},{3,7},{... | collective-permute-start | bytes 442376 | tf_op jit(solution)/shard_map/ppermute | solution.py:41
  46.3 1.3 %collective-permute-start.9 = (f32[18,16,128]{2,1,0:T(8,128)S(1)}, f32[18,16,128]{2,1,0:T(8,128)S(1)}, u32[]{:S(2)}, u32[]{:S(2)}) collective-permute-start(f32[18,16,128]{2,1,0:T(8,128)S(1)} %pad_maximum_fusion.2), channel_id=1, source_target_pairs={{4,0},{8,4},{12,8},{5,1},{9,5},{13,9},{6,2},{10,6},{14,10},{7,3},{... | collective-permute-start | bytes 442376 | tf_op jit(solution)/shard_map/ppermute | solution.py:41
  47.6 1.3 %collective-permute-start.10 = (f32[2,16,128]{2,1,0:T(8,128)S(1)}, f32[2,16,128]{2,1,0:T(8,128)S(1)}, u32[]{:S(2)}, u32[]{:S(2)}) collective-permute-start(f32[2,16,128]{2,1,0:T(8,128)S(1)} %get-tuple-element.54), channel_id=1, source_target_pairs={{8,0},{12,4},{9,1},{13,5},{10,2},{14,6},{11,3},{15,7},{24,16},{28,... | collective-permute-start | bytes 49160 | tf_op jit(solution)/shard_map/ppermute | solution.py:41
  48.9 5.4 %collective-permute-start.8 = (f32[2,16,128]{2,1,0:T(8,128)S(1)}, f32[2,16,128]{2,1,0:T(8,128)S(1)}, u32[]{:S(2)}, u32[]{:S(2)}) collective-permute-start(f32[2,16,128]{2,1,0:T(8,128)S(1)} %get-tuple-element.56), channel_id=1, source_target_pairs={{0,8},{4,12},{1,9},{5,13},{2,10},{6,14},{3,11},{7,15},{16,24},{20,... | collective-permute-start | bytes 49160 | tf_op jit(solution)/shard_map/ppermute | solution.py:41
  54.3 0.0 collective-permute-done.9
  54.4 1.0 %slice_add_fusion = f32[16,16,128]{2,1,0:T(8,128)S(1)} fusion(f32[18,16,128]{2,1,0:T(8,128)S(1)} %collective-permute-done.9, f32[18,16,128]{2,1,0:T(8,128)} %collective-permute-done.7, f32[3,16,16,128]{3,2,1,0:T(8,128)} %copy-done.11), kind=kLoop, calls=%fused_computation.6 | loop fusion | flops 65536 | bytes 524288 | tf_op jit(solution)/shard_map/add | solution.py:792
  55.4 0.4 collective-permute-done.8
  55.8 0.8 fusion.3
  56.5 0.6 collective-permute-start.11
  57.2 3.2 %collective-permute-done.11 = f32[20,2,128]{2,1,0:T(2,128)S(1)} collective-permute-done((f32[20,2,128]{2,1,0:T(2,128)S(1)}, f32[20,2,128]{2,1,0:T(2,128)S(1)}, u32[]{:S(2)}, u32[]{:S(2)}) %collective-permute-start.11) | collective-permute-done | bytes 20512 | tf_op jit(solution)/shard_map/ppermute | solution.py:45
  60.5 0.1 collective-permute-start.12
  60.5 1.5 %collective-permute-done.12.zo_ref = f32[20,20,128]{2,1,0:T(8,128)S(1)} collective-permute-done((f32[20,20,128]{2,1,0:T(8,128)S(1)}, f32[20,20,128]{2,1,0:T(8,128)S(1)}, u32[]{:S(2)}, u32[]{:S(2)}) %collective-permute-start.12) | collective-permute-done | bytes 204832 | tf_op jit(solution)/shard_map/ppermute | solution.py:45
  62.1 1.5 %conduction.1.t_ref = f32[16,16,128]{2,1,0:T(8,128)} custom-call(f32[20,20,128]{2,1,0:T(8,128)S(1)} %pad_maximum_fusion.z_ref, f32[20,20,128]{2,1,0:T(8,128)S(1)} %collective-permute-done.12.zo_ref, f32[16,16,128]{2,1,0:T(8,128)S(1)} %copy-done.8, f32[16,16,128]{2,1,0:T(8,128)S(1)} %copy-done.10, f32[27,32,128]{2,1,0:T(8,128)S(1)} %collective-permute-done.lo_ref, ...), custom_call_target="tpu_custom_call" | custom-call | tf_op jit(solution)/shard_map/conduction/pallas_call | solution.py:715
  63.6 4.5 %collective-permute-start.13 = (f32[16,16,128]{2,1,0:T(8,128)}, f32[16,16,128]{2,1,0:T(8,128)S(1)}, u32[]{:S(2)}, u32[]{:S(2)}) collective-permute-start(f32[16,16,128]{2,1,0:T(8,128)} %conduction.1.t_ref), channel_id=1, source_target_pairs={{0,4},{4,8},{8,12},{1,5},{5,9},{9,13},{2,6},{6,10},{10,14},{3,7},{... | collective-permute-start | bytes 393224 | tf_op jit(solution)/shard_map/ppermute | solution.py:41
  68.1 1.3 %collective-permute-start.14 = (f32[16,16,128]{2,1,0:T(8,128)}, f32[16,16,128]{2,1,0:T(8,128)S(1)}, u32[]{:S(2)}, u32[]{:S(2)}) collective-permute-start(f32[16,16,128]{2,1,0:T(8,128)} %conduction.1.t_ref), channel_id=1, source_target_pairs={{4,0},{8,4},{12,8},{5,1},{9,5},{13,9},{6,2},{10,6},{14,10},{7,3},{... | collective-permute-start | bytes 393224 | tf_op jit(solution)/shard_map/ppermute | solution.py:41
  69.4 2.0 %collective-permute-done.13.lo_ref = f32[16,16,128]{2,1,0:T(8,128)S(1)} collective-permute-done((f32[16,16,128]{2,1,0:T(8,128)}, f32[16,16,128]{2,1,0:T(8,128)S(1)}, u32[]{:S(2)}, u32[]{:S(2)}) %collective-permute-start.13) | collective-permute-done | bytes 131104 | tf_op jit(solution)/shard_map/ppermute | solution.py:41
  71.5 4.0 %collective-permute-done.14.hi_ref = f32[16,16,128]{2,1,0:T(8,128)S(1)} collective-permute-done((f32[16,16,128]{2,1,0:T(8,128)}, f32[16,16,128]{2,1,0:T(8,128)S(1)}, u32[]{:S(2)}, u32[]{:S(2)}) %collective-permute-start.14) | collective-permute-done | bytes 131104 | tf_op jit(solution)/shard_map/ppermute | solution.py:41
  75.5 0.9 %copy-done.12 = f32[16,16,128]{2,1,0:T(8,128)S(1)} copy-done((f32[16,16,128]{2,1,0:T(8,128)S(1)}, f32[16,16,128]{2,1,0:T(8,128)}, u32[]{:S(2)}) %copy-start.12) | copy-done | bytes 131096
  76.4 1.6 %lookup.1 = f32[32,32,128]{2,1,0:T(8,128)} custom-call(s32[8,128]{1,0:T(8,128)S(1)} %copy-done.13, f32[16,16,128]{2,1,0:T(8,128)S(1)} %copy-done.12, f32[16,16,128]{2,1,0:T(8,128)S(1)} %collective-permute-done.13.lo_ref, f32[16,16,128]{2,1,0:T(8,128)S(1)} %collective-permute-done.14.hi_ref, f32[32,32,128]{2,1,0:T(8,128)S(1)} %copy-done.3), custom_call_target="tpu_custom_call" | custom-call | tf_op jit(solution)/shard_map/lookup/pallas_call | solution.py:745
  (25 shorter events, 0.2 us)
Async XLA Ops:
  0.6 17.3 %copy-start = (f32[3,32,32,128]{3,2,1,0:T(8,128)S(1)}, f32[3,32,32,128]{3,2,1,0:T(8,128)}, u32[]{:S(2)}) copy-start(f32[3,32,32,128]{3,2,1,0:T(8,128)} %e_ref.4) | copy-start | bytes 4718596
  4.2 20.1 %collective-permute-start.2 = (f32[116,8,128]{2,1,0:T(8,128)}, f32[116,8,128]{2,1,0:T(8,128)S(1)}, u32[]{:S(2)}, u32[]{:S(2)}) collective-permute-start(f32[116,8,128]{2,1,0:T(8,128)} %get-tuple-element.37), channel_id=1, source_target_pairs={{0,2},{2,0},{1,3},{3,1},{4,6},{6,4},{5,7},{7,5},{8,10},{10,8},{9,1... | collective-permute-start | bytes 1425416 | tf_op jit(solution)/shard_map/ppermute | solution.py:45
  7.2 17.1 %collective-permute-start = (f32[27,32,128]{2,1,0:T(8,128)}, f32[27,32,128]{2,1,0:T(8,128)S(1)}, u32[]{:S(2)}, u32[]{:S(2)}) collective-permute-start(f32[27,32,128]{2,1,0:T(8,128)} %get-tuple-element.35), channel_id=1, source_target_pairs={{0,4},{4,8},{8,12},{1,5},{5,9},{9,13},{2,6},{6,10},{10,14},{3,7},{... | collective-permute-start | bytes 1327112 | tf_op jit(solution)/shard_map/ppermute | solution.py:41
  10.8 13.6 %collective-permute-start.1 = (f32[24,32,128]{2,1,0:T(8,128)}, f32[24,32,128]{2,1,0:T(8,128)S(1)}, u32[]{:S(2)}, u32[]{:S(2)}) collective-permute-start(f32[24,32,128]{2,1,0:T(8,128)} %get-tuple-element.36), channel_id=1, source_target_pairs={{4,0},{8,4},{12,8},{5,1},{9,5},{13,9},{6,2},{10,6},{14,10},{7,3},{... | collective-permute-start | bytes 1179656 | tf_op jit(solution)/shard_map/ppermute | solution.py:41
  12.1 11.4 %collective-permute-start.3 = (f32[14,8,128]{2,1,0:T(8,128)}, f32[14,8,128]{2,1,0:T(8,128)S(1)}, u32[]{:S(2)}, u32[]{:S(2)}) collective-permute-start(f32[14,8,128]{2,1,0:T(8,128)} %get-tuple-element.38), channel_id=1, source_target_pairs={{0,6},{2,4},{4,10},{6,8},{8,14},{10,12},{1,7},{3,5},{5,11},{7,9},{... | collective-permute-start | bytes 172040 | tf_op jit(solution)/shard_map/ppermute | solution.py:175
  16.6 7.8 %collective-permute-start.4 = (f32[14,8,128]{2,1,0:T(8,128)}, f32[14,8,128]{2,1,0:T(8,128)S(1)}, u32[]{:S(2)}, u32[]{:S(2)}) collective-permute-start(f32[14,8,128]{2,1,0:T(8,128)} %get-tuple-element.39), channel_id=1, source_target_pairs={{4,2},{6,0},{8,6},{10,4},{12,10},{14,8},{5,3},{7,1},{9,7},{11,5},{... | collective-permute-start | bytes 172040 | tf_op jit(solution)/shard_map/ppermute | solution.py:175
  17.9 1.4 %copy-start.1 = (f32[3,32,32,128]{3,2,1,0:T(8,128)S(1)}, f32[3,32,32,128]{3,2,1,0:T(8,128)}, u32[]{:S(2)}) copy-start(f32[3,32,32,128]{3,2,1,0:T(8,128)} %h_ref.4) | copy-start | bytes 4718596
  19.3 1.0 %copy-start.3 = (f32[32,32,128]{2,1,0:T(8,128)S(1)}, f32[32,32,128]{2,1,0:T(8,128)}, u32[]{:S(2)}) copy-start(f32[32,32,128]{2,1,0:T(8,128)} %c_ref.6) | copy-start | bytes 1572868
  20.3 0.9 %copy-start.6 = (f32[16,16,128]{2,1,0:T(8,128)S(1)}, f32[16,16,128]{2,1,0:T(8,128)}, u32[]{:S(2)}) copy-start(f32[16,16,128]{2,1,0:T(8,128)} %t_ref.6) | copy-start | bytes 393220
  21.2 0.9 %copy-start.9 = (f32[16,16,128]{2,1,0:T(8,128)S(1)}, f32[16,16,128]{2,1,0:T(8,128)}, u32[]{:S(2)}) copy-start(f32[16,16,128]{2,1,0:T(8,128)} %cap_ref.4) | copy-start | bytes 393220
  23.4 3.5 %copy-start.2 = (f32[3,32,32,128]{3,2,1,0:T(8,128)S(1)}, f32[3,32,32,128]{3,2,1,0:T(8,128)}, u32[]{:S(2)}) copy-start(f32[3,32,32,128]{3,2,1,0:T(8,128)} %h_ref.4) | copy-start | bytes 4718596
  23.4 3.5 %copy-start.7 = (f32[16,16,128]{2,1,0:T(8,128)S(1)}, f32[16,16,128]{2,1,0:T(8,128)}, u32[]{:S(2)}) copy-start(f32[16,16,128]{2,1,0:T(8,128)} %t_ref.6) | copy-start | bytes 393220
  23.5 3.5 %copy-start.13 = (s32[8,128]{1,0:T(8,128)S(1)}, s32[8,128]{1,0:T(8,128)}, u32[]{:S(2)}) copy-start(s32[8,128]{1,0:T(8,128)} %get-tuple-element.29.ids_ref) | copy-start | bytes 12292
  24.4 2.5 %collective-permute-start.5 = (f32[12,128,128]{2,1,0:T(8,128)S(1)}, f32[12,128,128]{2,1,0:T(8,128)S(1)}, u32[]{:S(2)}, u32[]{:S(2)}) collective-permute-start(f32[12,128,128]{2,1,0:T(8,128)S(1)} %columns.1.own_ref), channel_id=1, source_target_pairs={{0,1},{1,0},{2,3},{3,2},{4,5},{5,4},{6,7},{7,6},{8,9},{9,8},{10,11... | collective-permute-start | bytes 2359304 | tf_op jit(solution)/shard_map/ppermute | solution.py:45
  25.2 1.7 %collective-permute-start.6 = (f32[2,128,128]{2,1,0:T(8,128)S(1)}, f32[2,128,128]{2,1,0:T(8,128)S(1)}, u32[]{:S(2)}, u32[]{:S(2)}) collective-permute-start(f32[2,128,128]{2,1,0:T(8,128)S(1)} %rims.1.own_rim), channel_id=1, source_target_pairs={{0,1},{1,0},{2,3},{3,2},{4,5},{5,4},{6,7},{7,6},{8,9},{9,8},{10,11... | collective-permute-start | bytes 393224 | tf_op jit(solution)/shard_map/ppermute | solution.py:45
  26.9 13.2 %copy-start.4 = (f32[12,128,128]{2,1,0:T(8,128)}, f32[12,128,128]{2,1,0:T(8,128)S(1)}, u32[]{:S(2)}) copy-start(f32[12,128,128]{2,1,0:T(8,128)S(1)} %collective-permute-done.5.other_ref) | copy-start | bytes 2359300
  40.2 0.7 copy-start.11
  40.2 21.9 %copy-start.8 = (f32[16,16,128]{2,1,0:T(8,128)S(1)}, f32[16,16,128]{2,1,0:T(8,128)}, u32[]{:S(2)}) copy-start(f32[16,16,128]{2,1,0:T(8,128)} %t_ref.6) | copy-start | bytes 393220
  40.2 21.8 %copy-start.10 = (f32[16,16,128]{2,1,0:T(8,128)S(1)}, f32[16,16,128]{2,1,0:T(8,128)}, u32[]{:S(2)}) copy-start(f32[16,16,128]{2,1,0:T(8,128)} %cap_ref.4) | copy-start | bytes 393220
  40.2 21.8 %copy-start.5 = (f32[12,128,128]{2,1,0:T(8,128)S(1)}, f32[12,128,128]{2,1,0:T(8,128)}, u32[]{:S(2)}) copy-start(f32[12,128,128]{2,1,0:T(8,128)} %copy-done.4) | copy-start | bytes 2359300
  41.0 13.4 %collective-permute-start.7 = (f32[18,16,128]{2,1,0:T(8,128)S(1)}, f32[18,16,128]{2,1,0:T(8,128)}, u32[]{:S(2)}, u32[]{:S(2)}) collective-permute-start(f32[18,16,128]{2,1,0:T(8,128)S(1)} %pad_maximum_fusion.1), channel_id=1, source_target_pairs={{0,4},{4,8},{8,12},{1,5},{5,9},{9,13},{2,6},{6,10},{10,14},{3,7},{... | collective-permute-start | bytes 442376 | tf_op jit(solution)/shard_map/ppermute | solution.py:41
  46.3 8.1 %collective-permute-start.9 = (f32[18,16,128]{2,1,0:T(8,128)S(1)}, f32[18,16,128]{2,1,0:T(8,128)S(1)}, u32[]{:S(2)}, u32[]{:S(2)}) collective-permute-start(f32[18,16,128]{2,1,0:T(8,128)S(1)} %pad_maximum_fusion.2), channel_id=1, source_target_pairs={{4,0},{8,4},{12,8},{5,1},{9,5},{13,9},{6,2},{10,6},{14,10},{7,3},{... | collective-permute-start | bytes 442376 | tf_op jit(solution)/shard_map/ppermute | solution.py:41
  47.6 7.8 %collective-permute-start.10 = (f32[2,16,128]{2,1,0:T(8,128)S(1)}, f32[2,16,128]{2,1,0:T(8,128)S(1)}, u32[]{:S(2)}, u32[]{:S(2)}) collective-permute-start(f32[2,16,128]{2,1,0:T(8,128)S(1)} %get-tuple-element.54), channel_id=1, source_target_pairs={{8,0},{12,4},{9,1},{13,5},{10,2},{14,6},{11,3},{15,7},{24,16},{28,... | collective-permute-start | bytes 49160 | tf_op jit(solution)/shard_map/ppermute | solution.py:41
  48.9 6.9 %collective-permute-start.8 = (f32[2,16,128]{2,1,0:T(8,128)S(1)}, f32[2,16,128]{2,1,0:T(8,128)S(1)}, u32[]{:S(2)}, u32[]{:S(2)}) collective-permute-start(f32[2,16,128]{2,1,0:T(8,128)S(1)} %get-tuple-element.56), channel_id=1, source_target_pairs={{0,8},{4,12},{1,9},{5,13},{2,10},{6,14},{3,11},{7,15},{16,24},{20,... | collective-permute-start | bytes 49160 | tf_op jit(solution)/shard_map/ppermute | solution.py:41
  56.5 3.8 %collective-permute-start.11 = (f32[20,2,128]{2,1,0:T(2,128)S(1)}, f32[20,2,128]{2,1,0:T(2,128)S(1)}, u32[]{:S(2)}, u32[]{:S(2)}) collective-permute-start(f32[20,2,128]{2,1,0:T(2,128)S(1)} %fusion.1), channel_id=1, source_target_pairs={{0,2},{2,0},{1,3},{3,1},{4,6},{6,4},{5,7},{7,5},{8,10},{10,8},{9,1... | collective-permute-start | bytes 61448 | tf_op jit(solution)/shard_map/ppermute | solution.py:45
  60.5 1.6 %collective-permute-start.12 = (f32[20,20,128]{2,1,0:T(8,128)S(1)}, f32[20,20,128]{2,1,0:T(8,128)S(1)}, u32[]{:S(2)}, u32[]{:S(2)}) collective-permute-start(f32[20,20,128]{2,1,0:T(8,128)S(1)} %pad_maximum_fusion.z_ref), channel_id=1, source_target_pairs={{0,1},{1,0},{2,3},{3,2},{4,5},{5,4},{6,7},{7,6},{8,9},{9,8},{10,11... | collective-permute-start | bytes 614408 | tf_op jit(solution)/shard_map/ppermute | solution.py:45
  63.6 7.9 %collective-permute-start.13 = (f32[16,16,128]{2,1,0:T(8,128)}, f32[16,16,128]{2,1,0:T(8,128)S(1)}, u32[]{:S(2)}, u32[]{:S(2)}) collective-permute-start(f32[16,16,128]{2,1,0:T(8,128)} %conduction.1.t_ref), channel_id=1, source_target_pairs={{0,4},{4,8},{8,12},{1,5},{5,9},{9,13},{2,6},{6,10},{10,14},{3,7},{... | collective-permute-start | bytes 393224 | tf_op jit(solution)/shard_map/ppermute | solution.py:41
  68.1 7.4 %collective-permute-start.14 = (f32[16,16,128]{2,1,0:T(8,128)}, f32[16,16,128]{2,1,0:T(8,128)S(1)}, u32[]{:S(2)}, u32[]{:S(2)}) collective-permute-start(f32[16,16,128]{2,1,0:T(8,128)} %conduction.1.t_ref), channel_id=1, source_target_pairs={{4,0},{8,4},{12,8},{5,1},{9,5},{13,9},{6,2},{10,6},{14,10},{7,3},{... | collective-permute-start | bytes 393224 | tf_op jit(solution)/shard_map/ppermute | solution.py:41
  75.5 0.9 %copy-start.12 = (f32[16,16,128]{2,1,0:T(8,128)S(1)}, f32[16,16,128]{2,1,0:T(8,128)}, u32[]{:S(2)}) copy-start(f32[16,16,128]{2,1,0:T(8,128)} %conduction.1.t_ref) | copy-start | bytes 393220

commit v3 on v2

--- a/solution.py
+++ b/solution.py
@@ -10,6 +10,7 @@
 STEPS = 4
 SWEEPS = 3
 W = STEPS
+R = SWEEPS - 1
 
 time_step = 0.5
 conduction = 2.0
@@ -20,7 +21,7 @@
 BF16 = jnp.bfloat16
 VMEM_LIMIT = 20 * 1024 * 1024
 SMALL_LIMIT = 12 * 1024 * 1024
-PACK_LIMIT = 62 * 1024 * 1024
+PACK_LIMIT = 60 * 1024 * 1024
 
 
 def chebyshev_constants(sweep_count):
@@ -361,7 +362,7 @@
     n_slab, n_sub,
     e_ref, h_ref, c_ref, t_ref, ids_ref, lo_ref, hi_ref, ml_ref, mh_ref,
     kl0_ref, kl1_ref, kh0_ref, kh1_ref, own_ref, other_ref, own_rim, other_rim,
-    e_out, h_out, d_out,
+    e_out, h_out, here_out, up_out, dn_out, far_up_out, far_dn_out,
     e_done, h_done, out_sem, es, hs, ce, ch, heat, sde, sdh, sce, sch, bt, bp,
 ):
     s_dev, y_dev, lanes = c_ref.shape
@@ -480,8 +481,8 @@
         h1 = (sdh[1, i] - ((up_x(e0) - e0) - (sde[2, i + 1] - e2))) * inside
         h2 = (sdh[2, i] - ((sde[1, i + 1] - e1) - (up_y(e0) - e0))) * inside
         sdh[0, i], sdh[1, i], sdh[2, i] = h0, h1, h2
-        bt[pl.ds(at + 8, 1), :] = h0[W - 1 : W] * h_on
-        bt[pl.ds(at + 9, 1), :] = h1[W - 1 : W] * h_on
+        bt[pl.ds(at + 8, 1), :] = h1[W - 1 : W] * h_on
+        bt[pl.ds(at + 9, 1), :] = h0[W - 1 : W] * h_on
 
     def side_e(i):
         h0, h1, h2 = sdh[0, i], sdh[1, i], sdh[2, i]
@@ -506,8 +507,8 @@
     above = pl.ds(TOP + 1, y_ext)
     below = pl.ds(TOP - 1, y_ext)
 
-    def border(i, q, to):
-        shift = lax.rem(2 * lanes + to - (i % 8) * 16 - q, lanes)
+    def border(i, q):
+        shift = lax.rem(2 * lanes - 1 - (i % 8) * 16 - q, lanes)
         return pltpu.roll(bp[i // 8], shift, 1)
 
     def put_h(c, i, curl):
@@ -519,16 +520,20 @@
 
     def main_h(step, i):
         e0, e1, e2 = es[0, i, centre, :], es[1, i, centre, :], es[2, i, centre, :]
-        e0x = jnp.where(is_last, border(i, 2 * step, lanes - 1), pltpu.roll(e0, lanes - 1, 1))
-        e1x = jnp.where(is_last, border(i, 2 * step + 1, lanes - 1), pltpu.roll(e1, lanes - 1, 1))
+        beyond = border(i, 2 * step)
+        e0x = jnp.where(is_last, beyond, pltpu.roll(e0, lanes - 1, 1))
+        beyond = border(i, 2 * step + 1)
+        e1x = jnp.where(is_last, beyond, pltpu.roll(e1, lanes - 1, 1))
         put_h(0, i, (es[2, i, above, :] - e2) - (e1x - e1))
         put_h(1, i, (e0x - e0) - (es[2, i + 1, centre, :] - e2))
         put_h(2, i, (es[1, i + 1, centre, :] - e1) - (es[0, i, above, :] - e0))
 
     def main_e(step, i):
         h0, h1, h2 = hs[0, i, centre, :], hs[1, i, centre, :], hs[2, i, centre, :]
-        h0x = jnp.where(is_first, border(i, 8 + 2 * step, 0), pltpu.roll(h0, 1, 1))
-        h1x = jnp.where(is_first, border(i, 8 + 2 * step + 1, 0), pltpu.roll(h1, 1, 1))
+        beyond = border(i, 8 + 2 * step)
+        h0x = jnp.where(is_first, beyond, pltpu.roll(h0, 1, 1))
+        beyond = border(i, 8 + 2 * step - 1)
+        h1x = jnp.where(is_first, beyond, pltpu.roll(h1, 1, 1))
         keep, gain = ce[i, centre, :], ch[i]
         e0, e1, e2 = es[0, i, centre, :], es[1, i, centre, :], es[2, i, centre, :]
         n0 = keep * e0 + gain * ((h2 - hs[2, i, below, :]) - (h1 - h1x))
@@ -543,14 +548,11 @@
 
     heat[...] = jnp.zeros_like(heat)
 
-    def main_step(step, carry):
-        for i in range(s_ext - 1):
+    for step in range(STEPS):
+        for i in range(step, s_ext - 1 - step):
             main_h(step, i)
-        for i in range(1, s_ext - 1):
+        for i in range(step + 1, s_ext - 1 - step):
             main_e(step, i)
-        return carry
-
-    lax.fori_loop(0, STEPS, main_step, 0)
 
     ys = pl.ds(TOP + W, y_dev)
     copies = []
@@ -571,7 +573,15 @@
         chosen = [jnp.where(kinds == ids[a : a + 1], 1.0, 0.0).astype(BF16) for a in range(ids.shape[0])]
         chosen = jnp.concatenate(chosen, 1)
         sums = jnp.dot(chosen, parts, preferred_element_type=F32)
-        d_out[n] = (sums[:, :lanes] + sums[:, lanes:]).reshape(t_ref.shape)
+        sums = (sums[:, :lanes] + sums[:, lanes:]).reshape(t_ref.shape)
+        if n == 0:
+            dn_out[pl.ds(0, t_ref.shape[0])] = sums
+            far_dn_out[...] = sums[:R]
+        elif n == 1:
+            here_out[...] = sums
+        else:
+            up_out[pl.ds(R, t_ref.shape[0])] = sums
+            far_up_out[...] = sums[-R:]
 
     ts, ty = t_ref.shape[0], t_ref.shape[1]
     per = lanes // ty
@@ -593,7 +603,12 @@
         left_x = jnp.where(lane_t == 0, from_low, pltpu.roll(x, 1, 1))
         right_x = jnp.where(lane_t == lanes - 1, from_high, pltpu.roll(x, lanes - 1, 1))
         beside = before + after + left_y + right_y + left_x + right_x
-        d_out[1, i] = d_out[1, i] - conduction * (6.0 * x - beside)
+        value = here_out[i] - conduction * (6.0 * x - beside)
+        here_out[i] = value
+        if i < R:
+            dn_out[ts + i] = value
+        if i >= ts - R:
+            up_out[i - ts + R] = value
     for copy in copies:
         copy.wait()
 
@@ -602,18 +617,20 @@
     s_dev, y_dev, lanes = conduct.shape
     s_ext, y_ext = s_dev + 2 * W, y_dev + 2 * W
     tall = TOP + y_ext + 8
+    ts, ty, _ = temp_old.shape
     return pl.pallas_call(
         functools.partial(main_kernel, lax.axis_size("slab"), lax.axis_size("sub")),
         out_shape=[
             jax.ShapeDtypeStruct(electric.shape, F32),
             jax.ShapeDtypeStruct(magnetic.shape, F32),
-            jax.ShapeDtypeStruct((3,) + temp_old.shape, F32),
+            jax.ShapeDtypeStruct(temp_old.shape, F32),
+            jax.ShapeDtypeStruct((ts + R, ty, lanes), F32),
+            jax.ShapeDtypeStruct((ts + R, ty, lanes), F32),
+            jax.ShapeDtypeStruct((R, ty, lanes), F32),
+            jax.ShapeDtypeStruct((R, ty, lanes), F32),
         ],
-        out_specs=[
-            pl.BlockSpec(memory_space=pl.ANY),
-            pl.BlockSpec(memory_space=pl.ANY),
-            pl.BlockSpec(memory_space=pltpu.VMEM),
-        ],
+        out_specs=[pl.BlockSpec(memory_space=pl.ANY)] * 2
+        + [pl.BlockSpec(memory_space=pltpu.VMEM)] * 5,
         scratch_shapes=[
             pltpu.VMEM(electric.shape, F32),
             pltpu.VMEM(magnetic.shape, F32),
@@ -635,13 +652,12 @@
     )(electric, magnetic, conduct, temp_old, ids, *halos)
 
 
-R = SWEEPS - 1
 TTOP = 8
 
 
 def thermal_kernel(
     n_slab, n_sub, z_ref, zo_ref, t_ref, cap_ref, lo_ref, hi_ref, ml_ref, mh_ref, other_ref,
-    out_ref, d0, d1, r0, cs,
+    out_ref, send_ref, d0, d1, r0, cs,
 ):
     ts, ty, lanes = t_ref.shape
     center, spread, rhos = chebyshev_constants(SWEEPS)
@@ -706,7 +722,9 @@
         resid = r0[0, i, chunk, :] - av
         last = (rhos[2] * rhos[1]) * v + (2.0 * rhos[2] / spread) * resid
         r0[0, i, chunk, :] = d0[0, i, chunk, :] + v + last
-        out_ref[i - R] = t_ref[i - R] + r0[0, i, mine, :]
+        value = t_ref[i - R] + r0[0, i, mine, :]
+        out_ref[i - R] = value
+        send_ref[i - R] = value
 
 
 def thermal_call(z, z_other, temp_old, capacity, lo, hi, m_lo, m_hi, other):
@@ -714,7 +732,7 @@
     wide = pltpu.VMEM((2, ts + 2 * R, TTOP + 24 + 8, lanes), F32)
     return pl.pallas_call(
         functools.partial(thermal_kernel, lax.axis_size("slab"), lax.axis_size("sub")),
-        out_shape=jax.ShapeDtypeStruct(temp_old.shape, F32),
+        out_shape=[jax.ShapeDtypeStruct(temp_old.shape, F32)] * 2,
         scratch_shapes=[wide, wide, wide, pltpu.VMEM((2, ts + 2, TTOP + 24 + 8, lanes), F32)],
         compiler_params=pltpu.CompilerParams(vmem_limit_bytes=SMALL_LIMIT),
         name="conduction",
@@ -750,19 +768,46 @@
     )(ids, temp_new, lo, hi, conduct)
 
 
-def sub_edges(values, depth):
-    count = lax.axis_size("sub")
-    index = lax.axis_index("sub")
-    length = values.shape[1]
-    if count == 2:
-        start = jnp.where(index == 0, length - depth, 0)
-        received = swapped(lax.dynamic_slice_in_dim(values, start, depth, axis=1), "sub")
-        zero = jnp.zeros_like(received)
-        return jnp.where(index == 0, zero, received), jnp.where(index == 0, received, zero)
-    return (
-        passed_along(values[:, length - depth :], "sub", 1),
-        passed_along(values[:, :depth], "sub", -1),
-    )
+def combine_kernel(
+    n_slab, edges, here_ref, up_ref, dn_ref, low_ref, high_ref, far_low_ref, far_high_ref,
+    out_ref, *edge_refs
+):
+    ts, ty, _ = here_ref.shape
+    slab_lo, slab_hi = inside_flags("slab", n_slab)
+    low = dn_ref[pl.ds(ts - R, R)] + low_ref[pl.ds(0, R)] + far_low_ref[...]
+    high = up_ref[pl.ds(R, R)] + high_ref[pl.ds(ts, R)] + far_high_ref[...]
+    out_ref[pl.ds(0, R)] = jnp.where(slab_lo, low, 0.0)
+    out_ref[pl.ds(R, ts)] = here_ref[...] + low_ref[pl.ds(R, ts)] + high_ref[pl.ds(0, ts)]
+    out_ref[pl.ds(R + ts, R)] = jnp.where(slab_hi, high, 0.0)
+    for edge, ref in zip(edges, edge_refs):
+        if edge == "either":
+            start = jnp.where(lax.axis_index("sub") == 0, ty - R, 0)
+        else:
+            start = ty - R if edge == "high" else 0
+        ref[...] = out_ref[:, pl.ds(start, R), :]
+
+
+def residual(here, up, dn, far_up, far_dn):
+    ts, ty, lanes = here.shape
+    from_low, from_high = passed_along(up, "slab", 1), passed_along(dn, "slab", -1)
+    far_low, far_high = passed_along(far_up, "slab", 2), passed_along(far_dn, "slab", -2)
+    two = lax.axis_size("sub") == 2
+    edges = ("either",) if two else ("high", "low")
+    r0, *messages = pl.pallas_call(
+        functools.partial(combine_kernel, lax.axis_size("slab"), edges),
+        out_shape=[jax.ShapeDtypeStruct((ts + 2 * R, ty, lanes), F32)]
+        + [jax.ShapeDtypeStruct((ts + 2 * R, R, lanes), F32)] * len(edges),
+        compiler_params=pltpu.CompilerParams(vmem_limit_bytes=SMALL_LIMIT),
+        name="combine",
+    )(here, up, dn, from_low, from_high, far_low, far_high)
+    if two:
+        received = swapped(messages[0], "sub")
+        index = lax.axis_index("sub")
+        y_lo, y_hi = jnp.where(index == 0, 0.0, received), jnp.where(index == 0, received, 0.0)
+    else:
+        y_lo = passed_along(messages[0], "sub", 1)
+        y_hi = passed_along(messages[1], "sub", -1)
+    return jnp.concatenate([y_lo, r0, y_hi], 1)
 
 
 def on_device(electric, magnetic, conduct, temp_old, capacity, offsets, targets):
@@ -777,26 +822,15 @@
     other = swapped(own, "comp")
     own_rim = rim_columns(conduct.shape[0], *halos)
     other_rim = swapped(own_rim, "comp")
-    electric, magnetic, sums = main_call(
+    electric, magnetic, *shares = main_call(
         electric, magnetic, conduct, temp_old, ids, *halos, own, other, own_rim, other_rim
     )
-    below, here, above = sums[0], sums[1], sums[2]
-    from_low = passed_along(jnp.concatenate([here[-R:], above], 0), "slab", 1)
-    from_high = passed_along(jnp.concatenate([below, here[:R]], 0), "slab", -1)
-    far_low = passed_along(above[-R:], "slab", 2)
-    far_high = passed_along(below[:R], "slab", -2)
-    index = lax.axis_index("slab")
-    low_rows = jnp.where(index > 0, below[-R:] + from_low[:R] + far_low, 0.0)
-    high_rows = above[:R] + from_high[-R:] + far_high
-    high_rows = jnp.where(index < lax.axis_size("slab") - 1, high_rows, 0.0)
-    r0 = jnp.concatenate([low_rows, here + from_low[R:] + from_high[:-R], high_rows], 0)
-    y_lo, y_hi = sub_edges(r0, R)
-    z = jnp.concatenate([y_lo, r0, y_hi], 1)
+    z = residual(*shares)
     z_other = swapped(z, "comp")
-    temp_new = thermal_call(z, z_other, temp_old, capacity, lo, hi, m_lo, m_hi, other)
-    t_lo = passed_along(temp_new, "slab", 1)
-    t_hi = passed_along(temp_new, "slab", -1)
-    conduct_new = lookup_call(ids, temp_new, t_lo, t_hi, conduct)
+    temp_new, temp_sent = thermal_call(z, z_other, temp_old, capacity, lo, hi, m_lo, m_hi, other)
+    t_lo = passed_along(temp_sent, "slab", 1)
+    t_hi = passed_along(temp_sent, "slab", -1)
+    conduct_new = lookup_call(ids, temp_sent, t_lo, t_hi, conduct)
     return (electric, magnetic, temp_new, conduct_new)
 
 

time: 78.6 us -> 74.2 us (0.944)
  local copies, waits for them, and re-layouts: 5.9 us -> 2.35 us
  waiting for transfers between devices: 13.2 us -> 15.9 us
  other arithmetic: 1.86 us -> 0.06 us
  starting transfers between devices: 34.1 us -> 33.3 us
    unnamed x28 -> x20, local copies, waits for them, and re-layouts: 5.88 us -> 2.35 us
    ppermute x2, waiting for transfers between devices: 0.88 us -> 3.72 us  [along_both(): return lax.ppermute(array, ('slab', 'sub'), pairs)]
    ppermute x8, starting transfers between devices: 23.9 us -> 22.2 us  [passed_along(): return lax.ppermute(array, axis, pairs)]
    add x1 -> x0, other arithmetic: 0.99 us -> none  [on_device(): here + from_low[R:] + from_high[:-R]]
    ppermute x5, starting transfers between devices: 4.3 us -> 5.26 us  [swapped(): return lax.ppermute(array, axis, [(0, 1), (1, 0)])]
    ppermute x5, waiting for transfers between devices: 5.89 us -> 4.94 us  [swapped(): return lax.ppermute(array, axis, [(0, 1), (1, 0)])]
    ppermute x8, waiting for transfers between devices: 6.47 us -> 7.29 us  [passed_along(): return lax.ppermute(array, axis, pairs)]
    pallas_call x1, Pallas kernels: 13.2 us -> 12.4 us  [main_call(): pl.pallas_call(functools.partial(main_kernel, lax.axis_size('slab'), lax....]
  transfers between devices with their start and end apart: 15 -> 15, of which waited for: 7 -> 9; matrix products, arithmetic and copies ran while one was open for 1% -> 0% of each run, Pallas kernels for 3% -> 3%
where the time goes in v3:
time: 74.2 us; the launch traced here: 73.7 us
  starting transfers between devices  33.3 us (45%)
  Pallas kernels  21.2 us (29%)
  waiting for transfers between devices  15.9 us (21%)
  local copies, waits for them, and re-layouts  2.35 us (3%)
  between operations  0.9 us (1%)
    ppermute x8, starting transfers between devices, passed_along(): return lax.ppermute(array, axis, pairs)  22.2 us
    pallas_call x1, Pallas kernels, main_call(): pl.pallas_call(functools.partial(main_kernel, lax.axis_size('slab'), lax....  12.4 us
    ppermute x8, waiting for transfers between devices, passed_along(): return lax.ppermute(array, axis, pairs)  7.29 us
    ppermute x2, starting transfers between devices, along_both(): return lax.ppermute(array, ('slab', 'sub'), pairs)  5.81 us
    ppermute x5, starting transfers between devices, swapped(): return lax.ppermute(array, axis, [(0, 1), (1, 0)])  5.26 us
    ppermute x5, waiting for transfers between devices, swapped(): return lax.ppermute(array, axis, [(0, 1), (1, 0)])  4.94 us
    ppermute x2, waiting for transfers between devices, along_both(): return lax.ppermute(array, ('slab', 'sub'), pairs)  3.72 us
    pallas_call x1, Pallas kernels, halo_exchange(): pl.pallas_call(functools.partial(pack_kernel, edges), in_specs=[pl.BlockS...  3.63 us
  transfers between devices with their start and end apart: 15, of which 9 were waited for; matrix products, arithmetic and copies ran while one was open for 0% of the time, Pallas kernels for 3%

profile of v3, /device:TPU:0, one launch (start us, length us, event | category | flops | bytes accessed | tf_op | source)
XLA Modules:
  0.0 73.7 jit_solution(6879192126239456955)
XLA Ops:
  0.6 0.0 copy-start
  0.7 0.0 copy-start.7
  0.7 3.6 %pack.1 = (s32[8,128]{1,0:T(8,128)}, f32[27,32,128]{2,1,0:T(8,128)}, f32[24,32,128]{2,1,0:T(8,128)}, f32[116,8,128]{2,1,0:T(8,128)}, f32[14,8,128]{2,1,0:T(8,128)}, /*index=5*/f32[14,8,128]{2,1,0:T(8,128)}) custom-call(f32[3,32,32,128]{3,2,1,0:T(8,128)} %e_ref.4, f32[3,32,32,128]{3,2,1,0:T(8,128)} %h_ref.4, f32[32,32,128]{2,1,0:T(8,128)} %c_ref.6, ...), custom_call_target="tpu_custom_call" | custom-call | tf_op jit(solution)/shard_map/pack/pallas_call | solution.py:188
  4.3 3.0 %collective-permute-start.2 = (f32[116,8,128]{2,1,0:T(8,128)}, f32[116,8,128]{2,1,0:T(8,128)S(1)}, u32[]{:S(2)}, u32[]{:S(2)}) collective-permute-start(f32[116,8,128]{2,1,0:T(8,128)} %get-tuple-element.45), channel_id=1, source_target_pairs={{0,2},{2,0},{1,3},{3,1},{4,6},{6,4},{5,7},{7,5},{8,10},{10,8},{9,1... | collective-permute-start | bytes 1425416 | tf_op jit(solution)/shard_map/ppermute | solution.py:46
  7.3 3.5 %collective-permute-start = (f32[27,32,128]{2,1,0:T(8,128)}, f32[27,32,128]{2,1,0:T(8,128)S(1)}, u32[]{:S(2)}, u32[]{:S(2)}) collective-permute-start(f32[27,32,128]{2,1,0:T(8,128)} %get-tuple-element.43), channel_id=1, source_target_pairs={{0,4},{4,8},{8,12},{1,5},{5,9},{9,13},{2,6},{6,10},{10,14},{3,7},{... | collective-permute-start | bytes 1327112 | tf_op jit(solution)/shard_map/ppermute | solution.py:42
  10.8 1.3 %collective-permute-start.1 = (f32[24,32,128]{2,1,0:T(8,128)}, f32[24,32,128]{2,1,0:T(8,128)S(1)}, u32[]{:S(2)}, u32[]{:S(2)}) collective-permute-start(f32[24,32,128]{2,1,0:T(8,128)} %get-tuple-element.44), channel_id=1, source_target_pairs={{4,0},{8,4},{12,8},{5,1},{9,5},{13,9},{6,2},{10,6},{14,10},{7,3},{... | collective-permute-start | bytes 1179656 | tf_op jit(solution)/shard_map/ppermute | solution.py:42
  12.1 4.5 %collective-permute-start.3 = (f32[14,8,128]{2,1,0:T(8,128)}, f32[14,8,128]{2,1,0:T(8,128)S(1)}, u32[]{:S(2)}, u32[]{:S(2)}) collective-permute-start(f32[14,8,128]{2,1,0:T(8,128)} %get-tuple-element.46), channel_id=1, source_target_pairs={{0,6},{2,4},{4,10},{6,8},{8,14},{10,12},{1,7},{3,5},{5,11},{7,9},{... | collective-permute-start | bytes 172040 | tf_op jit(solution)/shard_map/ppermute | solution.py:176
  16.6 1.3 %collective-permute-start.4 = (f32[14,8,128]{2,1,0:T(8,128)}, f32[14,8,128]{2,1,0:T(8,128)S(1)}, u32[]{:S(2)}, u32[]{:S(2)}) collective-permute-start(f32[14,8,128]{2,1,0:T(8,128)} %get-tuple-element.47), channel_id=1, source_target_pairs={{4,2},{6,0},{8,6},{10,4},{12,10},{14,8},{5,3},{7,1},{9,7},{11,5},{... | collective-permute-start | bytes 172040 | tf_op jit(solution)/shard_map/ppermute | solution.py:176
  17.9 0.0 copy-done
  18.0 0.0 copy-done.3
  18.0 0.0 copy-done.6
  18.0 0.0 copy-done.7
  18.0 0.0 copy-start.1
  18.0 1.4 %copy-done.1 = f32[3,32,32,128]{3,2,1,0:T(8,128)S(1)} copy-done((f32[3,32,32,128]{3,2,1,0:T(8,128)S(1)}, f32[3,32,32,128]{3,2,1,0:T(8,128)}, u32[]{:S(2)}) %copy-start.1) | copy-done | bytes 1572888
  19.4 1.3 %columns.1.own_ref = f32[12,128,128]{2,1,0:T(8,128)S(1)} custom-call(f32[3,32,32,128]{3,2,1,0:T(8,128)S(1)} %copy-done, f32[3,32,32,128]{3,2,1,0:T(8,128)S(1)} %copy-done.1, f32[32,32,128]{2,1,0:T(8,128)S(1)} %copy-done.3, f32[16,16,128]{2,1,0:T(8,128)S(1)} %copy-done.6, f32[16,16,128]{2,1,0:T(8,128)S(1)} %copy-done.7), custom_call_target="tpu_custom_call" | custom-call | flops 10000000 | bytes 8000000 | tf_op jit(solution)/shard_map/columns/pallas_call | solution.py:321
  20.7 0.0 copy-start.2
  20.7 0.0 copy-start.9
  20.7 0.8 %collective-permute-done.3.kl0_ref.kh0_ref = f32[14,8,128]{2,1,0:T(8,128)S(1)} collective-permute-done((f32[14,8,128]{2,1,0:T(8,128)}, f32[14,8,128]{2,1,0:T(8,128)S(1)}, u32[]{:S(2)}, u32[]{:S(2)}) %collective-permute-start.3) | collective-permute-done | bytes 57376 | tf_op jit(solution)/shard_map/ppermute | solution.py:176
  21.5 3.0 %collective-permute-done.4.kl1_ref.kh1_ref = f32[14,8,128]{2,1,0:T(8,128)S(1)} collective-permute-done((f32[14,8,128]{2,1,0:T(8,128)}, f32[14,8,128]{2,1,0:T(8,128)S(1)}, u32[]{:S(2)}, u32[]{:S(2)}) %collective-permute-start.4) | collective-permute-done | bytes 57376 | tf_op jit(solution)/shard_map/ppermute | solution.py:176
  24.4 0.0 collective-permute-done.1.hi_ref
  24.4 0.0 collective-permute-done.lo_ref
  24.4 0.0 collective-permute-done.2.ml_ref.mh_ref
  24.4 0.1 collective-permute-start.5
  24.5 0.8 %rims.1.own_rim = f32[2,128,128]{2,1,0:T(8,128)S(1)} custom-call(f32[27,32,128]{2,1,0:T(8,128)S(1)} %collective-permute-done.lo_ref, f32[24,32,128]{2,1,0:T(8,128)S(1)} %collective-permute-done.1.hi_ref, f32[116,8,128]{2,1,0:T(8,128)S(1)} %collective-permute-done.2.ml_ref.mh_ref, f32[116,8,128]{2,1,0:T(8,128)S(1)} %collective-permute-done.2.ml_ref.mh_ref, ...), custom_call_target="tpu_custom_call" | custom-call | tf_op jit(solution)/shard_map/rims/pallas_call | solution.py:333
  25.3 0.6 collective-permute-start.6
  25.8 1.1 %collective-permute-done.6.other_rim = f32[2,128,128]{2,1,0:T(8,128)S(1)} collective-permute-done((f32[2,128,128]{2,1,0:T(8,128)S(1)}, f32[2,128,128]{2,1,0:T(8,128)S(1)}, u32[]{:S(2)}, u32[]{:S(2)}) %collective-permute-start.6) | collective-permute-done | bytes 131104 | tf_op jit(solution)/shard_map/ppermute | solution.py:46
  27.0 0.0 collective-permute-done.5.other_ref
  27.0 0.0 copy-done.2
  27.0 12.4 %leapfrog.1 = (f32[3,32,32,128]{3,2,1,0:T(8,128)}, f32[3,32,32,128]{3,2,1,0:T(8,128)}, f32[16,16,128]{2,1,0:T(8,128)S(1)}, f32[18,16,128]{2,1,0:T(8,128)S(1)}, f...) custom-call(f32[3,32,32,128]{3,2,1,0:T(8,128)S(1)} %copy-done, ...), custom_call_target="tpu_custom_call" | custom-call | tf_op jit(solution)/shard_map/leapfrog/pallas_call | solution.py:621
  39.4 3.6 %collective-permute-start.7 = (f32[18,16,128]{2,1,0:T(8,128)S(1)}, f32[18,16,128]{2,1,0:T(8,128)S(1)}, u32[]{:S(2)}, u32[]{:S(2)}) collective-permute-start(f32[18,16,128]{2,1,0:T(8,128)S(1)} %get-tuple-element.60.up_ref), channel_id=1, source_target_pairs={{0,4},{4,8},{8,12},{1,5},{5,9},{9,13},{2,6},{6,10},{10,14},{3,7},{... | collective-permute-start | bytes 442376 | tf_op jit(solution)/shard_map/ppermute | solution.py:42
  43.0 1.3 %collective-permute-start.8 = (f32[18,16,128]{2,1,0:T(8,128)S(1)}, f32[18,16,128]{2,1,0:T(8,128)S(1)}, u32[]{:S(2)}, u32[]{:S(2)}) collective-permute-start(f32[18,16,128]{2,1,0:T(8,128)S(1)} %get-tuple-element.61.dn_ref), channel_id=1, source_target_pairs={{4,0},{8,4},{12,8},{5,1},{9,5},{13,9},{6,2},{10,6},{14,10},{7,3},{... | collective-permute-start | bytes 442376 | tf_op jit(solution)/shard_map/ppermute | solution.py:42
  44.3 1.3 %collective-permute-start.10 = (f32[2,16,128]{2,1,0:T(8,128)S(1)}, f32[2,16,128]{2,1,0:T(8,128)S(1)}, u32[]{:S(2)}, u32[]{:S(2)}) collective-permute-start(f32[2,16,128]{2,1,0:T(8,128)S(1)} %get-tuple-element.63), channel_id=1, source_target_pairs={{8,0},{12,4},{9,1},{13,5},{10,2},{14,6},{11,3},{15,7},{24,16},{28,... | collective-permute-start | bytes 49160 | tf_op jit(solution)/shard_map/ppermute | solution.py:42
  45.6 5.6 %collective-permute-start.9 = (f32[2,16,128]{2,1,0:T(8,128)S(1)}, f32[2,16,128]{2,1,0:T(8,128)S(1)}, u32[]{:S(2)}, u32[]{:S(2)}) collective-permute-start(f32[2,16,128]{2,1,0:T(8,128)S(1)} %get-tuple-element.62), channel_id=1, source_target_pairs={{0,8},{4,12},{1,9},{5,13},{2,10},{6,14},{3,11},{7,15},{16,24},{20,... | collective-permute-start | bytes 49160 | tf_op jit(solution)/shard_map/ppermute | solution.py:42
  51.2 0.9 %collective-permute-done.10.far_high_ref = f32[2,16,128]{2,1,0:T(8,128)S(1)} collective-permute-done((f32[2,16,128]{2,1,0:T(8,128)S(1)}, f32[2,16,128]{2,1,0:T(8,128)S(1)}, u32[]{:S(2)}, u32[]{:S(2)}) %collective-permute-start.10) | collective-permute-done | bytes 16416 | tf_op jit(solution)/shard_map/ppermute | solution.py:42
  52.2 0.5 collective-permute-done.9.far_low_ref
  52.6 0.0 collective-permute-done.7.low_ref
  52.6 0.0 collective-permute-done.8.high_ref
  52.7 1.6 %collective-permute-start.11 = (f32[20,2,128]{2,1,0:T(2,128)S(1)}, f32[20,2,128]{2,1,0:T(2,128)S(1)}, u32[]{:S(2)}, u32[]{:S(2)}) collective-permute-start(f32[20,2,128]{2,1,0:T(2,128)S(1)} %get-tuple-element.64), channel_id=1, source_target_pairs={{0,2},{2,0},{1,3},{3,1},{4,6},{6,4},{5,7},{7,5},{8,10},{10,8},{9,1... | collective-permute-start | bytes 61448 | tf_op jit(solution)/shard_map/ppermute | solution.py:46
  54.2 2.3 %collective-permute-done.11 = f32[20,2,128]{2,1,0:T(2,128)S(1)} collective-permute-done((f32[20,2,128]{2,1,0:T(2,128)S(1)}, f32[20,2,128]{2,1,0:T(2,128)S(1)}, u32[]{:S(2)}, u32[]{:S(2)}) %collective-permute-start.11) | collective-permute-done | bytes 20512 | tf_op jit(solution)/shard_map/ppermute | solution.py:46
  56.6 0.1 collective-permute-start.12
  56.7 1.5 %collective-permute-done.12.zo_ref = f32[20,20,128]{2,1,0:T(8,128)S(1)} collective-permute-done((f32[20,20,128]{2,1,0:T(8,128)S(1)}, f32[20,20,128]{2,1,0:T(8,128)S(1)}, u32[]{:S(2)}, u32[]{:S(2)}) %collective-permute-start.12) | collective-permute-done | bytes 204832 | tf_op jit(solution)/shard_map/ppermute | solution.py:46
  58.2 0.9 %copy-done.8 = f32[16,16,128]{2,1,0:T(8,128)S(1)} copy-done((f32[16,16,128]{2,1,0:T(8,128)S(1)}, f32[16,16,128]{2,1,0:T(8,128)}, u32[]{:S(2)}) %copy-start.8) | copy-done | bytes 131096
  59.1 1.5 %conduction.1 = (f32[16,16,128]{2,1,0:T(8,128)}, f32[16,16,128]{2,1,0:T(8,128)S(1)}) custom-call(f32[20,20,128]{2,1,0:T(8,128)S(1)} %pad_maximum_fusion.z_ref, f32[20,20,128]{2,1,0:T(8,128)S(1)} %collective-permute-done.12.zo_ref, f32[16,16,128]{2,1,0:T(8,128)S(1)} %copy-done.6, f32[16,16,128]{2,1,0:T(8,128)S(1)} %copy-done.8, ...), custom_call_target="tpu_custom_call" | custom-call | tf_op jit(solution)/shard_map/conduction/pallas_call | solution.py:733
  60.6 4.4 %collective-permute-start.13 = (f32[16,16,128]{2,1,0:T(8,128)S(1)}, f32[16,16,128]{2,1,0:T(8,128)S(1)}, u32[]{:S(2)}, u32[]{:S(2)}) collective-permute-start(f32[16,16,128]{2,1,0:T(8,128)S(1)} %get-tuple-element.67.t_ref), channel_id=1, source_target_pairs={{0,4},{4,8},{8,12},{1,5},{5,9},{9,13},{2,6},{6,10},{10,14},{3,7},{... | collective-permute-start | bytes 393224 | tf_op jit(solution)/shard_map/ppermute | solution.py:42
  65.0 1.3 %collective-permute-start.14 = (f32[16,16,128]{2,1,0:T(8,128)S(1)}, f32[16,16,128]{2,1,0:T(8,128)S(1)}, u32[]{:S(2)}, u32[]{:S(2)}) collective-permute-start(f32[16,16,128]{2,1,0:T(8,128)S(1)} %get-tuple-element.67.t_ref), channel_id=1, source_target_pairs={{4,0},{8,4},{12,8},{5,1},{9,5},{13,9},{6,2},{10,6},{14,10},{7,3},{... | collective-permute-start | bytes 393224 | tf_op jit(solution)/shard_map/ppermute | solution.py:42
  66.3 1.7 %collective-permute-done.13.lo_ref = f32[16,16,128]{2,1,0:T(8,128)S(1)} collective-permute-done((f32[16,16,128]{2,1,0:T(8,128)S(1)}, f32[16,16,128]{2,1,0:T(8,128)S(1)}, u32[]{:S(2)}, u32[]{:S(2)}) %collective-permute-start.13) | collective-permute-done | bytes 131104 | tf_op jit(solution)/shard_map/ppermute | solution.py:42
  68.1 4.1 %collective-permute-done.14.hi_ref = f32[16,16,128]{2,1,0:T(8,128)S(1)} collective-permute-done((f32[16,16,128]{2,1,0:T(8,128)S(1)}, f32[16,16,128]{2,1,0:T(8,128)S(1)}, u32[]{:S(2)}, u32[]{:S(2)}) %collective-permute-start.14) | collective-permute-done | bytes 131104 | tf_op jit(solution)/shard_map/ppermute | solution.py:42
  72.2 1.6 %lookup.1 = f32[32,32,128]{2,1,0:T(8,128)} custom-call(s32[8,128]{1,0:T(8,128)S(1)} %copy-done.9, f32[16,16,128]{2,1,0:T(8,128)S(1)} %get-tuple-element.67.t_ref, f32[16,16,128]{2,1,0:T(8,128)S(1)} %collective-permute-done.13.lo_ref, f32[16,16,128]{2,1,0:T(8,128)S(1)} %collective-permute-done.14.hi_ref, f32[32,32,128]{2,1,0:T(8,128)S(1)} %copy-done.3), custom_call_target="tpu_custom_call" | custom-call | tf_op jit(solution)/shard_map/lookup/pallas_call | solution.py:763
  (11 shorter events, 0.1 us)
Async XLA Ops:
  0.6 17.3 %copy-start = (f32[3,32,32,128]{3,2,1,0:T(8,128)S(1)}, f32[3,32,32,128]{3,2,1,0:T(8,128)}, u32[]{:S(2)}) copy-start(f32[3,32,32,128]{3,2,1,0:T(8,128)} %e_ref.4) | copy-start | bytes 4718596
  0.6 17.3 %copy-start.3 = (f32[32,32,128]{2,1,0:T(8,128)S(1)}, f32[32,32,128]{2,1,0:T(8,128)}, u32[]{:S(2)}) copy-start(f32[32,32,128]{2,1,0:T(8,128)} %c_ref.6) | copy-start | bytes 1572868
  0.7 17.3 %copy-start.6 = (f32[16,16,128]{2,1,0:T(8,128)S(1)}, f32[16,16,128]{2,1,0:T(8,128)}, u32[]{:S(2)}) copy-start(f32[16,16,128]{2,1,0:T(8,128)} %t_ref.6) | copy-start | bytes 393220
  0.7 17.3 %copy-start.7 = (f32[16,16,128]{2,1,0:T(8,128)S(1)}, f32[16,16,128]{2,1,0:T(8,128)}, u32[]{:S(2)}) copy-start(f32[16,16,128]{2,1,0:T(8,128)} %cap_ref.4) | copy-start | bytes 393220
  4.3 20.1 %collective-permute-start.2 = (f32[116,8,128]{2,1,0:T(8,128)}, f32[116,8,128]{2,1,0:T(8,128)S(1)}, u32[]{:S(2)}, u32[]{:S(2)}) collective-permute-start(f32[116,8,128]{2,1,0:T(8,128)} %get-tuple-element.45), channel_id=1, source_target_pairs={{0,2},{2,0},{1,3},{3,1},{4,6},{6,4},{5,7},{7,5},{8,10},{10,8},{9,1... | collective-permute-start | bytes 1425416 | tf_op jit(solution)/shard_map/ppermute | solution.py:46
  7.3 17.1 %collective-permute-start = (f32[27,32,128]{2,1,0:T(8,128)}, f32[27,32,128]{2,1,0:T(8,128)S(1)}, u32[]{:S(2)}, u32[]{:S(2)}) collective-permute-start(f32[27,32,128]{2,1,0:T(8,128)} %get-tuple-element.43), channel_id=1, source_target_pairs={{0,4},{4,8},{8,12},{1,5},{5,9},{9,13},{2,6},{6,10},{10,14},{3,7},{... | collective-permute-start | bytes 1327112 | tf_op jit(solution)/shard_map/ppermute | solution.py:42
  10.8 13.6 %collective-permute-start.1 = (f32[24,32,128]{2,1,0:T(8,128)}, f32[24,32,128]{2,1,0:T(8,128)S(1)}, u32[]{:S(2)}, u32[]{:S(2)}) collective-permute-start(f32[24,32,128]{2,1,0:T(8,128)} %get-tuple-element.44), channel_id=1, source_target_pairs={{4,0},{8,4},{12,8},{5,1},{9,5},{13,9},{6,2},{10,6},{14,10},{7,3},{... | collective-permute-start | bytes 1179656 | tf_op jit(solution)/shard_map/ppermute | solution.py:42
  12.1 9.3 %collective-permute-start.3 = (f32[14,8,128]{2,1,0:T(8,128)}, f32[14,8,128]{2,1,0:T(8,128)S(1)}, u32[]{:S(2)}, u32[]{:S(2)}) collective-permute-start(f32[14,8,128]{2,1,0:T(8,128)} %get-tuple-element.46), channel_id=1, source_target_pairs={{0,6},{2,4},{4,10},{6,8},{8,14},{10,12},{1,7},{3,5},{5,11},{7,9},{... | collective-permute-start | bytes 172040 | tf_op jit(solution)/shard_map/ppermute | solution.py:176
  16.6 7.8 %collective-permute-start.4 = (f32[14,8,128]{2,1,0:T(8,128)}, f32[14,8,128]{2,1,0:T(8,128)S(1)}, u32[]{:S(2)}, u32[]{:S(2)}) collective-permute-start(f32[14,8,128]{2,1,0:T(8,128)} %get-tuple-element.47), channel_id=1, source_target_pairs={{4,2},{6,0},{8,6},{10,4},{12,10},{14,8},{5,3},{7,1},{9,7},{11,5},{... | collective-permute-start | bytes 172040 | tf_op jit(solution)/shard_map/ppermute | solution.py:176
  18.0 1.4 %copy-start.1 = (f32[3,32,32,128]{3,2,1,0:T(8,128)S(1)}, f32[3,32,32,128]{3,2,1,0:T(8,128)}, u32[]{:S(2)}) copy-start(f32[3,32,32,128]{3,2,1,0:T(8,128)} %h_ref.4) | copy-start | bytes 4718596
  20.7 6.3 %copy-start.2 = (f32[3,32,32,128]{3,2,1,0:T(8,128)S(1)}, f32[3,32,32,128]{3,2,1,0:T(8,128)}, u32[]{:S(2)}) copy-start(f32[3,32,32,128]{3,2,1,0:T(8,128)} %h_ref.4) | copy-start | bytes 4718596
  20.7 6.3 %copy-start.9 = (s32[8,128]{1,0:T(8,128)S(1)}, s32[8,128]{1,0:T(8,128)}, u32[]{:S(2)}) copy-start(s32[8,128]{1,0:T(8,128)} %get-tuple-element.37.ids_ref) | copy-start | bytes 12292
  24.4 2.5 %collective-permute-start.5 = (f32[12,128,128]{2,1,0:T(8,128)S(1)}, f32[12,128,128]{2,1,0:T(8,128)S(1)}, u32[]{:S(2)}, u32[]{:S(2)}) collective-permute-start(f32[12,128,128]{2,1,0:T(8,128)S(1)} %columns.1.own_ref), channel_id=1, source_target_pairs={{0,1},{1,0},{2,3},{3,2},{4,5},{5,4},{6,7},{7,6},{8,9},{9,8},{10,11... | collective-permute-start | bytes 2359304 | tf_op jit(solution)/shard_map/ppermute | solution.py:46
  25.3 1.7 %collective-permute-start.6 = (f32[2,128,128]{2,1,0:T(8,128)S(1)}, f32[2,128,128]{2,1,0:T(8,128)S(1)}, u32[]{:S(2)}, u32[]{:S(2)}) collective-permute-start(f32[2,128,128]{2,1,0:T(8,128)S(1)} %rims.1.own_rim), channel_id=1, source_target_pairs={{0,1},{1,0},{2,3},{3,2},{4,5},{5,4},{6,7},{7,6},{8,9},{9,8},{10,11... | collective-permute-start | bytes 393224 | tf_op jit(solution)/shard_map/ppermute | solution.py:46
  27.0 12.4 %copy-start.4 = (f32[12,128,128]{2,1,0:T(8,128)}, f32[12,128,128]{2,1,0:T(8,128)S(1)}, u32[]{:S(2)}) copy-start(f32[12,128,128]{2,1,0:T(8,128)S(1)} %collective-permute-done.5.other_ref) | copy-start | bytes 2359300
  39.4 18.7 %copy-start.5 = (f32[12,128,128]{2,1,0:T(8,128)S(1)}, f32[12,128,128]{2,1,0:T(8,128)}, u32[]{:S(2)}) copy-start(f32[12,128,128]{2,1,0:T(8,128)} %copy-done.4) | copy-start | bytes 2359300
  39.4 13.2 %collective-permute-start.7 = (f32[18,16,128]{2,1,0:T(8,128)S(1)}, f32[18,16,128]{2,1,0:T(8,128)S(1)}, u32[]{:S(2)}, u32[]{:S(2)}) collective-permute-start(f32[18,16,128]{2,1,0:T(8,128)S(1)} %get-tuple-element.60.up_ref), channel_id=1, source_target_pairs={{0,4},{4,8},{8,12},{1,5},{5,9},{9,13},{2,6},{6,10},{10,14},{3,7},{... | collective-permute-start | bytes 442376 | tf_op jit(solution)/shard_map/ppermute | solution.py:42
  43.0 9.6 %collective-permute-start.8 = (f32[18,16,128]{2,1,0:T(8,128)S(1)}, f32[18,16,128]{2,1,0:T(8,128)S(1)}, u32[]{:S(2)}, u32[]{:S(2)}) collective-permute-start(f32[18,16,128]{2,1,0:T(8,128)S(1)} %get-tuple-element.61.dn_ref), channel_id=1, source_target_pairs={{4,0},{8,4},{12,8},{5,1},{9,5},{13,9},{6,2},{10,6},{14,10},{7,3},{... | collective-permute-start | bytes 442376 | tf_op jit(solution)/shard_map/ppermute | solution.py:42
  44.3 7.8 %collective-permute-start.10 = (f32[2,16,128]{2,1,0:T(8,128)S(1)}, f32[2,16,128]{2,1,0:T(8,128)S(1)}, u32[]{:S(2)}, u32[]{:S(2)}) collective-permute-start(f32[2,16,128]{2,1,0:T(8,128)S(1)} %get-tuple-element.63), channel_id=1, source_target_pairs={{8,0},{12,4},{9,1},{13,5},{10,2},{14,6},{11,3},{15,7},{24,16},{28,... | collective-permute-start | bytes 49160 | tf_op jit(solution)/shard_map/ppermute | solution.py:42
  45.6 7.0 %collective-permute-start.9 = (f32[2,16,128]{2,1,0:T(8,128)S(1)}, f32[2,16,128]{2,1,0:T(8,128)S(1)}, u32[]{:S(2)}, u32[]{:S(2)}) collective-permute-start(f32[2,16,128]{2,1,0:T(8,128)S(1)} %get-tuple-element.62), channel_id=1, source_target_pairs={{0,8},{4,12},{1,9},{5,13},{2,10},{6,14},{3,11},{7,15},{16,24},{20,... | collective-permute-start | bytes 49160 | tf_op jit(solution)/shard_map/ppermute | solution.py:42
  52.7 3.8 %collective-permute-start.11 = (f32[20,2,128]{2,1,0:T(2,128)S(1)}, f32[20,2,128]{2,1,0:T(2,128)S(1)}, u32[]{:S(2)}, u32[]{:S(2)}) collective-permute-start(f32[20,2,128]{2,1,0:T(2,128)S(1)} %get-tuple-element.64), channel_id=1, source_target_pairs={{0,2},{2,0},{1,3},{3,1},{4,6},{6,4},{5,7},{7,5},{8,10},{10,8},{9,1... | collective-permute-start | bytes 61448 | tf_op jit(solution)/shard_map/ppermute | solution.py:46
  56.6 1.6 %collective-permute-start.12 = (f32[20,20,128]{2,1,0:T(8,128)S(1)}, f32[20,20,128]{2,1,0:T(8,128)S(1)}, u32[]{:S(2)}, u32[]{:S(2)}) collective-permute-start(f32[20,20,128]{2,1,0:T(8,128)S(1)} %pad_maximum_fusion.z_ref), channel_id=1, source_target_pairs={{0,1},{1,0},{2,3},{3,2},{4,5},{5,4},{6,7},{7,6},{8,9},{9,8},{10,11... | collective-permute-start | bytes 614408 | tf_op jit(solution)/shard_map/ppermute | solution.py:46
  58.2 0.9 %copy-start.8 = (f32[16,16,128]{2,1,0:T(8,128)S(1)}, f32[16,16,128]{2,1,0:T(8,128)}, u32[]{:S(2)}) copy-start(f32[16,16,128]{2,1,0:T(8,128)} %cap_ref.4) | copy-start | bytes 393220
  60.6 7.5 %collective-permute-start.13 = (f32[16,16,128]{2,1,0:T(8,128)S(1)}, f32[16,16,128]{2,1,0:T(8,128)S(1)}, u32[]{:S(2)}, u32[]{:S(2)}) collective-permute-start(f32[16,16,128]{2,1,0:T(8,128)S(1)} %get-tuple-element.67.t_ref), channel_id=1, source_target_pairs={{0,4},{4,8},{8,12},{1,5},{5,9},{9,13},{2,6},{6,10},{10,14},{3,7},{... | collective-permute-start | bytes 393224 | tf_op jit(solution)/shard_map/ppermute | solution.py:42
  65.0 7.2 %collective-permute-start.14 = (f32[16,16,128]{2,1,0:T(8,128)S(1)}, f32[16,16,128]{2,1,0:T(8,128)S(1)}, u32[]{:S(2)}, u32[]{:S(2)}) collective-permute-start(f32[16,16,128]{2,1,0:T(8,128)S(1)} %get-tuple-element.67.t_ref), channel_id=1, source_target_pairs={{4,0},{8,4},{12,8},{5,1},{9,5},{13,9},{6,2},{10,6},{14,10},{7,3},{... | collective-permute-start | bytes 393224 | tf_op jit(solution)/shard_map/ppermute | solution.py:42

commit v4 on v3

--- a/solution.py
+++ b/solution.py
@@ -518,22 +518,26 @@
         hs[c, i, pl.ds(TOP, 8), :] = value[:8] * in_y[:8]
         hs[c, i, pl.ds(TOP + 8, y_ext - 8), :] = value[8:]
 
-    def main_h(step, i):
+    def main_h(step, i, low_half):
         e0, e1, e2 = es[0, i, centre, :], es[1, i, centre, :], es[2, i, centre, :]
-        beyond = border(i, 2 * step)
+        if low_half:
+            beyond, beyond1 = border(i, 2 * step), border(i, 2 * step + 1)
+        else:
+            beyond, beyond1 = 0.0, 0.0
         e0x = jnp.where(is_last, beyond, pltpu.roll(e0, lanes - 1, 1))
-        beyond = border(i, 2 * step + 1)
-        e1x = jnp.where(is_last, beyond, pltpu.roll(e1, lanes - 1, 1))
+        e1x = jnp.where(is_last, beyond1, pltpu.roll(e1, lanes - 1, 1))
         put_h(0, i, (es[2, i, above, :] - e2) - (e1x - e1))
         put_h(1, i, (e0x - e0) - (es[2, i + 1, centre, :] - e2))
         put_h(2, i, (es[1, i + 1, centre, :] - e1) - (es[0, i, above, :] - e0))
 
-    def main_e(step, i):
+    def main_e(step, i, low_half):
         h0, h1, h2 = hs[0, i, centre, :], hs[1, i, centre, :], hs[2, i, centre, :]
-        beyond = border(i, 8 + 2 * step)
+        if low_half:
+            beyond, beyond1 = 0.0, 0.0
+        else:
+            beyond, beyond1 = border(i, 8 + 2 * step), border(i, 8 + 2 * step - 1)
         h0x = jnp.where(is_first, beyond, pltpu.roll(h0, 1, 1))
-        beyond = border(i, 8 + 2 * step - 1)
-        h1x = jnp.where(is_first, beyond, pltpu.roll(h1, 1, 1))
+        h1x = jnp.where(is_first, beyond1, pltpu.roll(h1, 1, 1))
         keep, gain = ce[i, centre, :], ch[i]
         e0, e1, e2 = es[0, i, centre, :], es[1, i, centre, :], es[2, i, centre, :]
         n0 = keep * e0 + gain * ((h2 - hs[2, i, below, :]) - (h1 - h1x))
@@ -548,11 +552,15 @@
 
     heat[...] = jnp.zeros_like(heat)
 
-    for step in range(STEPS):
-        for i in range(step, s_ext - 1 - step):
-            main_h(step, i)
-        for i in range(step + 1, s_ext - 1 - step):
-            main_e(step, i)
+    for low_half in (True, False):
+
+        @pl.when((comp == 0) == low_half)
+        def _(low_half=low_half):
+            for step in range(STEPS):
+                for i in range(step, s_ext - 1 - step):
+                    main_h(step, i, low_half)
+                for i in range(step + 1, s_ext - 1 - step):
+                    main_e(step, i, low_half)
 
     ys = pl.ds(TOP + W, y_dev)
     copies = []

time: 74.2 us -> 73.9 us (level)
  no operation moved by 1% of the time
where the time goes in v4:
time: 73.9 us; the launch traced here: 73.5 us
  starting transfers between devices  33.3 us (45%)
  Pallas kernels  20.9 us (28%)
  waiting for transfers between devices  15.9 us (22%)
  local copies, waits for them, and re-layouts  2.35 us (3%)
  between operations  0.9 us (1%)
    ppermute x8, starting transfers between devices, passed_along(): return lax.ppermute(array, axis, pairs)  22.2 us
    pallas_call x1, Pallas kernels, main_call(): pl.pallas_call(functools.partial(main_kernel, lax.axis_size('slab'), lax....  12.2 us
    ppermute x8, waiting for transfers between devices, passed_along(): return lax.ppermute(array, axis, pairs)  7.29 us
    ppermute x2, starting transfers between devices, along_both(): return lax.ppermute(array, ('slab', 'sub'), pairs)  5.81 us
    ppermute x5, starting transfers between devices, swapped(): return lax.ppermute(array, axis, [(0, 1), (1, 0)])  5.26 us
    ppermute x5, waiting for transfers between devices, swapped(): return lax.ppermute(array, axis, [(0, 1), (1, 0)])  4.94 us
    ppermute x2, waiting for transfers between devices, along_both(): return lax.ppermute(array, ('slab', 'sub'), pairs)  3.72 us
    pallas_call x1, Pallas kernels, halo_exchange(): pl.pallas_call(functools.partial(pack_kernel, edges), in_specs=[pl.BlockS...  3.63 us
  transfers between devices with their start and end apart: 15, of which 9 were waited for; matrix products, arithmetic and copies ran while one was open for 0% of the time, Pallas kernels for 3%

profile of v4, /device:TPU:0, one launch (start us, length us, event | category | flops | bytes accessed | tf_op | source)
XLA Modules:
  0.0 73.5 jit_solution(15204375941007466468)
XLA Ops:
  0.6 0.0 copy-start
  0.7 0.0 copy-start.7
  0.7 3.6 %pack.1 = (s32[8,128]{1,0:T(8,128)}, f32[27,32,128]{2,1,0:T(8,128)}, f32[24,32,128]{2,1,0:T(8,128)}, f32[116,8,128]{2,1,0:T(8,128)}, f32[14,8,128]{2,1,0:T(8,128)}, /*index=5*/f32[14,8,128]{2,1,0:T(8,128)}) custom-call(f32[3,32,32,128]{3,2,1,0:T(8,128)} %e_ref.4, f32[3,32,32,128]{3,2,1,0:T(8,128)} %h_ref.4, f32[32,32,128]{2,1,0:T(8,128)} %c_ref.6, ...), custom_call_target="tpu_custom_call" | custom-call | tf_op jit(solution)/shard_map/pack/pallas_call | solution.py:188
  4.3 3.0 %collective-permute-start.2 = (f32[116,8,128]{2,1,0:T(8,128)}, f32[116,8,128]{2,1,0:T(8,128)S(1)}, u32[]{:S(2)}, u32[]{:S(2)}) collective-permute-start(f32[116,8,128]{2,1,0:T(8,128)} %get-tuple-element.45), channel_id=1, source_target_pairs={{0,2},{2,0},{1,3},{3,1},{4,6},{6,4},{5,7},{7,5},{8,10},{10,8},{9,1... | collective-permute-start | bytes 1425416 | tf_op jit(solution)/shard_map/ppermute | solution.py:46
  7.3 3.5 %collective-permute-start = (f32[27,32,128]{2,1,0:T(8,128)}, f32[27,32,128]{2,1,0:T(8,128)S(1)}, u32[]{:S(2)}, u32[]{:S(2)}) collective-permute-start(f32[27,32,128]{2,1,0:T(8,128)} %get-tuple-element.43), channel_id=1, source_target_pairs={{0,4},{4,8},{8,12},{1,5},{5,9},{9,13},{2,6},{6,10},{10,14},{3,7},{... | collective-permute-start | bytes 1327112 | tf_op jit(solution)/shard_map/ppermute | solution.py:42
  10.8 1.3 %collective-permute-start.1 = (f32[24,32,128]{2,1,0:T(8,128)}, f32[24,32,128]{2,1,0:T(8,128)S(1)}, u32[]{:S(2)}, u32[]{:S(2)}) collective-permute-start(f32[24,32,128]{2,1,0:T(8,128)} %get-tuple-element.44), channel_id=1, source_target_pairs={{4,0},{8,4},{12,8},{5,1},{9,5},{13,9},{6,2},{10,6},{14,10},{7,3},{... | collective-permute-start | bytes 1179656 | tf_op jit(solution)/shard_map/ppermute | solution.py:42
  12.1 4.5 %collective-permute-start.3 = (f32[14,8,128]{2,1,0:T(8,128)}, f32[14,8,128]{2,1,0:T(8,128)S(1)}, u32[]{:S(2)}, u32[]{:S(2)}) collective-permute-start(f32[14,8,128]{2,1,0:T(8,128)} %get-tuple-element.46), channel_id=1, source_target_pairs={{0,6},{2,4},{4,10},{6,8},{8,14},{10,12},{1,7},{3,5},{5,11},{7,9},{... | collective-permute-start | bytes 172040 | tf_op jit(solution)/shard_map/ppermute | solution.py:176
  16.6 1.3 %collective-permute-start.4 = (f32[14,8,128]{2,1,0:T(8,128)}, f32[14,8,128]{2,1,0:T(8,128)S(1)}, u32[]{:S(2)}, u32[]{:S(2)}) collective-permute-start(f32[14,8,128]{2,1,0:T(8,128)} %get-tuple-element.47), channel_id=1, source_target_pairs={{4,2},{6,0},{8,6},{10,4},{12,10},{14,8},{5,3},{7,1},{9,7},{11,5},{... | collective-permute-start | bytes 172040 | tf_op jit(solution)/shard_map/ppermute | solution.py:176
  17.9 0.0 copy-done
  18.0 0.0 copy-done.3
  18.0 0.0 copy-done.6
  18.0 0.0 copy-done.7
  18.0 0.0 copy-start.1
  18.0 1.4 %copy-done.1 = f32[3,32,32,128]{3,2,1,0:T(8,128)S(1)} copy-done((f32[3,32,32,128]{3,2,1,0:T(8,128)S(1)}, f32[3,32,32,128]{3,2,1,0:T(8,128)}, u32[]{:S(2)}) %copy-start.1) | copy-done | bytes 1572888
  19.4 1.3 %columns.1.own_ref = f32[12,128,128]{2,1,0:T(8,128)S(1)} custom-call(f32[3,32,32,128]{3,2,1,0:T(8,128)S(1)} %copy-done, f32[3,32,32,128]{3,2,1,0:T(8,128)S(1)} %copy-done.1, f32[32,32,128]{2,1,0:T(8,128)S(1)} %copy-done.3, f32[16,16,128]{2,1,0:T(8,128)S(1)} %copy-done.6, f32[16,16,128]{2,1,0:T(8,128)S(1)} %copy-done.7), custom_call_target="tpu_custom_call" | custom-call | flops 10000000 | bytes 8000000 | tf_op jit(solution)/shard_map/columns/pallas_call | solution.py:321
  20.7 0.0 copy-start.2
  20.7 0.0 copy-start.9
  20.7 0.8 %collective-permute-done.3.kl0_ref.kh0_ref = f32[14,8,128]{2,1,0:T(8,128)S(1)} collective-permute-done((f32[14,8,128]{2,1,0:T(8,128)}, f32[14,8,128]{2,1,0:T(8,128)S(1)}, u32[]{:S(2)}, u32[]{:S(2)}) %collective-permute-start.3) | collective-permute-done | bytes 57376 | tf_op jit(solution)/shard_map/ppermute | solution.py:176
  21.5 3.0 %collective-permute-done.4.kl1_ref.kh1_ref = f32[14,8,128]{2,1,0:T(8,128)S(1)} collective-permute-done((f32[14,8,128]{2,1,0:T(8,128)}, f32[14,8,128]{2,1,0:T(8,128)S(1)}, u32[]{:S(2)}, u32[]{:S(2)}) %collective-permute-start.4) | collective-permute-done | bytes 57376 | tf_op jit(solution)/shard_map/ppermute | solution.py:176
  24.4 0.0 collective-permute-done.1.hi_ref
  24.4 0.0 collective-permute-done.lo_ref
  24.4 0.0 collective-permute-done.2.ml_ref.mh_ref
  24.4 0.1 collective-permute-start.5
  24.5 0.8 %rims.1.own_rim = f32[2,128,128]{2,1,0:T(8,128)S(1)} custom-call(f32[27,32,128]{2,1,0:T(8,128)S(1)} %collective-permute-done.lo_ref, f32[24,32,128]{2,1,0:T(8,128)S(1)} %collective-permute-done.1.hi_ref, f32[116,8,128]{2,1,0:T(8,128)S(1)} %collective-permute-done.2.ml_ref.mh_ref, f32[116,8,128]{2,1,0:T(8,128)S(1)} %collective-permute-done.2.ml_ref.mh_ref, ...), custom_call_target="tpu_custom_call" | custom-call | tf_op jit(solution)/shard_map/rims/pallas_call | solution.py:333
  25.3 0.6 collective-permute-start.6
  25.8 1.1 %collective-permute-done.6.other_rim = f32[2,128,128]{2,1,0:T(8,128)S(1)} collective-permute-done((f32[2,128,128]{2,1,0:T(8,128)S(1)}, f32[2,128,128]{2,1,0:T(8,128)S(1)}, u32[]{:S(2)}, u32[]{:S(2)}) %collective-permute-start.6) | collective-permute-done | bytes 131104 | tf_op jit(solution)/shard_map/ppermute | solution.py:46
  27.0 0.0 collective-permute-done.5.other_ref
  27.0 0.0 copy-done.2
  27.0 12.2 %leapfrog.1 = (f32[3,32,32,128]{3,2,1,0:T(8,128)}, f32[3,32,32,128]{3,2,1,0:T(8,128)}, f32[16,16,128]{2,1,0:T(8,128)S(1)}, f32[18,16,128]{2,1,0:T(8,128)S(1)}, f...) custom-call(f32[3,32,32,128]{3,2,1,0:T(8,128)S(1)} %copy-done, ...), custom_call_target="tpu_custom_call" | custom-call | tf_op jit(solution)/shard_map/leapfrog/pallas_call | solution.py:629
  39.2 3.6 %collective-permute-start.7 = (f32[18,16,128]{2,1,0:T(8,128)S(1)}, f32[18,16,128]{2,1,0:T(8,128)S(1)}, u32[]{:S(2)}, u32[]{:S(2)}) collective-permute-start(f32[18,16,128]{2,1,0:T(8,128)S(1)} %get-tuple-element.60.up_ref), channel_id=1, source_target_pairs={{0,4},{4,8},{8,12},{1,5},{5,9},{9,13},{2,6},{6,10},{10,14},{3,7},{... | collective-permute-start | bytes 442376 | tf_op jit(solution)/shard_map/ppermute | solution.py:42
  42.8 1.3 %collective-permute-start.8 = (f32[18,16,128]{2,1,0:T(8,128)S(1)}, f32[18,16,128]{2,1,0:T(8,128)S(1)}, u32[]{:S(2)}, u32[]{:S(2)}) collective-permute-start(f32[18,16,128]{2,1,0:T(8,128)S(1)} %get-tuple-element.61.dn_ref), channel_id=1, source_target_pairs={{4,0},{8,4},{12,8},{5,1},{9,5},{13,9},{6,2},{10,6},{14,10},{7,3},{... | collective-permute-start | bytes 442376 | tf_op jit(solution)/shard_map/ppermute | solution.py:42
  44.1 1.3 %collective-permute-start.10 = (f32[2,16,128]{2,1,0:T(8,128)S(1)}, f32[2,16,128]{2,1,0:T(8,128)S(1)}, u32[]{:S(2)}, u32[]{:S(2)}) collective-permute-start(f32[2,16,128]{2,1,0:T(8,128)S(1)} %get-tuple-element.63), channel_id=1, source_target_pairs={{8,0},{12,4},{9,1},{13,5},{10,2},{14,6},{11,3},{15,7},{24,16},{28,... | collective-permute-start | bytes 49160 | tf_op jit(solution)/shard_map/ppermute | solution.py:42
  45.4 5.6 %collective-permute-start.9 = (f32[2,16,128]{2,1,0:T(8,128)S(1)}, f32[2,16,128]{2,1,0:T(8,128)S(1)}, u32[]{:S(2)}, u32[]{:S(2)}) collective-permute-start(f32[2,16,128]{2,1,0:T(8,128)S(1)} %get-tuple-element.62), channel_id=1, source_target_pairs={{0,8},{4,12},{1,9},{5,13},{2,10},{6,14},{3,11},{7,15},{16,24},{20,... | collective-permute-start | bytes 49160 | tf_op jit(solution)/shard_map/ppermute | solution.py:42
  51.0 0.2 collective-permute-done.10.far_high_ref
  51.2 1.2 %collective-permute-done.9.far_low_ref = f32[2,16,128]{2,1,0:T(8,128)S(1)} collective-permute-done((f32[2,16,128]{2,1,0:T(8,128)S(1)}, f32[2,16,128]{2,1,0:T(8,128)S(1)}, u32[]{:S(2)}, u32[]{:S(2)}) %collective-permute-start.9) | collective-permute-done | bytes 16416 | tf_op jit(solution)/shard_map/ppermute | solution.py:42
  52.4 0.0 collective-permute-done.7.low_ref
  52.4 0.0 collective-permute-done.8.high_ref
  52.4 1.6 %collective-permute-start.11 = (f32[20,2,128]{2,1,0:T(2,128)S(1)}, f32[20,2,128]{2,1,0:T(2,128)S(1)}, u32[]{:S(2)}, u32[]{:S(2)}) collective-permute-start(f32[20,2,128]{2,1,0:T(2,128)S(1)} %get-tuple-element.64), channel_id=1, source_target_pairs={{0,2},{2,0},{1,3},{3,1},{4,6},{6,4},{5,7},{7,5},{8,10},{10,8},{9,1... | collective-permute-start | bytes 61448 | tf_op jit(solution)/shard_map/ppermute | solution.py:46
  54.0 2.3 %collective-permute-done.11 = f32[20,2,128]{2,1,0:T(2,128)S(1)} collective-permute-done((f32[20,2,128]{2,1,0:T(2,128)S(1)}, f32[20,2,128]{2,1,0:T(2,128)S(1)}, u32[]{:S(2)}, u32[]{:S(2)}) %collective-permute-start.11) | collective-permute-done | bytes 20512 | tf_op jit(solution)/shard_map/ppermute | solution.py:46
  56.4 0.1 collective-permute-start.12
  56.4 1.5 %collective-permute-done.12.zo_ref = f32[20,20,128]{2,1,0:T(8,128)S(1)} collective-permute-done((f32[20,20,128]{2,1,0:T(8,128)S(1)}, f32[20,20,128]{2,1,0:T(8,128)S(1)}, u32[]{:S(2)}, u32[]{:S(2)}) %collective-permute-start.12) | collective-permute-done | bytes 204832 | tf_op jit(solution)/shard_map/ppermute | solution.py:46
  57.9 0.9 %copy-done.8 = f32[16,16,128]{2,1,0:T(8,128)S(1)} copy-done((f32[16,16,128]{2,1,0:T(8,128)S(1)}, f32[16,16,128]{2,1,0:T(8,128)}, u32[]{:S(2)}) %copy-start.8) | copy-done | bytes 131096
  58.8 1.5 %conduction.1 = (f32[16,16,128]{2,1,0:T(8,128)}, f32[16,16,128]{2,1,0:T(8,128)S(1)}) custom-call(f32[20,20,128]{2,1,0:T(8,128)S(1)} %pad_maximum_fusion.z_ref, f32[20,20,128]{2,1,0:T(8,128)S(1)} %collective-permute-done.12.zo_ref, f32[16,16,128]{2,1,0:T(8,128)S(1)} %copy-done.6, f32[16,16,128]{2,1,0:T(8,128)S(1)} %copy-done.8, ...), custom_call_target="tpu_custom_call" | custom-call | tf_op jit(solution)/shard_map/conduction/pallas_call | solution.py:741
  60.3 4.4 %collective-permute-start.13 = (f32[16,16,128]{2,1,0:T(8,128)S(1)}, f32[16,16,128]{2,1,0:T(8,128)S(1)}, u32[]{:S(2)}, u32[]{:S(2)}) collective-permute-start(f32[16,16,128]{2,1,0:T(8,128)S(1)} %get-tuple-element.67.t_ref), channel_id=1, source_target_pairs={{0,4},{4,8},{8,12},{1,5},{5,9},{9,13},{2,6},{6,10},{10,14},{3,7},{... | collective-permute-start | bytes 393224 | tf_op jit(solution)/shard_map/ppermute | solution.py:42
  64.8 1.3 %collective-permute-start.14 = (f32[16,16,128]{2,1,0:T(8,128)S(1)}, f32[16,16,128]{2,1,0:T(8,128)S(1)}, u32[]{:S(2)}, u32[]{:S(2)}) collective-permute-start(f32[16,16,128]{2,1,0:T(8,128)S(1)} %get-tuple-element.67.t_ref), channel_id=1, source_target_pairs={{4,0},{8,4},{12,8},{5,1},{9,5},{13,9},{6,2},{10,6},{14,10},{7,3},{... | collective-permute-start | bytes 393224 | tf_op jit(solution)/shard_map/ppermute | solution.py:42
  66.1 1.7 %collective-permute-done.13.lo_ref = f32[16,16,128]{2,1,0:T(8,128)S(1)} collective-permute-done((f32[16,16,128]{2,1,0:T(8,128)S(1)}, f32[16,16,128]{2,1,0:T(8,128)S(1)}, u32[]{:S(2)}, u32[]{:S(2)}) %collective-permute-start.13) | collective-permute-done | bytes 131104 | tf_op jit(solution)/shard_map/ppermute | solution.py:42
  67.8 4.1 %collective-permute-done.14.hi_ref = f32[16,16,128]{2,1,0:T(8,128)S(1)} collective-permute-done((f32[16,16,128]{2,1,0:T(8,128)S(1)}, f32[16,16,128]{2,1,0:T(8,128)S(1)}, u32[]{:S(2)}, u32[]{:S(2)}) %collective-permute-start.14) | collective-permute-done | bytes 131104 | tf_op jit(solution)/shard_map/ppermute | solution.py:42
  71.9 1.6 %lookup.1 = f32[32,32,128]{2,1,0:T(8,128)} custom-call(s32[8,128]{1,0:T(8,128)S(1)} %copy-done.9, f32[16,16,128]{2,1,0:T(8,128)S(1)} %get-tuple-element.67.t_ref, f32[16,16,128]{2,1,0:T(8,128)S(1)} %collective-permute-done.13.lo_ref, f32[16,16,128]{2,1,0:T(8,128)S(1)} %collective-permute-done.14.hi_ref, f32[32,32,128]{2,1,0:T(8,128)S(1)} %copy-done.3), custom_call_target="tpu_custom_call" | custom-call | tf_op jit(solution)/shard_map/lookup/pallas_call | solution.py:771
  (11 shorter events, 0.1 us)
Async XLA Ops:
  0.6 17.3 %copy-start = (f32[3,32,32,128]{3,2,1,0:T(8,128)S(1)}, f32[3,32,32,128]{3,2,1,0:T(8,128)}, u32[]{:S(2)}) copy-start(f32[3,32,32,128]{3,2,1,0:T(8,128)} %e_ref.4) | copy-start | bytes 4718596
  0.6 17.3 %copy-start.3 = (f32[32,32,128]{2,1,0:T(8,128)S(1)}, f32[32,32,128]{2,1,0:T(8,128)}, u32[]{:S(2)}) copy-start(f32[32,32,128]{2,1,0:T(8,128)} %c_ref.6) | copy-start | bytes 1572868
  0.7 17.3 %copy-start.6 = (f32[16,16,128]{2,1,0:T(8,128)S(1)}, f32[16,16,128]{2,1,0:T(8,128)}, u32[]{:S(2)}) copy-start(f32[16,16,128]{2,1,0:T(8,128)} %t_ref.6) | copy-start | bytes 393220
  0.7 17.3 %copy-start.7 = (f32[16,16,128]{2,1,0:T(8,128)S(1)}, f32[16,16,128]{2,1,0:T(8,128)}, u32[]{:S(2)}) copy-start(f32[16,16,128]{2,1,0:T(8,128)} %cap_ref.4) | copy-start | bytes 393220
  4.3 20.1 %collective-permute-start.2 = (f32[116,8,128]{2,1,0:T(8,128)}, f32[116,8,128]{2,1,0:T(8,128)S(1)}, u32[]{:S(2)}, u32[]{:S(2)}) collective-permute-start(f32[116,8,128]{2,1,0:T(8,128)} %get-tuple-element.45), channel_id=1, source_target_pairs={{0,2},{2,0},{1,3},{3,1},{4,6},{6,4},{5,7},{7,5},{8,10},{10,8},{9,1... | collective-permute-start | bytes 1425416 | tf_op jit(solution)/shard_map/ppermute | solution.py:46
  7.3 17.1 %collective-permute-start = (f32[27,32,128]{2,1,0:T(8,128)}, f32[27,32,128]{2,1,0:T(8,128)S(1)}, u32[]{:S(2)}, u32[]{:S(2)}) collective-permute-start(f32[27,32,128]{2,1,0:T(8,128)} %get-tuple-element.43), channel_id=1, source_target_pairs={{0,4},{4,8},{8,12},{1,5},{5,9},{9,13},{2,6},{6,10},{10,14},{3,7},{... | collective-permute-start | bytes 1327112 | tf_op jit(solution)/shard_map/ppermute | solution.py:42
  10.8 13.6 %collective-permute-start.1 = (f32[24,32,128]{2,1,0:T(8,128)}, f32[24,32,128]{2,1,0:T(8,128)S(1)}, u32[]{:S(2)}, u32[]{:S(2)}) collective-permute-start(f32[24,32,128]{2,1,0:T(8,128)} %get-tuple-element.44), channel_id=1, source_target_pairs={{4,0},{8,4},{12,8},{5,1},{9,5},{13,9},{6,2},{10,6},{14,10},{7,3},{... | collective-permute-start | bytes 1179656 | tf_op jit(solution)/shard_map/ppermute | solution.py:42
  12.1 9.3 %collective-permute-start.3 = (f32[14,8,128]{2,1,0:T(8,128)}, f32[14,8,128]{2,1,0:T(8,128)S(1)}, u32[]{:S(2)}, u32[]{:S(2)}) collective-permute-start(f32[14,8,128]{2,1,0:T(8,128)} %get-tuple-element.46), channel_id=1, source_target_pairs={{0,6},{2,4},{4,10},{6,8},{8,14},{10,12},{1,7},{3,5},{5,11},{7,9},{... | collective-permute-start | bytes 172040 | tf_op jit(solution)/shard_map/ppermute | solution.py:176
  16.6 7.8 %collective-permute-start.4 = (f32[14,8,128]{2,1,0:T(8,128)}, f32[14,8,128]{2,1,0:T(8,128)S(1)}, u32[]{:S(2)}, u32[]{:S(2)}) collective-permute-start(f32[14,8,128]{2,1,0:T(8,128)} %get-tuple-element.47), channel_id=1, source_target_pairs={{4,2},{6,0},{8,6},{10,4},{12,10},{14,8},{5,3},{7,1},{9,7},{11,5},{... | collective-permute-start | bytes 172040 | tf_op jit(solution)/shard_map/ppermute | solution.py:176
  18.0 1.4 %copy-start.1 = (f32[3,32,32,128]{3,2,1,0:T(8,128)S(1)}, f32[3,32,32,128]{3,2,1,0:T(8,128)}, u32[]{:S(2)}) copy-start(f32[3,32,32,128]{3,2,1,0:T(8,128)} %h_ref.4) | copy-start | bytes 4718596
  20.7 6.3 %copy-start.2 = (f32[3,32,32,128]{3,2,1,0:T(8,128)S(1)}, f32[3,32,32,128]{3,2,1,0:T(8,128)}, u32[]{:S(2)}) copy-start(f32[3,32,32,128]{3,2,1,0:T(8,128)} %h_ref.4) | copy-start | bytes 4718596
  20.7 6.3 %copy-start.9 = (s32[8,128]{1,0:T(8,128)S(1)}, s32[8,128]{1,0:T(8,128)}, u32[]{:S(2)}) copy-start(s32[8,128]{1,0:T(8,128)} %get-tuple-element.37.ids_ref) | copy-start | bytes 12292
  24.4 2.5 %collective-permute-start.5 = (f32[12,128,128]{2,1,0:T(8,128)S(1)}, f32[12,128,128]{2,1,0:T(8,128)S(1)}, u32[]{:S(2)}, u32[]{:S(2)}) collective-permute-start(f32[12,128,128]{2,1,0:T(8,128)S(1)} %columns.1.own_ref), channel_id=1, source_target_pairs={{0,1},{1,0},{2,3},{3,2},{4,5},{5,4},{6,7},{7,6},{8,9},{9,8},{10,11... | collective-permute-start | bytes 2359304 | tf_op jit(solution)/shard_map/ppermute | solution.py:46
  25.3 1.7 %collective-permute-start.6 = (f32[2,128,128]{2,1,0:T(8,128)S(1)}, f32[2,128,128]{2,1,0:T(8,128)S(1)}, u32[]{:S(2)}, u32[]{:S(2)}) collective-permute-start(f32[2,128,128]{2,1,0:T(8,128)S(1)} %rims.1.own_rim), channel_id=1, source_target_pairs={{0,1},{1,0},{2,3},{3,2},{4,5},{5,4},{6,7},{7,6},{8,9},{9,8},{10,11... | collective-permute-start | bytes 393224 | tf_op jit(solution)/shard_map/ppermute | solution.py:46
  27.0 12.2 %copy-start.4 = (f32[12,128,128]{2,1,0:T(8,128)}, f32[12,128,128]{2,1,0:T(8,128)S(1)}, u32[]{:S(2)}) copy-start(f32[12,128,128]{2,1,0:T(8,128)S(1)} %collective-permute-done.5.other_ref) | copy-start | bytes 2359300
  39.2 18.7 %copy-start.5 = (f32[12,128,128]{2,1,0:T(8,128)S(1)}, f32[12,128,128]{2,1,0:T(8,128)}, u32[]{:S(2)}) copy-start(f32[12,128,128]{2,1,0:T(8,128)} %copy-done.4) | copy-start | bytes 2359300
  39.2 13.2 %collective-permute-start.7 = (f32[18,16,128]{2,1,0:T(8,128)S(1)}, f32[18,16,128]{2,1,0:T(8,128)S(1)}, u32[]{:S(2)}, u32[]{:S(2)}) collective-permute-start(f32[18,16,128]{2,1,0:T(8,128)S(1)} %get-tuple-element.60.up_ref), channel_id=1, source_target_pairs={{0,4},{4,8},{8,12},{1,5},{5,9},{9,13},{2,6},{6,10},{10,14},{3,7},{... | collective-permute-start | bytes 442376 | tf_op jit(solution)/shard_map/ppermute | solution.py:42
  42.8 9.6 %collective-permute-start.8 = (f32[18,16,128]{2,1,0:T(8,128)S(1)}, f32[18,16,128]{2,1,0:T(8,128)S(1)}, u32[]{:S(2)}, u32[]{:S(2)}) collective-permute-start(f32[18,16,128]{2,1,0:T(8,128)S(1)} %get-tuple-element.61.dn_ref), channel_id=1, source_target_pairs={{4,0},{8,4},{12,8},{5,1},{9,5},{13,9},{6,2},{10,6},{14,10},{7,3},{... | collective-permute-start | bytes 442376 | tf_op jit(solution)/shard_map/ppermute | solution.py:42
  44.1 7.1 %collective-permute-start.10 = (f32[2,16,128]{2,1,0:T(8,128)S(1)}, f32[2,16,128]{2,1,0:T(8,128)S(1)}, u32[]{:S(2)}, u32[]{:S(2)}) collective-permute-start(f32[2,16,128]{2,1,0:T(8,128)S(1)} %get-tuple-element.63), channel_id=1, source_target_pairs={{8,0},{12,4},{9,1},{13,5},{10,2},{14,6},{11,3},{15,7},{24,16},{28,... | collective-permute-start | bytes 49160 | tf_op jit(solution)/shard_map/ppermute | solution.py:42
  45.4 7.0 %collective-permute-start.9 = (f32[2,16,128]{2,1,0:T(8,128)S(1)}, f32[2,16,128]{2,1,0:T(8,128)S(1)}, u32[]{:S(2)}, u32[]{:S(2)}) collective-permute-start(f32[2,16,128]{2,1,0:T(8,128)S(1)} %get-tuple-element.62), channel_id=1, source_target_pairs={{0,8},{4,12},{1,9},{5,13},{2,10},{6,14},{3,11},{7,15},{16,24},{20,... | collective-permute-start | bytes 49160 | tf_op jit(solution)/shard_map/ppermute | solution.py:42
  52.4 3.8 %collective-permute-start.11 = (f32[20,2,128]{2,1,0:T(2,128)S(1)}, f32[20,2,128]{2,1,0:T(2,128)S(1)}, u32[]{:S(2)}, u32[]{:S(2)}) collective-permute-start(f32[20,2,128]{2,1,0:T(2,128)S(1)} %get-tuple-element.64), channel_id=1, source_target_pairs={{0,2},{2,0},{1,3},{3,1},{4,6},{6,4},{5,7},{7,5},{8,10},{10,8},{9,1... | collective-permute-start | bytes 61448 | tf_op jit(solution)/shard_map/ppermute | solution.py:46
  56.4 1.6 %collective-permute-start.12 = (f32[20,20,128]{2,1,0:T(8,128)S(1)}, f32[20,20,128]{2,1,0:T(8,128)S(1)}, u32[]{:S(2)}, u32[]{:S(2)}) collective-permute-start(f32[20,20,128]{2,1,0:T(8,128)S(1)} %pad_maximum_fusion.z_ref), channel_id=1, source_target_pairs={{0,1},{1,0},{2,3},{3,2},{4,5},{5,4},{6,7},{7,6},{8,9},{9,8},{10,11... | collective-permute-start | bytes 614408 | tf_op jit(solution)/shard_map/ppermute | solution.py:46
  57.9 0.9 %copy-start.8 = (f32[16,16,128]{2,1,0:T(8,128)S(1)}, f32[16,16,128]{2,1,0:T(8,128)}, u32[]{:S(2)}) copy-start(f32[16,16,128]{2,1,0:T(8,128)} %cap_ref.4) | copy-start | bytes 393220
  60.3 7.5 %collective-permute-start.13 = (f32[16,16,128]{2,1,0:T(8,128)S(1)}, f32[16,16,128]{2,1,0:T(8,128)S(1)}, u32[]{:S(2)}, u32[]{:S(2)}) collective-permute-start(f32[16,16,128]{2,1,0:T(8,128)S(1)} %get-tuple-element.67.t_ref), channel_id=1, source_target_pairs={{0,4},{4,8},{8,12},{1,5},{5,9},{9,13},{2,6},{6,10},{10,14},{3,7},{... | collective-permute-start | bytes 393224 | tf_op jit(solution)/shard_map/ppermute | solution.py:42
  64.8 7.2 %collective-permute-start.14 = (f32[16,16,128]{2,1,0:T(8,128)S(1)}, f32[16,16,128]{2,1,0:T(8,128)S(1)}, u32[]{:S(2)}, u32[]{:S(2)}) collective-permute-start(f32[16,16,128]{2,1,0:T(8,128)S(1)} %get-tuple-element.67.t_ref), channel_id=1, source_target_pairs={{4,0},{8,4},{12,8},{5,1},{9,5},{13,9},{6,2},{10,6},{14,10},{7,3},{... | collective-permute-start | bytes 393224 | tf_op jit(solution)/shard_map/ppermute | solution.py:42
